TPU v7x, 256 devices: a whole 4x4x8 slice. The times are simulated.
256 devices in a mesh: gx: 4 (over x), gy: 8 (over z), gz: 8 (over y, core).
Axes of the slice: x: 4, y: 4, z: 8, core: 2. Of those that a mesh axis runs over, the one named last changes fastest.
Arguments:
- right_side: float32 [128, 256, 1024], P('gx', 'gy', 'gz'), may hold values from -8 to 8
- conductivity: float32 [128, 256, 1024], P('gx', 'gy', 'gz'), may hold values from 0.1 to 10
Outputs:
- correction: float32 [128, 256, 1024], P('gx', 'gy', 'gz')
All inputs are finite; a program needn't handle non-finite values.
Results may differ from a plain program's by a relative error of at most 0.0003.
Values sent between devices are 32-bit elements; how exact they have to be, the bound alone decides.
No kernel may reach another device: no remote copies, remote signals or barrier semaphores. Data moves between devices by JAX's collectives and lax.ppermute only.
A program may use at most 128 MiB of HBM per device.

v0:
```python
import jax
import jax.numpy as jnp
from jax import lax
from jax.sharding import PartitionSpec as P

COARSEST = 7


center_eig = 1.25
half_width = 0.75
rho_first = half_width / center_eig
rho_second = 1.0 / (2.0 * center_eig / half_width - rho_first)
keep_coef = rho_second * rho_first
push_coef = 2.0 * rho_second / half_width


def extended(shard, sides, width):
    for axis, dim in sides:
        devices, length = (lax.axis_size(axis), shard.shape[dim])
        up = [(i, (i + 1) % devices) for i in range(devices - 1)]
        down = [(j, i) for i, j in up]
        last = lax.slice_in_dim(shard, length - width, length, axis=dim)
        leading = lax.slice_in_dim(shard, 0, width, axis=dim)
        before = lax.ppermute(last, axis, up)
        after = lax.ppermute(leading, axis, down)
        shard = jnp.concatenate([before, shard, after], axis=dim)
    return shard


def harmonic(left_side, right_hand):
    product = left_side * right_hand
    inside = product > 0
    return jnp.where(
        inside,
        2.0 * product / jnp.where(inside, left_side + right_hand, 1.0),
        left_side + right_hand,
    )


def shifted(tensor, dimension, offset):
    slicer = [slice(1, -1), slice(1, -1), slice(1, -1)]
    slicer[dimension] = slice(1 + offset, tensor.shape[dimension] - 1 + offset)
    return tensor[tuple(slicer)]


def apply_stencil(values, conduct, level_scale):
    center = shifted(values, 0, 0)
    middle = shifted(conduct, 0, 0)
    summed = jnp.zeros(center.shape, jnp.float32)
    for dimension in range(3):
        lower_face = harmonic(middle, shifted(conduct, dimension, -1))
        upper_face = harmonic(middle, shifted(conduct, dimension, 1))
        summed = (
            summed
            + lower_face * (center - shifted(values, dimension, -1))
            + upper_face * (center - shifted(values, dimension, 1))
        )
    return level_scale * summed


def inverse_diag(conduct, level_scale):
    middle = shifted(conduct, 0, 0)
    weights = jnp.zeros(middle.shape, jnp.float32)
    for dimension in range(3):
        weights = (
            weights
            + harmonic(middle, shifted(conduct, dimension, -1))
            + harmonic(middle, shifted(conduct, dimension, 1))
        )
    inside = middle > 0
    return jnp.where(inside, 1.0 / jnp.where(inside, level_scale * weights, 1.0), 0.0)


def restrict(values):
    reshaped = values.reshape(
        values.shape[0] // 2, 2, values.shape[1] // 2, 2, values.shape[2] // 2, 2
    )
    return reshaped.mean(axis=(1, 3, 5))


def prolong(coarse):
    grid_shape = (coarse.shape[0], 2, coarse.shape[1], 2, coarse.shape[2], 2)
    expanded = jnp.broadcast_to(coarse[:, None, :, None, :, None], grid_shape)
    return expanded.reshape(2 * coarse.shape[0], 2 * coarse.shape[1], 2 * coarse.shape[2])


def cycle(source, conduct, level_index):
    level_scale = 0.25 ** (level_index - 2)
    cond_pad = jnp.pad(conduct, 1)
    inverse = inverse_diag(cond_pad, level_scale)
    first_step = inverse * source / center_eig
    rest_one = source - apply_stencil(jnp.pad(first_step, 1), cond_pad, level_scale)
    second_step = keep_coef * first_step + push_coef * inverse * rest_one
    approx = first_step + second_step
    if level_index == COARSEST:
        return approx
    leftover = rest_one - apply_stencil(jnp.pad(second_step, 1), cond_pad, level_scale)
    coarse = cycle(restrict(leftover), restrict(conduct), level_index + 1)
    approx = approx + prolong(coarse)
    start_resid = source - apply_stencil(jnp.pad(approx, 1), cond_pad, level_scale)
    first_step = inverse * start_resid / center_eig
    rest_one = start_resid - apply_stencil(jnp.pad(first_step, 1), cond_pad, level_scale)
    second_step = keep_coef * first_step + push_coef * inverse * rest_one
    return approx + first_step + second_step


def descend_near(source, conduct, level_scale):
    cond_pad = extended(conduct, (("gx", 0), ("gy", 1), ("gz", 2)), 1)
    inverse = inverse_diag(cond_pad, level_scale)
    first_step = inverse * source / center_eig
    first_pad = extended(first_step, (("gx", 0), ("gy", 1), ("gz", 2)), 1)
    rest_one = source - apply_stencil(first_pad, cond_pad, level_scale)
    second_step = keep_coef * first_step + push_coef * inverse * rest_one
    approx = first_step + second_step
    second_pad = extended(second_step, (("gx", 0), ("gy", 1), ("gz", 2)), 1)
    leftover = rest_one - apply_stencil(second_pad, cond_pad, level_scale)
    return (approx, leftover, (source, cond_pad, inverse))


def ascend_near(approx, kept_state, level_scale):
    source, cond_pad, inverse = kept_state
    approx_pad = extended(approx, (("gx", 0), ("gy", 1), ("gz", 2)), 1)
    start_resid = source - apply_stencil(approx_pad, cond_pad, level_scale)
    first_step = inverse * start_resid / center_eig
    first_pad = extended(first_step, (("gx", 0), ("gy", 1), ("gz", 2)), 1)
    rest_one = start_resid - apply_stencil(first_pad, cond_pad, level_scale)
    second_step = keep_coef * first_step + push_coef * inverse * rest_one
    return approx + first_step + second_step


def assemble(gathered, count_x, count_y, count_z):
    block_shape = gathered.shape[2:]
    regrouped = gathered.reshape(
        count_x, count_y, count_z, 2, block_shape[0], block_shape[1], block_shape[2]
    )
    regrouped = jnp.transpose(regrouped, (3, 0, 4, 1, 5, 2, 6))
    regrouped = regrouped.reshape(
        2, count_x * block_shape[0], count_y * block_shape[1], count_z * block_shape[2]
    )
    return (regrouped[0], regrouped[1])


def shards(right_side, conductivity):
    descend, ascend = (descend_near, ascend_near)
    split_last = 5
    source, conduct = (right_side, conductivity)
    saved_states = []
    for level_index in range(2, split_last + 1):
        level_scale = 0.25 ** (level_index - 2)
        approx, leftover, kept_state = descend(source, conduct, level_scale)
        saved_states.append((approx, kept_state, level_scale))
        source = restrict(leftover)
        conduct = restrict(conduct)
    stacked = jnp.stack([source, conduct])[None]
    gathered = lax.all_gather(stacked, ("gx", "gy", "gz"), axis=0, tiled=True)
    whole_source, whole_conduct = assemble(
        gathered, lax.axis_size("gx"), lax.axis_size("gy"), lax.axis_size("gz")
    )
    correction = cycle(whole_source, whole_conduct, split_last + 1)
    widths = source.shape
    starts = (
        lax.axis_index("gx") * widths[0],
        lax.axis_index("gy") * widths[1],
        lax.axis_index("gz") * widths[2],
    )
    correction = lax.dynamic_slice(correction, starts, widths)
    for approx, kept_state, level_scale in reversed(saved_states):
        correction = ascend(approx + prolong(correction), kept_state, level_scale)
    return correction


def solution(mesh):
    in_specs = (P("gx", "gy", "gz"), P("gx", "gy", "gz"))
    out_specs = P("gx", "gy", "gz")
    return jax.shard_map(shards, mesh=mesh, in_specs=in_specs, out_specs=out_specs, check_vma=False)
```

profile of v0, /device:TPU:1, one launch (start us, length us, event | category | flops | bytes accessed | tf_op | source)
XLA Modules:
  0.0 843.1 jit_solution(7779082198861110483)
XLA Ops:
  18.2 6.4 collective-permute-start.4
  31.2 4.1 multiply_multiply_fusion
  40.6 34.8 %reshape.78 = f32[16,2,16,2,64,2]{5,4,3,2,1,0:T(8,128)} reshape(f32[32,32,128]{2,1,0:T(8,128)S(1)} %copy-done) | data formatting | bytes 1048576 | tf_op jit(solution)/shard_map/reshape | solution.py:75
  75.4 12.2 %reduce_sum.97 = f32[16,16,64]{2,1,0:T(8,128)S(1)} reduce(f32[16,2,16,2,64,2]{5,4,3,2,1,0:T(8,128)} %reshape.78, f32[]{:T(128)} %constant.38.clone.1), dimensions={1,3,5}, to_apply=%region_0.1 | reduce | flops 114688 | bytes 589828 | tf_op jit(solution)/shard_map/reduce_sum | solution.py:78
  93.6 4.5 collective-permute-done.9
  109.8 4.3 collective-permute-start.12
  119.4 5.6 multiply_add_fusion
  130.3 4.8 collective-permute-start.14
  136.5 4.3 collective-permute-start.20
  149.4 6.2 collective-permute-start.22
  170.3 5.0 fusion.42
  175.3 35.6 %reshape.79 = f32[16,2,16,2,64,2]{5,4,3,2,1,0:T(8,128)} reshape(f32[32,32,128]{2,1,0:T(8,128)} %fusion.42) | data formatting | bytes 1048576 | tf_op jit(solution)/shard_map/reshape | solution.py:75
  210.9 12.2 %reduce_sum.98 = f32[16,16,64]{2,1,0:T(8,128)S(1)} reduce(f32[16,2,16,2,64,2]{5,4,3,2,1,0:T(8,128)} %reshape.79, f32[]{:T(128)} %constant.38.clone.1), dimensions={1,3,5}, to_apply=%region_1.2 | reduce | flops 114688 | bytes 589828 | tf_op jit(solution)/shard_map/reduce_sum | solution.py:78
  226.6 4.8 collective-permute-start.24
  232.7 5.7 div.170
  253.1 5.2 collective-permute-start.28
  260.8 4.8 collective-permute-start.30
  283.5 4.3 collective-permute-start.38
  292.4 6.2 collective-permute-start.40
  308.9 6.5 reshape.80
  320.4 4.3 collective-permute-start.42
  329.7 4.2 collective-permute-start.44
  341.8 5.4 collective-permute-start.46
  354.6 4.3 collective-permute-start.54
  361.0 4.3 collective-permute-start.50
  375.1 4.1 collective-permute-start.58
  395.6 4.8 collective-permute-start.60
  415.9 6.4 collective-permute-start.64
  439.0 5.3 collective-permute-start.68
  450.3 4.7 collective-permute-start.70
  465.8 59.9 %all-gather = f32[512,2,2,8]{3,2,1,0:T(2,128)S(1)} all-gather(f32[2,2,2,8]{3,2,1,0:T(2,128)S(1)} %pad_maximum_fusion.414), channel_id=2, replica_groups=mesh['gx'=4,'gy'=8,'gz'=8] {'gx','gy','gz'}, dimensions={0}, use_global_device_ids=true | all-gather | bytes 65792 | tf_op jit(solution)/shard_map/all_gather | solution.py:155
  537.9 4.4 reshape.84
  581.1 4.7 collective-permute-start.76
  606.7 4.4 collective-permute-start.82
  628.7 4.1 collective-permute-start.86
  637.7 4.4 collective-permute-start.88
  663.3 4.7 collective-permute-start.94
  677.5 5.5 reshape.88
  697.6 4.7 collective-permute-start.100
  705.1 4.4 collective-permute-done.101
  724.4 4.6 collective-permute-start.106
  731.9 4.4 collective-permute-done.107
  736.9 11.4 %broadcast_in_dim.218 = f32[16,2,16,2,64,2]{5,4,3,2,1,0:T(8,128)} broadcast(f32[16,16,64]{2,1,0:T(8,128)S(1)} %fusion.86), dimensions={0,2,4} | broadcast | bytes 589824 | tf_op jit(solution)/shard_map/broadcast_in_dim | solution.py:83
  748.3 24.4 %reshape.89 = f32[32,32,128]{2,1,0:T(8,128)} reshape(f32[16,2,16,2,64,2]{5,4,3,2,1,0:T(8,128)} %broadcast_in_dim.218) | data formatting | bytes 1048576 | tf_op jit(solution)/shard_map/reshape | solution.py:84
  790.7 4.6 collective-permute-start.112
  803.0 5.0 broadcast_multiply_fusion
  824.4 4.8 collective-permute-start.118
  836.9 6.0 fusion.6
  (458 shorter events, 449.1 us)
Async XLA Ops:
  18.2 8.7 %collective-permute-start.4 = (f32[34,34,1]{1,2,0:T(1,128)S(1)}, f32[34,34,1]{1,2,0:T(1,128)S(1)}, u32[]{:S(2)}, u32[]{:S(2)}) collective-permute-start(f32[34,34,1]{1,2,0:T(1,128)S(1)} %copy.27), channel_id=1, source_target_pairs={{0,1},{1,2},{2,3},{3,4},{4,5},{5,6},{6,7},{8,9},{9,10},{10,11},{11... | collective-permute-start | bytes 13880 | tf_op jit(solution)/shard_map/ppermute | solution.py:24
  36.2 51.5 %collective-permute-start.6 = (f32[1,32,128]{2,1,0:T(8,128)S(1)}, f32[1,32,128]{2,1,0:T(8,128)S(1)}, u32[]{:S(2)}, u32[]{:S(2)}) collective-permute-start(f32[1,32,128]{2,1,0:T(8,128)S(1)} %get-tuple-element.83), channel_id=1, source_target_pairs={{0,64},{64,128},{128,192},{1,65},{65,129},{129,193},{2,66},{66,130... | collective-permute-start | bytes 49160 | tf_op jit(solution)/shard_map/ppermute | solution.py:24
  39.3 48.4 %collective-permute-start.7 = (f32[1,32,128]{2,1,0:T(8,128)S(1)}, f32[1,32,128]{2,1,0:T(8,128)S(1)}, u32[]{:S(2)}, u32[]{:S(2)}) collective-permute-start(f32[1,32,128]{2,1,0:T(8,128)S(1)} %get-tuple-element.84), channel_id=1, source_target_pairs={{64,0},{128,64},{192,128},{65,1},{129,65},{193,129},{66,2},{130,66... | collective-permute-start | bytes 49160 | tf_op jit(solution)/shard_map/ppermute | solution.py:25
  102.5 12.9 %collective-permute-start.10 = (f32[34,34,1]{1,2,0:T(1,128)}, f32[34,34,1]{1,2,0:T(1,128)}, u32[]{:S(2)}, u32[]{:S(2)}) collective-permute-start(f32[34,34,1]{1,2,0:T(1,128)} %copy.31), channel_id=1, source_target_pairs={{0,1},{1,2},{2,3},{3,4},{4,5},{5,6},{6,7},{8,9},{9,10},{10,11},{11... | collective-permute-start | bytes 13880 | tf_op jit(solution)/shard_map/ppermute | solution.py:24
  107.9 9.5 %collective-permute-start.11 = (f32[34,34,1]{1,2,0:T(1,128)}, f32[34,34,1]{1,2,0:T(1,128)}, u32[]{:S(2)}, u32[]{:S(2)}) collective-permute-start(f32[34,34,1]{1,2,0:T(1,128)} %copy.33), channel_id=1, source_target_pairs={{1,0},{2,1},{3,2},{4,3},{5,4},{6,5},{7,6},{9,8},{10,9},{11,10},{12... | collective-permute-start | bytes 13880 | tf_op jit(solution)/shard_map/ppermute | solution.py:25
  109.8 20.4 %collective-permute-start.12 = (f32[1,16,64]{2,1,0:T(8,128)S(1)}, f32[1,16,64]{2,1,0:T(8,128)S(1)}, u32[]{:S(2)}, u32[]{:S(2)}) collective-permute-start(f32[1,16,64]{2,1,0:T(8,128)S(1)} %get-tuple-element.115), channel_id=1, source_target_pairs={{0,64},{64,128},{128,192},{1,65},{65,129},{129,193},{2,66},{66,130... | collective-permute-start | bytes 12296 | tf_op jit(solution)/shard_map/ppermute | solution.py:24
  114.2 16.1 %collective-permute-start.13 = (f32[1,16,64]{2,1,0:T(8,128)S(1)}, f32[1,16,64]{2,1,0:T(8,128)S(1)}, u32[]{:S(2)}, u32[]{:S(2)}) collective-permute-start(f32[1,16,64]{2,1,0:T(8,128)S(1)} %get-tuple-element.116), channel_id=1, source_target_pairs={{64,0},{128,64},{192,128},{65,1},{129,65},{193,129},{66,2},{130,66... | collective-permute-start | bytes 12296 | tf_op jit(solution)/shard_map/ppermute | solution.py:25
  124.9 11.5 %collective-permute-start.18 = (f32[1,32,128]{2,1,0:T(8,128)S(1)}, f32[1,32,128]{2,1,0:T(8,128)S(1)}, u32[]{:S(2)}, u32[]{:S(2)}) collective-permute-start(f32[1,32,128]{2,1,0:T(8,128)S(1)} %get-tuple-element.81), channel_id=1, source_target_pairs={{0,64},{64,128},{128,192},{1,65},{65,129},{129,193},{2,66},{66,130... | collective-permute-start | bytes 49160 | tf_op jit(solution)/shard_map/ppermute | solution.py:24
  128.9 7.5 collective-permute-start.19
  130.3 11.8 %collective-permute-start.14 = (f32[18,1,64]{2,1,0:T(1,128)S(1)}, f32[18,1,64]{2,1,0:T(1,128)S(1)}, u32[]{:S(2)}, u32[]{:S(2)}) collective-permute-start(f32[18,1,64]{2,1,0:T(1,128)S(1)} %get-tuple-element.105), channel_id=1, source_target_pairs={{0,8},{8,16},{16,24},{24,32},{32,40},{40,48},{48,56},{1,9},{9,17},... | collective-permute-start | bytes 13832 | tf_op jit(solution)/shard_map/ppermute | solution.py:24
  135.2 7.0 collective-permute-start.15
  149.4 17.0 %collective-permute-start.22 = (f32[34,34,1]{1,2,0:T(1,128)}, f32[34,34,1]{1,2,0:T(1,128)}, u32[]{:S(2)}, u32[]{:S(2)}) collective-permute-start(f32[34,34,1]{1,2,0:T(1,128)} %copy.35), channel_id=1, source_target_pairs={{0,1},{1,2},{2,3},{3,4},{4,5},{5,6},{6,7},{8,9},{9,10},{10,11},{11... | collective-permute-start | bytes 13880 | tf_op jit(solution)/shard_map/ppermute | solution.py:24
  157.6 10.8 %collective-permute-start.23 = (f32[34,34,1]{1,2,0:T(1,128)}, f32[34,34,1]{1,2,0:T(1,128)}, u32[]{:S(2)}, u32[]{:S(2)}) collective-permute-start(f32[34,34,1]{1,2,0:T(1,128)} %copy.37), channel_id=1, source_target_pairs={{1,0},{2,1},{3,2},{4,3},{5,4},{6,5},{7,6},{9,8},{10,9},{11,10},{12... | collective-permute-start | bytes 13880 | tf_op jit(solution)/shard_map/ppermute | solution.py:25
  160.3 62.7 %collective-permute-start.16 = (f32[18,18,1]{2,1,0:T(8,128)}, f32[18,18,1]{2,1,0:T(8,128)}, u32[]{:S(2)}, u32[]{:S(2)}) collective-permute-start(f32[18,18,1]{2,1,0:T(8,128)} %get-tuple-element.96), channel_id=1, source_target_pairs={{0,1},{1,2},{2,3},{3,4},{4,5},{5,6},{6,7},{8,9},{9,10},{10,11},{11... | collective-permute-start | bytes 3896 | tf_op jit(solution)/shard_map/ppermute | solution.py:24
  164.0 59.1 %collective-permute-start.17 = (f32[18,18,1]{2,1,0:T(8,128)}, f32[18,18,1]{2,1,0:T(8,128)}, u32[]{:S(2)}, u32[]{:S(2)}) collective-permute-start(f32[18,18,1]{2,1,0:T(8,128)} %get-tuple-element.95), channel_id=1, source_target_pairs={{1,0},{2,1},{3,2},{4,3},{5,4},{6,5},{7,6},{9,8},{10,9},{11,10},{12... | collective-permute-start | bytes 3896 | tf_op jit(solution)/shard_map/ppermute | solution.py:25
  226.6 15.0 %collective-permute-start.24 = (f32[1,16,64]{2,1,0:T(8,128)}, f32[1,16,64]{2,1,0:T(8,128)}, u32[]{:S(2)}, u32[]{:S(2)}) collective-permute-start(f32[1,16,64]{2,1,0:T(8,128)} %get-tuple-element.113), channel_id=1, source_target_pairs={{0,64},{64,128},{128,192},{1,65},{65,129},{129,193},{2,66},{66,130... | collective-permute-start | bytes 12296 | tf_op jit(solution)/shard_map/ppermute | solution.py:24
  231.4 10.2 %collective-permute-start.25 = (f32[1,16,64]{2,1,0:T(8,128)}, f32[1,16,64]{2,1,0:T(8,128)}, u32[]{:S(2)}, u32[]{:S(2)}) collective-permute-start(f32[1,16,64]{2,1,0:T(8,128)} %get-tuple-element.114), channel_id=1, source_target_pairs={{64,0},{128,64},{192,128},{65,1},{129,65},{193,129},{66,2},{130,66... | collective-permute-start | bytes 12296 | tf_op jit(solution)/shard_map/ppermute | solution.py:25
  253.1 17.5 %collective-permute-start.28 = (f32[18,18,1]{2,1,0:T(8,128)}, f32[18,18,1]{2,1,0:T(8,128)}, u32[]{:S(2)}, u32[]{:S(2)}) collective-permute-start(f32[18,18,1]{2,1,0:T(8,128)} %get-tuple-element.93), channel_id=1, source_target_pairs={{0,1},{1,2},{2,3},{3,4},{4,5},{5,6},{6,7},{8,9},{9,10},{10,11},{11... | collective-permute-start | bytes 3896 | tf_op jit(solution)/shard_map/ppermute | solution.py:24
  258.3 12.3 %collective-permute-start.29 = (f32[18,18,1]{2,1,0:T(8,128)}, f32[18,18,1]{2,1,0:T(8,128)}, u32[]{:S(2)}, u32[]{:S(2)}) collective-permute-start(f32[18,18,1]{2,1,0:T(8,128)} %get-tuple-element.94), channel_id=1, source_target_pairs={{1,0},{2,1},{3,2},{4,3},{5,4},{6,5},{7,6},{9,8},{10,9},{11,10},{12... | collective-permute-start | bytes 3896 | tf_op jit(solution)/shard_map/ppermute | solution.py:25
  260.8 17.2 %collective-permute-start.30 = (f32[1,8,32]{2,1,0:T(8,128)}, f32[1,8,32]{2,1,0:T(8,128)}, u32[]{:S(2)}, u32[]{:S(2)}) collective-permute-start(f32[1,8,32]{2,1,0:T(8,128)} %get-tuple-element.147), channel_id=1, source_target_pairs={{0,64},{64,128},{128,192},{1,65},{65,129},{129,193},{2,66},{66,130... | collective-permute-start | bytes 3080 | tf_op jit(solution)/shard_map/ppermute | solution.py:24
  265.7 12.4 %collective-permute-start.31 = (f32[1,8,32]{2,1,0:T(8,128)}, f32[1,8,32]{2,1,0:T(8,128)}, u32[]{:S(2)}, u32[]{:S(2)}) collective-permute-start(f32[1,8,32]{2,1,0:T(8,128)} %get-tuple-element.148), channel_id=1, source_target_pairs={{64,0},{128,64},{192,128},{65,1},{129,65},{193,129},{66,2},{130,66... | collective-permute-start | bytes 3080 | tf_op jit(solution)/shard_map/ppermute | solution.py:25
  272.7 10.8 %collective-permute-start.36 = (f32[1,16,64]{2,1,0:T(8,128)S(1)}, f32[1,16,64]{2,1,0:T(8,128)S(1)}, u32[]{:S(2)}, u32[]{:S(2)}) collective-permute-start(f32[1,16,64]{2,1,0:T(8,128)S(1)} %get-tuple-element.111), channel_id=1, source_target_pairs={{0,64},{64,128},{128,192},{1,65},{65,129},{129,193},{2,66},{66,130... | collective-permute-start | bytes 12296 | tf_op jit(solution)/shard_map/ppermute | solution.py:24
  276.7 6.8 collective-permute-start.37
  278.9 10.2 %collective-permute-start.32 = (f32[10,1,32]{2,1,0:T(1,128)S(1)}, f32[10,1,32]{2,1,0:T(1,128)S(1)}, u32[]{:S(2)}, u32[]{:S(2)}) collective-permute-start(f32[10,1,32]{2,1,0:T(1,128)S(1)} %get-tuple-element.137), channel_id=1, source_target_pairs={{0,8},{8,16},{16,24},{24,32},{32,40},{40,48},{48,56},{1,9},{9,17},... | collective-permute-start | bytes 3848 | tf_op jit(solution)/shard_map/ppermute | solution.py:24
  282.2 7.0 collective-permute-start.33
  292.4 14.4 %collective-permute-start.40 = (f32[18,18,1]{2,1,0:T(8,128)S(1)}, f32[18,18,1]{2,1,0:T(8,128)S(1)}, u32[]{:S(2)}, u32[]{:S(2)}) collective-permute-start(f32[18,18,1]{2,1,0:T(8,128)S(1)} %get-tuple-element.91), channel_id=1, source_target_pairs={{0,1},{1,2},{2,3},{3,4},{4,5},{5,6},{6,7},{8,9},{9,10},{10,11},{11... | collective-permute-start | bytes 3896 | tf_op jit(solution)/shard_map/ppermute | solution.py:24
  298.6 8.2 collective-permute-start.41
  301.3 17.3 %collective-permute-start.34 = (f32[10,10,1]{2,1,0:T(8,128)}, f32[10,10,1]{2,1,0:T(8,128)}, u32[]{:S(2)}, u32[]{:S(2)}) collective-permute-start(f32[10,10,1]{2,1,0:T(8,128)} %get-tuple-element.126), channel_id=1, source_target_pairs={{0,1},{1,2},{2,3},{3,4},{4,5},{5,6},{6,7},{8,9},{9,10},{10,11},{11... | collective-permute-start | bytes 1208 | tf_op jit(solution)/shard_map/ppermute | solution.py:24
  304.9 13.7 %collective-permute-start.35 = (f32[10,10,1]{2,1,0:T(8,128)}, f32[10,10,1]{2,1,0:T(8,128)}, u32[]{:S(2)}, u32[]{:S(2)}) collective-permute-start(f32[10,10,1]{2,1,0:T(8,128)} %get-tuple-element.125), channel_id=1, source_target_pairs={{1,0},{2,1},{3,2},{4,3},{5,4},{6,5},{7,6},{9,8},{10,9},{11,10},{12... | collective-permute-start | bytes 1208 | tf_op jit(solution)/shard_map/ppermute | solution.py:25
  329.7 10.5 %collective-permute-start.44 = (f32[10,1,32]{2,1,0:T(1,128)}, f32[10,1,32]{2,1,0:T(1,128)}, u32[]{:S(2)}, u32[]{:S(2)}) collective-permute-start(f32[10,1,32]{2,1,0:T(1,128)} %get-tuple-element.135), channel_id=1, source_target_pairs={{0,8},{8,16},{16,24},{24,32},{32,40},{40,48},{48,56},{1,9},{9,17},... | collective-permute-start | bytes 3848 | tf_op jit(solution)/shard_map/ppermute | solution.py:24
  335.8 24.4 %collective-permute-start.48 = (f32[1,4,16]{2,1,0:T(4,128)}, f32[1,4,16]{2,1,0:T(4,128)}, u32[]{:S(2)}, u32[]{:S(2)}) collective-permute-start(f32[1,4,16]{2,1,0:T(4,128)} %get-tuple-element.177), channel_id=1, source_target_pairs={{0,64},{64,128},{128,192},{1,65},{65,129},{129,193},{2,66},{66,130... | collective-permute-start | bytes 776 | tf_op jit(solution)/shard_map/ppermute | solution.py:24
  338.2 22.0 %collective-permute-start.49 = (f32[1,4,16]{2,1,0:T(4,128)}, f32[1,4,16]{2,1,0:T(4,128)}, u32[]{:S(2)}, u32[]{:S(2)}) collective-permute-start(f32[1,4,16]{2,1,0:T(4,128)} %get-tuple-element.178), channel_id=1, source_target_pairs={{64,0},{128,64},{192,128},{65,1},{129,65},{193,129},{66,2},{130,66... | collective-permute-start | bytes 776 | tf_op jit(solution)/shard_map/ppermute | solution.py:25
  341.8 8.8 %collective-permute-start.46 = (f32[10,10,1]{2,1,0:T(8,128)}, f32[10,10,1]{2,1,0:T(8,128)}, u32[]{:S(2)}, u32[]{:S(2)}) collective-permute-start(f32[10,10,1]{2,1,0:T(8,128)} %get-tuple-element.123), channel_id=1, source_target_pairs={{0,1},{1,2},{2,3},{3,4},{4,5},{5,6},{6,7},{8,9},{9,10},{10,11},{11... | collective-permute-start | bytes 1208 | tf_op jit(solution)/shard_map/ppermute | solution.py:24
  354.6 11.9 %collective-permute-start.54 = (f32[1,8,32]{2,1,0:T(8,128)S(1)}, f32[1,8,32]{2,1,0:T(8,128)S(1)}, u32[]{:S(2)}, u32[]{:S(2)}) collective-permute-start(f32[1,8,32]{2,1,0:T(8,128)S(1)} %get-tuple-element.143), channel_id=1, source_target_pairs={{0,64},{64,128},{128,192},{1,65},{65,129},{129,193},{2,66},{66,130... | collective-permute-start | bytes 3080 | tf_op jit(solution)/shard_map/ppermute | solution.py:24
  358.9 7.7 collective-permute-start.55
  361.0 10.9 %collective-permute-start.50 = (f32[6,1,16]{2,1,0:T(1,128)S(1)}, f32[6,1,16]{2,1,0:T(1,128)S(1)}, u32[]{:S(2)}, u32[]{:S(2)}) collective-permute-start(f32[6,1,16]{2,1,0:T(1,128)S(1)} %get-tuple-element.167), channel_id=1, source_target_pairs={{0,8},{8,16},{16,24},{24,32},{32,40},{40,48},{48,56},{1,9},{9,17},... | collective-permute-start | bytes 1160 | tf_op jit(solution)/shard_map/ppermute | solution.py:24
  375.1 12.5 %collective-permute-start.58 = (f32[10,10,1]{2,1,0:T(8,128)S(1)}, f32[10,10,1]{2,1,0:T(8,128)S(1)}, u32[]{:S(2)}, u32[]{:S(2)}) collective-permute-start(f32[10,10,1]{2,1,0:T(8,128)S(1)} %get-tuple-element.121), channel_id=1, source_target_pairs={{0,1},{1,2},{2,3},{3,4},{4,5},{5,6},{6,7},{8,9},{9,10},{10,11},{11... | collective-permute-start | bytes 1208 | tf_op jit(solution)/shard_map/ppermute | solution.py:24
  379.2 8.4 collective-permute-start.59
  381.8 11.1 %collective-permute-start.52 = (f32[6,6,1]{2,1,0:T(8,128)}, f32[6,6,1]{2,1,0:T(8,128)}, u32[]{:S(2)}, u32[]{:S(2)}) collective-permute-start(f32[6,6,1]{2,1,0:T(8,128)} %get-tuple-element.158), channel_id=1, source_target_pairs={{0,1},{1,2},{2,3},{3,4},{4,5},{5,6},{6,7},{8,9},{9,10},{10,11},{11... | collective-permute-start | bytes 440 | tf_op jit(solution)/shard_map/ppermute | solution.py:24
  385.4 7.4 collective-permute-start.53
  415.9 8.3 collective-permute-start.64
  663.3 6.7 collective-permute-start.94
  697.6 7.6 collective-permute-start.100
  702.3 7.3 collective-permute-start.101
  724.4 7.5 collective-permute-start.106
  729.1 7.3 collective-permute-start.107
  790.7 8.0 collective-permute-start.112
  824.4 8.1 collective-permute-start.118
  (115 other events, 1552.7 us)
where the time goes:
time: 857 us; the launch traced here: 843 us
  starting transfers between devices  323 us (38%)
  local copies, waits for them, and re-layouts  208 us (24%)
  waiting for transfers between devices  126 us (15%)
  other arithmetic  124 us (14%)
  blocking collectives  59.9 us (7%)
    ppermute x60, starting transfers between devices, extended(): before = lax.ppermute(last, axis, up)  232 us
    ppermute x60, waiting for transfers between devices, extended(): after = lax.ppermute(leading, axis, down)  124 us
    ppermute x60, starting transfers between devices, extended(): after = lax.ppermute(leading, axis, down)  90.8 us
    reshape x6, local copies, waits for them, and re-layouts, restrict(): values.reshape(values.shape[0] // 2, 2, values.shape[1] // 2, 2, values.s...  84.6 us
    all_gather x1, blocking collectives, shards(): gathered = lax.all_gather(stacked, ('gx', 'gy', 'gz'), axis=0, tiled=True)  59.9 us
    reduce_sum x11, other arithmetic, restrict(): return reshaped.mean(axis=(1, 3, 5))  43.1 us
    reshape x5, local copies, waits for them, and re-layouts, prolong(): expanded.reshape(2 * coarse.shape[0], 2 * coarse.shape[1], 2 * coarse.sha...  37.1 us
    slice x41, local copies, waits for them, and re-layouts, extended(): last = lax.slice_in_dim(shard, length - width, length, axis=dim)  20 us
  transfers between devices with their start and end apart: 120, of which 42 were waited for; matrix products, arithmetic and copies ran while one was open for 20% of the time, Pallas kernels for 0%

commit v1 on v0

v1 whole, which is shorter than its diff:
```python
import functools

import jax
import jax.numpy as jnp
from jax import lax
from jax.experimental import pallas as pl
from jax.experimental.pallas import tpu as pltpu
from jax.sharding import PartitionSpec as P

F32 = jnp.float32
AXES = ("gx", "gy", "gz")
DEV = (4, 8, 8)

center_eig = 1.25
half_width = 0.75
rho_first = half_width / center_eig
rho_second = 1.0 / (2.0 * center_eig / half_width - rho_first)
keep_coef = rho_second * rho_first
push_coef = 2.0 * rho_second / half_width
inv_center = 1.0 / center_eig

N2, R2, T2 = 40, 40, 56
N3, R3, T3 = 42, 48, 64
N4, R4, T4 = 20, 24, 40


def rcp(value):
    guess = pl.reciprocal(value, approx=True)
    return guess * (2.0 - value * guess)


def lanes_of(rows):
    return lax.broadcasted_iota(jnp.int32, (rows, 128), 1)


def rows_of(rows):
    return lax.broadcasted_iota(jnp.int32, (rows, 128), 0)


def rolled(value, shift):
    shift = shift % 128
    return value if shift == 0 else pltpu.roll(value, shift, 1)


def select_dot(value, matrix):
    return jnp.dot(value, matrix, precision=lax.Precision.HIGHEST, preferred_element_type=F32)


def square(condition, value):
    source = lax.broadcasted_iota(jnp.int32, (128, 128), 0)
    target = lax.broadcasted_iota(jnp.int32, (128, 128), 1)
    return jnp.where(condition(source, target), value, 0.0).astype(F32)


def loop(low, high, body):
    @pl.loop(low, high)
    def _(index):
        body(index)


def rows_kernel(pos, b, k, xlo, xhi, low, high):
    gx = pos[0]

    def put(plane, bv, kv):
        low[plane, 0:4] = bv[0:4]
        low[plane, 4:8] = kv[0:4]
        high[plane, 0:4] = bv[28:32]
        high[plane, 4:8] = kv[28:32]

    for j in range(4):
        kl = jnp.where(gx == 0, k[0], xlo[7]) if j == 3 else xlo[4 + j]
        kh = jnp.where(gx == DEV[0] - 1, k[31], xhi[4]) if j == 0 else xhi[4 + j]
        put(j, xlo[j], kl)
        put(36 + j, xhi[j], kh)
    loop(0, 32, lambda i: put(i + 4, b[i], k[i]))


def assemble_two(pos, b, k, xlo, xhi, ylo, yhi, put_b, put_k, get_k):
    gx, gy = pos[0], pos[1]
    for j in range(4):
        kl = jnp.where(gx == 0, k[0], xlo[7]) if j == 3 else xlo[4 + j]
        kh = jnp.where(gx == DEV[0] - 1, k[31], xhi[4]) if j == 0 else xhi[4 + j]
        put_b(j, 12, 32, xlo[j])
        put_k(j, 12, 32, kl)
        put_b(36 + j, 12, 32, xhi[j])
        put_k(36 + j, 12, 32, kh)

    def inner(i):
        put_b(i + 4, 12, 32, b[i])
        put_k(i + 4, 12, 32, k[i])

    loop(0, 32, inner)
    row = rows_of(4)

    def edges(i):
        put_b(i, 8, 4, ylo[i, 0:4])
        put_b(i, 44, 4, yhi[i, 0:4])
        kl = jnp.where((row == 3) & (gy == 0), get_k(i, 12, 1), ylo[i, 4:8])
        kh = jnp.where((row == 0) & (gy == DEV[1] - 1), get_k(i, 43, 1), yhi[i, 4:8])
        put_k(i, 8, 4, kl)
        put_k(i, 44, 4, kh)

    loop(0, N2, edges)


def accessors(b_ref, k_ref):
    def put_b(i, start, count, value):
        b_ref[i, start : start + count] = value

    def put_k(i, start, count, value):
        k_ref[i, start : start + count] = value

    def get_k(i, start, count):
        return k_ref[i, start : start + count]

    return put_b, put_k, get_k


def lanes_kernel(pos, b, k, xlo, xhi, ylo, yhi, low, high, eb, ek):
    assemble_two(pos, b, k, xlo, xhi, ylo, yhi, *accessors(eb, ek))
    group = lanes_of(R2) >> 2

    def column(col, slots):
        lo = jnp.zeros((R2, 128), F32)
        hi = jnp.zeros((R2, 128), F32)
        for s in range(slots):
            bv = eb[col * 16 + s, 8:48]
            kv = ek[col * 16 + s, 8:48]
            first, second = group == 2 * s, group == 2 * s + 1
            lo = jnp.where(first, rolled(bv, 8 * s), lo)
            lo = jnp.where(second, rolled(kv, 8 * s + 4), lo)
            hi = jnp.where(first, rolled(bv, 8 * s + 4), hi)
            hi = jnp.where(second, rolled(kv, 8 * s + 8), hi)
        low[col] = lo
        high[col] = hi

    loop(0, 2, lambda col: column(col, 16))
    column(2, 8)


def up_two(pair):
    last = lanes_of(pair[0].shape[0]) == 127
    left, right = pltpu.roll(pair[0], 127, 1), pltpu.roll(pair[1], 127, 1)
    return jnp.where(last, right, left), jnp.where(last, left, right)


def down_two(pair):
    first = lanes_of(pair[0].shape[0]) == 0
    left, right = pltpu.roll(pair[0], 1, 1), pltpu.roll(pair[1], 1, 1)
    return jnp.where(first, right, left), jnp.where(first, left, right)


def flux_two(v_ref, wx, wy, wz, p, start, rows, columns):
    here = slice(start, start + rows)
    above = slice(start + 1, start + rows + 1)
    below = slice(start - 1, start + rows - 1)
    v = [v_ref[c, p, here] for c in range(2)]
    fz = [wz[c, p, here] * (v[c] - u) for c, u in enumerate(up_two(v))]
    fzm = down_two(fz)
    result = []
    for c in range(columns):
        fx = wx[c, p, here] * (v[c] - v_ref[c, p + 1, here])
        gx = wx[c, p - 1, here] * (v_ref[c, p - 1, here] - v[c])
        fy = wy[c, p, here] * (v[c] - v_ref[c, p, above])
        gy = wy[c, p, below] * (v_ref[c, p, below] - v[c])
        result.append((fx - gx) + (fy - gy) + (fz[c] - fzm[c]))
    return result


def down_kernel(
    pos, b, k, xlo, xhi, ylo, yhi, zlo, zhi,
    bk3, eb, wx, wy, wz, inv, xs,
    ek, q, f, r1, s, masks, tmp,
):
    gx, gy, gz = pos[0], pos[1], pos[2]
    assemble_two(pos, b, k, xlo, xhi, ylo, yhi, *accessors(eb.at[0], ek))
    lane = lanes_of(R2)
    row = rows_of(R2) - 4
    here = slice(8, 48)

    def unpack(plane, lo, hi, slot):
        bv = jnp.where(lane < 4, rolled(hi, -8 * slot), 0.0)
        eb[1, plane, here] = jnp.where(lane >= 124, rolled(lo, 124 - 8 * slot), bv)
        kv = jnp.where(lane < 4, rolled(hi, -8 * slot - 4), 1.0)
        kv = jnp.where(lane >= 124, rolled(lo, 120 - 8 * slot), kv)
        q[1, plane, here] = 0.5 * rcp(kv)
        q[0, plane, here] = 0.5 * rcp(ek[plane, here])

    def column(col, slots):
        lo, hi = zlo[col], zhi[col]
        for slot in range(slots):
            unpack(col * 16 + slot, lo, hi, slot)

    loop(0, 2, lambda col: column(col, 16))
    column(2, 8)

    inside_y = ((row >= 0) | (gy > 0)) & ((row < 32) | (gy < DEV[1] - 1))
    inside_z = ((lane < 64) & (gz < DEV[2] - 1)) | ((lane >= 64) & (gz > 0))
    masks[0] = jnp.where(inside_y, 1.0, 0.0)
    masks[1] = jnp.where(inside_y & inside_z, 1.0, 0.0)
    low_edge = (lane == 127) & (gz == 0)
    high_edge = (lane == 127) & (gz == DEV[2] - 1)

    for c in range(2):
        wx[c, 0, here] = rcp(q[c, 0, here] + q[c, 1, here])

    def weigh(p):
        inside_x = ((p >= 4) | (gx > 0)) & ((p < 36) | (gx < DEV[0] - 1))
        scale_x = jnp.where(inside_x, 1.0, 0.0)
        v = [q[c, p, here] for c in range(2)]
        u = up_two(v)
        faces = [
            rcp(v[0] + jnp.where(high_edge, v[0], u[0])),
            rcp(u[1] + jnp.where(low_edge, u[1], v[1])),
        ]
        lower = down_two(faces)
        for c in range(2):
            face_x = rcp(v[c] + q[c, p + 1, here])
            face_y = rcp(v[c] + q[c, p, 9:49])
            wx[c, p, here] = face_x
            wy[c, p, here] = face_y
            wz[c, p, here] = faces[c]
            total = wx[c, p - 1, here] + face_x + face_y + wy[c, p, 7:47] + faces[c] + lower[c]
            value = jnp.where(masks[c] * scale_x > 0.5, rcp(total), 0.0)
            inv[c, p, here] = value
            f[c, p, here] = value * eb[c, p, here] * inv_center

    loop(1, N2 - 1, weigh)

    def smooth(p):
        flux = flux_two(f, wx, wy, wz, p, 8, R2, 2)
        for c in range(2):
            rest = eb[c, p, here] - flux[c]
            step = keep_coef * f[c, p, here] + push_coef * inv[c, p, here] * rest
            r1[c, p, here] = rest
            s[c, p, here] = step
            xs[c, p, here] = f[c, p, here] + step

    loop(2, N2 - 2, smooth)

    to_b = square(lambda i, j: (i >> 1) == j, 0.125)
    to_k = square(lambda i, j: (i >> 1) + 64 == j, 0.125)

    def coarsen(i):
        p = 2 * i + 4
        total = r1[0, p, 12:44] + r1[0, p + 1, 12:44]
        total = total - flux_two(s, wx, wy, wz, p, 12, 32, 1)[0]
        tmp[0, 0:32] = total - flux_two(s, wx, wy, wz, p + 1, 12, 32, 1)[0]
        tmp[1, 0:32] = ek[p, 12:44] + ek[p + 1, 12:44]
        pairs = [tmp[j, pl.ds(0, 16, stride=2)] + tmp[j, pl.ds(1, 16, stride=2)] for j in range(2)]
        bk3[i] = select_dot(pairs[0], to_b) + select_dot(pairs[1], to_k)

    loop(0, 16, coarsen)


def planes_kernel(pos, bk, xlo, xhi, out):
    gx = pos[0]
    right = lanes_of(16) >= 64
    for j in range(13):
        lo, hi = xlo[3 + j], xhi[j]
        if j == 12:
            lo = jnp.where(right & (gx == 0), bk[0], lo)
        if j == 0:
            hi = jnp.where(right & (gx == DEV[0] - 1), bk[15], hi)
        out[j] = lo
        out[29 + j] = hi
    for j in range(16):
        out[13 + j] = bk[j]


def three_rows(pos, own, ylo, yhi, p):
    gy = pos[1]
    right = lanes_of(16) >= 64
    row = rows_of(16)
    middle = own[p]
    lo = jnp.where(right & (row == 15) & (gy == 0), own[p, 0:1], ylo[p])
    hi = jnp.where(right & (row == 0) & (gy == DEV[1] - 1), own[p, 15:16], yhi[p])
    return lo, middle, hi


def slots_kernel(pos, own, ylo, yhi, low, high):
    lane = lanes_of(16)

    def column(col):
        total_lo = [None] * 3
        total_hi = [None] * 3
        for slot in range(4):
            p = jnp.minimum(col * 4 + slot, N3 - 1)
            for g, e in enumerate(three_rows(pos, own, ylo, yhi, p)):
                near = pltpu.roll(e, 80, 1)
                far = pltpu.roll(e, 32, 1)
                lo = rolled(jnp.where(lane < 16, e, near), 32 * slot)
                hi = rolled(jnp.where(lane < 16, near, far), 32 * slot)
                mine = (lane >> 5) == slot
                total_lo[g] = lo if slot == 0 else jnp.where(mine, lo, total_lo[g])
                total_hi[g] = hi if slot == 0 else jnp.where(mine, hi, total_hi[g])
        for g in range(3):
            low[col, 16 * g : 16 * g + 16] = total_lo[g]
            high[col, 16 * g : 16 * g + 16] = total_hi[g]

    loop(0, 11, column)


def flux_one(v_ref, wx, wy, wz, p, rows, full=None):
    here, above, below = slice(8, 8 + rows), slice(9, 9 + rows), slice(7, 7 + rows)
    v = v_ref[p, here]
    fx = wx[p, here] * (v - v_ref[p + 1, here])
    gx = wx[p - 1, here] * (v_ref[p - 1, here] - v)
    fy = wy[p, here] * (v - v_ref[p, above])
    gy = wy[p, below] * (v_ref[p, below] - v)
    up = pltpu.roll(v, 127, 1)
    if full is not None:
        lane = lanes_of(rows)
        up = jnp.where(lane == 127, 0.0, up)
    fz = wz[p, here] * (v - up)
    fzm = pltpu.roll(fz, 1, 1)
    if full is not None:
        fzm = jnp.where(lane == 0, -full[p, here] * v, fzm)
    return (fx - gx) + (fy - gy) + (fz - fzm)


def weigh_one(q, b, wx, wy, wz, inv, f, rows, low, high, last, low_edge, high_edge, inside, full=None):
    here = slice(8, 8 + rows)
    lane = lanes_of(rows)
    wx[low - 1, here] = rcp(q[low - 1, here] + q[low, here])

    def body(p):
        v = q[p, here]
        up = pltpu.roll(v, 127, 1)
        if full is None:
            v_low = jnp.where((lane == 127) & low_edge, up, v)
        else:
            v_low = v
        up = jnp.where((lane == last) & high_edge, v, up)
        face_x = rcp(v + q[p + 1, here])
        face_y = rcp(v + q[p, 9 : 9 + rows])
        face_z = rcp(v_low + up)
        lower_z = pltpu.roll(face_z, 1, 1)
        if full is not None:
            edge = rcp(v + v)
            full[p, here] = edge
            lower_z = jnp.where(lane == 0, edge, lower_z)
        wx[p, here] = face_x
        wy[p, here] = face_y
        wz[p, here] = face_z
        total = wx[p - 1, here] + face_x + face_y + wy[p, 7 : 7 + rows] + face_z + lower_z
        value = jnp.where(inside(p), rcp(total), 0.0)
        inv[p, here] = value
        f[p, here] = value * b[p, here] * inv_center

    loop(low, high, body)


def smooth_one(b, wx, wy, wz, inv, f, r1, s, xs, rows, low, high, full=None):
    here = slice(8, 8 + rows)

    def body(p):
        rest = b[p, here] - flux_one(f, wx, wy, wz, p, rows, full)
        step = keep_coef * f[p, here] + push_coef * inv[p, here] * rest
        r1[p, here] = rest
        s[p, here] = step
        xs[p, here] = f[p, here] + step

    loop(low, high, body)


def finish_one(b, wx, wy, wz, inv, xs, f, r0, out, shift, rows, ranges, full=None):
    here = slice(8, 8 + rows)

    def start(p):
        rest = b[p, here] - flux_one(xs, wx, wy, wz, p, rows, full)
        r0[p, here] = rest
        f[p, here] = inv[p, here] * rest * inv_center

    loop(*ranges[0], start)

    def end(p):
        rest = r0[p, here] - flux_one(f, wx, wy, wz, p, rows, full)
        step = keep_coef * f[p, here] + push_coef * inv[p, here] * rest
        out[p + shift, here] = xs[p, here] + f[p, here] + step

    loop(*ranges[1], end)


def signed(lane, limit):
    return jnp.where(lane < limit, lane, lane - 128)


def middle_kernel(
    pos, own, ylo, yhi, zlo, zhi,
    payload, b3, wx3, wy3, wz3, inv3, x3, b4, wx4, wy4, wz4, inv4, x4,
    k3, q3, f3, r3, s3, k4, q4, f4, r4, s4, tmp,
):
    gx, gy, gz = pos[0], pos[1], pos[2]
    lane = lanes_of(16)

    def unpack(p, lo, hi, slot):
        for g, e in enumerate(three_rows(pos, own, ylo, yhi, p)):
            rows = slice(8 + 16 * g, 24 + 16 * g)
            part = slice(16 * g, 16 * g + 16)
            up, dn = hi[part], lo[part]
            bv = jnp.where(lane < 80, rolled(up, 64 - 32 * slot), 0.0)
            bv = jnp.where(lane >= 112, rolled(dn, 112 - 32 * slot), bv)
            b3[p, rows] = jnp.where(lane < 64, e, bv)
            kv = jnp.where(lane < 80, rolled(up, 48 - 32 * slot), 1.0)
            kv = jnp.where(lane >= 112, rolled(dn, 96 - 32 * slot), kv)
            kv = jnp.where(lane < 64, pltpu.roll(e, 64, 1), kv)
            k3[p, rows] = kv
            q3[p, rows] = 2.0 * rcp(kv)

    def column(col, slots):
        lo, hi = zlo[col], zhi[col]
        for slot in range(slots):
            unpack(col * 4 + slot, lo, hi, slot)

    loop(0, 10, lambda col: column(col, 4))
    column(10, 2)

    def region(rows, y_first, x_first, nx, ny, nz):
        y = rows_of(rows) + y_first
        z = signed(lanes_of(rows), 96)
        inside_y = ((y >= 0) | (gy > 0)) & ((y < ny) | (gy < DEV[1] - 1))
        inside_z = ((z >= 0) | (gz > 0)) & ((z < nz) | (gz < DEV[2] - 1))
        inside_yz = jnp.where(inside_y & inside_z, 1.0, 0.0)

        def inside(p):
            x = p + x_first
            inside_x = ((x >= 0) | (gx > 0)) & ((x < nx) | (gx < DEV[0] - 1))
            return inside_yz * jnp.where(inside_x, 1.0, 0.0) > 0.5

        return inside

    low_edge, high_edge = gz == 0, gz == DEV[2] - 1
    inside = region(R3, -16, -13, 16, 16, 64)
    weigh_one(q3, b3, wx3, wy3, wz3, inv3, f3, R3, 1, N3 - 1, 63, low_edge, high_edge, inside)
    smooth_one(b3, wx3, wy3, wz3, inv3, f3, r3, s3, x3, R3, 2, N3 - 2)

    def pick(i, j):
        target = signed(j, 64)
        return ((signed(i, 96) >> 1) == target) & (target >= -6) & (target < 38)

    narrow = square(pick, 0.125)
    valid = (lanes_of(R4) < 38) | (lanes_of(R4) >= 122)
    row = rows_of(R4)

    def coarse_k(i):
        p = 2 * i + 1
        tmp[1, 8:56] = k3[p, 8:56] + k3[p + 1, 8:56]
        value = tmp[1, pl.ds(12, 24, stride=2)] + tmp[1, pl.ds(13, 24, stride=2)]
        value = jnp.where(valid, select_dot(value, narrow), 1.0)
        value = jnp.where((row == 5) & (gy == 0), pltpu.roll(value, R4 - 1, 0), value)
        value = jnp.where((row == 14) & (gy == DEV[1] - 1), pltpu.roll(value, 1, 0), value)
        k4[i, 8:32] = value

    def coarse_b(i):
        p = 2 * i + 1
        total = r3[p, 8:56] + r3[p + 1, 8:56] - flux_one(s3, wx3, wy3, wz3, p, R3)
        tmp[0, 8:56] = total - flux_one(s3, wx3, wy3, wz3, p + 1, R3)
        value = tmp[0, pl.ds(12, 24, stride=2)] + tmp[0, pl.ds(13, 24, stride=2)]
        b4[i, 8:32] = select_dot(value, narrow)

    loop(0, N4, coarse_k)
    loop(1, N4 - 1, coarse_b)
    k4[5, 8:32] = jnp.where(gx == 0, k4[6, 8:32], k4[5, 8:32])
    k4[14, 8:32] = jnp.where(gx == DEV[0] - 1, k4[13, 8:32], k4[14, 8:32])

    def invert(i):
        q4[i, 8:32] = 8.0 * rcp(k4[i, 8:32])

    loop(0, N4, invert)
    inside = region(R4, -6, -6, 8, 8, 32)
    weigh_one(q4, b4, wx4, wy4, wz4, inv4, f4, R4, 1, N4 - 1, 31, low_edge, high_edge, inside)
    smooth_one(b4, wx4, wy4, wz4, inv4, f4, r4, s4, x4, R4, 2, N4 - 2)

    spread = square(lambda i, j: (i < 32) & ((i >> 1) == (j & 15)), 0.125)
    slot = lanes_of(4) >> 4
    quad = rows_of(4)
    parts = [[None, None], [None, None]]
    for i in range(4):
        p = 2 * i + 6
        total = r4[p, 8:32] + r4[p + 1, 8:32] - flux_one(s4, wx4, wy4, wz4, p, R4)
        tmp[0, 8:32] = total - flux_one(s4, wx4, wy4, wz4, p + 1, R4)
        tmp[1, 8:32] = k4[p, 8:32] + k4[p + 1, 8:32]
        mine = slot == (i % 2) * 4 + quad
        for a in range(2):
            value = tmp[a, pl.ds(14, 4, stride=2)] + tmp[a, pl.ds(15, 4, stride=2)]
            value = jnp.where(mine, select_dot(value, spread), 0.0)
            value = jnp.sum(value, axis=0, keepdims=True)
            old = parts[a][i // 2]
            parts[a][i // 2] = value if old is None else old + value
    for a in range(2):
        for g in range(2):
            payload[2 * a + g : 2 * a + g + 1] = parts[a][g]


def exchange_blocks(value):
    row = rows_of(8)
    group = lanes_of(8) >> 4
    for bit in (1, 2):
        upper = pltpu.roll(pltpu.roll(value, 8 - bit, 0), 16 * bit, 1)
        lower = pltpu.roll(pltpu.roll(value, bit, 0), 128 - 16 * bit, 1)
        moved = jnp.where((row & bit) == 0, upper, lower)
        value = jnp.where((row & bit) == (group & bit), value, moved)
    moved = pltpu.roll(pltpu.roll(value, 4, 0), 64, 1)
    return jnp.where((row & 4) == (group & 4), value, moved)


WHOLE = ((16, 32, 128), (8, 16, 64), (4, 8, 32))


def up_kernel(
    pos, recv, b3, wx3, wy3, wz3, inv3, x3, b4, wx4, wy4, wz4, inv4, x4,
    eb, wx, wy, wz, inv, xs,
    out, *scratch,
):
    gx, gy, gz = pos[0], pos[1], pos[2]
    levels = [scratch[12 * i : 12 * i + 12] for i in range(3)]
    e5, e6, full, f4, r4, e4, y4, f3, r3, e3, y3, f2, r2, y2, tmp = scratch[36:]

    for level, (nx, ny, nz) in enumerate(WHOLE):
        b, k, q, wx_, wy_, wz_, inv_, f, r, s, x, r0 = levels[level]
        for ref in (f, s, x):
            ref[0] = jnp.zeros(ref.shape[1:], F32)
            ref[nx + 1] = jnp.zeros(ref.shape[1:], F32)

            def clear(p, ref=ref, ny=ny):
                ref[p, 0:8] = jnp.zeros((8, 128), F32)
                ref[p, 8 + ny : 16 + ny] = jnp.zeros((8, 128), F32)

            loop(1, nx + 1, clear)
    for p in (0, 1, 2, 19, 20, 21):
        e5[p] = jnp.zeros(e5.shape[1:], F32)

    def clear(p):
        e5[p, 0:8] = jnp.zeros((8, 128), F32)
        e5[p, 40:48] = jnp.zeros((8, 128), F32)

    loop(3, 19, clear)

    b5, k5 = levels[0][0], levels[0][1]

    def unpack(d):
        dx, dy = d // 8, d % 8
        rows = pl.ds(8 + 4 * dy, 4)
        for kind in range(4):
            value = exchange_blocks(recv[pl.ds(d * 32 + kind, 8, stride=4)])
            target = (b5, k5)[kind // 2]
            p = 1 + 4 * dx + 2 * (kind % 2)
            target[p, rows] = value[0:4]
            target[p + 1, rows] = value[4:8]

    loop(0, 32, unpack)

    def ends(level):
        nx, ny, nz = WHOLE[level]
        k, q = levels[level][1], levels[level][2]
        factor = 0.5 * 4.0 ** (level + 3)

        def invert(p):
            value = factor * rcp(k[p, 8 : 8 + ny])
            q[p, 8 : 8 + ny] = value
            q[p, 7:8] = value[0:1]
            q[p, 8 + ny : 9 + ny] = value[ny - 1 : ny]

        loop(1, nx + 1, invert)
        q[0] = q[1]
        q[nx + 1] = q[nx]

    def down(level):
        nx, ny, nz = WHOLE[level]
        b, k, q, wx_, wy_, wz_, inv_, f, r, s, x, r0 = levels[level]
        edge = full if level == 0 else None
        ends(level)

        def below(p):
            wy_[p, 7:8] = rcp(q[p, 7:8] + q[p, 8:9])

        loop(1, nx + 1, below)
        lane = lanes_of(ny)
        weigh_one(
            q, b, wx_, wy_, wz_, inv_, f, ny, 1, nx + 1, nz - 1, True, True,
            lambda p: lane < nz, edge,
        )
        smooth_one(b, wx_, wy_, wz_, inv_, f, r, s, x, ny, 1, nx + 1, edge)
        if level == 2:
            return
        nb, nk = levels[level + 1][0], levels[level + 1][1]
        half = nz // 2
        narrow = square(lambda i, j: ((i >> 1) == j) & (j < half), 0.125)
        valid = lanes_of(ny // 2) < half

        def coarsen(i):
            p = 2 * i - 1
            here = slice(8, 8 + ny)
            total = r[p, here] + r[p + 1, here] - flux_one(s, wx_, wy_, wz_, p, ny, edge)
            tmp[0, here] = total - flux_one(s, wx_, wy_, wz_, p + 1, ny, edge)
            tmp[1, here] = k[p, here] + k[p + 1, here]
            count = ny // 2
            for a, target in enumerate((nb, nk)):
                value = tmp[a, pl.ds(8, count, stride=2)] + tmp[a, pl.ds(9, count, stride=2)]
                value = select_dot(value, narrow)
                if a == 1:
                    value = jnp.where(valid, value, 1.0)
                target[i, 8 : 8 + count] = value

        loop(1, nx // 2 + 1, coarsen)

    for level in range(3):
        down(level)

    def up(level, coarse, target, shift):
        nx, ny, nz = WHOLE[level]
        b, k, q, wx_, wy_, wz_, inv_, f, r, s, x, r0 = levels[level]
        edge = full if level == 0 else None
        widen = square(lambda i, j: (i == (j >> 1)) & (j < nz), 1.0)
        count = ny // 2

        def add(i):
            value = select_dot(coarse[i, 8 : 8 + count], widen)
            tmp[0, pl.ds(8, count, stride=2)] = value
            tmp[0, pl.ds(9, count, stride=2)] = value
            wide = tmp[0, 8 : 8 + ny]
            x[2 * i - 1, 8 : 8 + ny] += wide
            x[2 * i, 8 : 8 + ny] += wide

        loop(1, nx // 2 + 1, add)
        span = (1, nx + 1)
        finish_one(b, wx_, wy_, wz_, inv_, x, f, r0, target, shift, ny, (span, span), edge)

    up(1, levels[2][10], e6, 0)
    up(0, e6, e5, 2)

    def pick_four(i, j):
        return i == gz * 16 + (signed(j, 64) >> 1)

    widen = square(pick_four, 1.0)

    def add_four(i):
        value = select_dot(e5[gx * 4 + i, pl.ds(5 + 4 * gy, 12)], widen)
        tmp[0, pl.ds(8, 12, stride=2)] = value
        tmp[0, pl.ds(9, 12, stride=2)] = value
        wide = tmp[0, 8:32]
        y4[2 * i, 8:32] = x4[2 * i, 8:32] + wide
        y4[2 * i + 1, 8:32] = x4[2 * i + 1, 8:32] + wide

    loop(1, 9, add_four)
    finish_one(b4, wx4, wy4, wz4, inv4, y4, f4, r4, e4, 0, R4, ((3, 17), (4, 16)))

    widen3 = square(lambda i, j: signed(i, 64) == (signed(j, 96) >> 1), 1.0)

    def add_three(i):
        value = select_dot(e4[i, 8:32], widen3)
        tmp[0, pl.ds(12, 24, stride=2)] = value
        tmp[0, pl.ds(13, 24, stride=2)] = value
        wide = tmp[0, 8:56]
        y3[2 * i + 1, 8:56] = x3[2 * i + 1, 8:56] + wide
        y3[2 * i + 2, 8:56] = x3[2 * i + 2, 8:56] + wide

    tmp[0, 8:16] = jnp.zeros((8, 128), F32)
    loop(4, 16, add_three)
    finish_one(b3, wx3, wy3, wz3, inv3, y3, f3, r3, e3, 0, R3, ((11, 31), (12, 30)))

    wide0 = square(lambda i, j: i == (j >> 1), 1.0)
    wide1 = square(lambda i, j: signed(i, 96) == ((jnp.where(j < 64, j + 128, j - 128)) >> 1), 1.0)

    def add_two(i):
        e = e3[i + 11, 22:46]
        for c, matrix in enumerate((wide0, wide1)):
            value = select_dot(e, matrix)
            tmp[c, pl.ds(8, 24, stride=2)] = value
            tmp[c, pl.ds(9, 24, stride=2)] = value
            wide = tmp[c, 8:48]
            y2[c, 2 * i, 8:48] = xs[c, 2 * i, 8:48] + wide
            y2[c, 2 * i + 1, 8:48] = xs[c, 2 * i + 1, 8:48] + wide

    loop(1, 19, add_two)
    here = slice(8, 48)

    def start(p):
        flux = flux_two(y2, wx, wy, wz, p, 8, R2, 2)
        for c in range(2):
            rest = eb[c, p, here] - flux[c]
            r2[c, p, here] = rest
            f2[c, p, here] = inv[c, p, here] * rest * inv_center

    loop(3, 37, start)
    core = slice(12, 44)

    def end(i):
        p = i + 4
        rest = r2[0, p, core] - flux_two(f2, wx, wy, wz, p, 12, 32, 1)[0]
        first = f2[0, p, core]
        step = keep_coef * first + push_coef * inv[0, p, core] * rest
        out[i] = y2[0, p, core] + first + step

    loop(0, 32, end)


def call(kernel, args, outs, scratch=()):
    return pl.pallas_call(
        kernel,
        out_shape=[jax.ShapeDtypeStruct(shape, F32) for shape in outs],
        in_specs=[pl.BlockSpec(memory_space=pltpu.SMEM)]
        + [pl.BlockSpec(memory_space=pltpu.VMEM)] * (len(args) - 1),
        out_specs=[pl.BlockSpec(memory_space=pltpu.VMEM)] * len(outs),
        scratch_shapes=[pltpu.VMEM(shape, F32) for shape in scratch],
        compiler_params=pltpu.CompilerParams(vmem_limit_bytes=56 * 1024 * 1024),
    )(*args)


def swap(low, high, axis):
    count = lax.axis_size(axis)
    ring = range(count)
    before = lax.ppermute(high, axis, [(i, (i + 1) % count) for i in ring])
    after = lax.ppermute(low, axis, [(i, (i - 1) % count) for i in ring])
    return before, after


def shards(b, k):
    pos = jnp.stack([lax.axis_index(axis) for axis in AXES]).astype(jnp.int32)
    low = jnp.concatenate([b[:4], k[:4]])
    high = jnp.concatenate([b[28:], k[28:]])
    xlo, xhi = swap(low, high, "gx")
    low, high = call(rows_kernel, (pos, b, k, xlo, xhi), [(N2, 8, 128)] * 2)
    ylo, yhi = swap(low, high, "gy")
    ext2 = (N2, T2, 128)
    low, high = call(
        lanes_kernel, (pos, b, k, xlo, xhi, ylo, yhi), [(3, R2, 128)] * 2, [ext2] * 2
    )
    zlo, zhi = swap(low, high, "gz")
    two = (2,) + ext2
    bk3, *state2 = call(
        down_kernel,
        (pos, b, k, xlo, xhi, ylo, yhi, zlo, zhi),
        [(16, 16, 128)] + [two] * 6,
        [ext2] + [two] * 4 + [(2, R2, 128), (2, 32, 128)],
    )
    xlo, xhi = swap(bk3, bk3, "gx")
    (own,) = call(planes_kernel, (pos, bk3, xlo, xhi), [(N3, 16, 128)])
    ylo, yhi = swap(own, own, "gy")
    low, high = call(slots_kernel, (pos, own, ylo, yhi), [(11, 48, 128)] * 2)
    zlo, zhi = swap(low, high, "gz")
    three, four = (N3, T3, 128), (N4, T4, 128)
    payload, *state = call(
        middle_kernel,
        (pos, own, ylo, yhi, zlo, zhi),
        [(4, 128)] + [three] * 6 + [four] * 6,
        [three] * 5 + [four] * 5 + [(2, 64, 128)],
    )
    copies = jnp.broadcast_to(payload[None], (256, 4, 128))
    recv = lax.all_to_all(copies, AXES, 0, 0, tiled=True).reshape(1024, 128)
    scratch = []
    for nx, ny, _ in WHOLE:
        scratch += [(nx + 2, ny + 16, 128)] * 12
    scratch += [(22, 48, 128), (10, 32, 128), (18, 48, 128)]
    scratch += [four] * 4 + [three] * 4 + [two] * 3 + [(2, 64, 128)]
    (out,) = call(up_kernel, (pos, recv, *state, *state2), [(32, 32, 128)], scratch)
    return out


def solution(mesh):
    spec = P(*AXES)
    return jax.shard_map(shards, mesh=mesh, in_specs=(spec, spec), out_specs=spec, check_vma=False)
```

time: 857 us -> 231 us (0.27); the launches traced: 843 us -> 230 us
  starting transfers between devices: 323 us -> 23.8 us
  local copies, waits for them, and re-layouts: 208 us -> 6.86 us
  Pallas kernels: 0 us -> 140 us
  other arithmetic: 124 us -> 0.63 us
  waiting for transfers between devices: 126 us -> 28.6 us
  blocking collectives: 59.9 us -> 29.7 us
    ppermute x120 -> x12, starting transfers between devices: 323 us -> 23.8 us  [the longest x6 14.1 us: swap(): before = lax.ppermute(high, axis, [(i, (i + 1) % count) for i in ring])]
    pallas_call x0 -> x7, Pallas kernels: none -> 140 us  [call(): pl.pallas_call(kernel, out_shape=[jax.ShapeDtypeStruct(shape, F32) for sh...]
    reshape x12 -> x0, local copies, waits for them, and re-layouts: 122 us -> none  [the longest x6 84.6 us: restrict(): values.reshape(values.shape[0] // 2, 2, values.shape[1] // 2, 2, values.s...]
    ppermute x120 -> x12, waiting for transfers between devices: 126 us -> 28.6 us  [the longest x6 15.6 us: swap(): before = lax.ppermute(high, axis, [(i, (i + 1) % count) for i in ring])]
    all_gather x1 -> x0, blocking collectives: 59.9 us -> none  [shards(): gathered = lax.all_gather(stacked, ('gx', 'gy', 'gz'), axis=0, tiled=True)]
    reduce_sum x11 -> x0, other arithmetic: 43.1 us -> none  [restrict(): return reshaped.mean(axis=(1, 3, 5))]
    all_to_all x0 -> x1, blocking collectives: none -> 29.7 us  [shards(): recv = lax.all_to_all(copies, AXES, 0, 0, tiled=True).reshape(1024, 128)]
    add x17 -> x0, other arithmetic: 29 us -> none  [the longest x4 10.7 us: descend_near(): second_step = keep_coef * first_step + push_coef * inverse * rest_one]
  transfers between devices with their start and end apart: 120 -> 12, of which waited for: 42 -> 11; matrix products, arithmetic and copies ran while one was open for 20% -> 0% of each run, Pallas kernels for 0% -> 0%
where the time goes in v1:
time: 231 us; the launch traced here: 230 us
  Pallas kernels  140 us (61%)
  blocking collectives  29.7 us (13%)
  waiting for transfers between devices  28.6 us (12%)
  starting transfers between devices  23.8 us (10%)
  local copies, waits for them, and re-layouts  6.86 us (3%)
    pallas_call x7, Pallas kernels, call(): pl.pallas_call(kernel, out_shape=[jax.ShapeDtypeStruct(shape, F32) for sh...  140 us
    all_to_all x1, blocking collectives, shards(): recv = lax.all_to_all(copies, AXES, 0, 0, tiled=True).reshape(1024, 128)  29.7 us
    ppermute x6, waiting for transfers between devices, swap(): before = lax.ppermute(high, axis, [(i, (i + 1) % count) for i in ring])  15.6 us
    ppermute x6, starting transfers between devices, swap(): before = lax.ppermute(high, axis, [(i, (i + 1) % count) for i in ring])  14.1 us
    ppermute x6, waiting for transfers between devices, swap(): after = lax.ppermute(low, axis, [(i, (i - 1) % count) for i in ring])  13 us
    ppermute x6, starting transfers between devices, swap(): after = lax.ppermute(low, axis, [(i, (i - 1) % count) for i in ring])  9.7 us
    unnamed x24, local copies, waits for them, and re-layouts  5.15 us
  transfers between devices with their start and end apart: 12, of which 11 were waited for; matrix products, arithmetic and copies ran while one was open for 0% of the time, Pallas kernels for 0%

profile of v1, /device:TPU:1, one launch (start us, length us, event | category | flops | bytes accessed | tf_op | source)
XLA Modules:
  0.0 230.2 jit_solution(8320432945209808450)
XLA Ops:
  0.0 1.0 fusion
  1.0 2.1 collective-permute-start
  3.1 1.4 collective-permute-start.1
  4.5 0.6 pad_add_fusion.pos
  5.1 1.6 collective-permute-done.xlo
  6.7 0.0 copy-start.2
  6.7 0.3 collective-permute-done.1.xhi
  7.0 0.4 copy-done.2
  7.4 0.6 copy-done.3
  8.0 2.3 shard_map.28
  10.3 2.4 %collective-permute-start.2 = (f32[40,8,128]{2,1,0:T(8,128)}, f32[40,8,128]{2,1,0:T(8,128)S(1)}, u32[]{:S(2)}, u32[]{:S(2)}) collective-permute-start(f32[40,8,128]{2,1,0:T(8,128)} %get-tuple-element.31), channel_id=1, source_target_pairs={{0,8},{8,16},{16,24},{24,32},{32,40},{40,48},{48,56},{56,0},{1,9},... | collective-permute-start | bytes 491528 | tf_op jit(solution)/shard_map/ppermute | solution.py:714
  12.7 3.9 %collective-permute-start.3 = (f32[40,8,128]{2,1,0:T(8,128)}, f32[40,8,128]{2,1,0:T(8,128)S(1)}, u32[]{:S(2)}, u32[]{:S(2)}) collective-permute-start(f32[40,8,128]{2,1,0:T(8,128)} %get-tuple-element.32), channel_id=1, source_target_pairs={{0,56},{8,0},{16,8},{24,16},{32,24},{40,32},{48,40},{56,48},{1,57}... | collective-permute-start | bytes 491528 | tf_op jit(solution)/shard_map/ppermute | solution.py:715
  16.6 2.9 %collective-permute-done.2.ylo = f32[40,8,128]{2,1,0:T(8,128)S(1)} collective-permute-done((f32[40,8,128]{2,1,0:T(8,128)}, f32[40,8,128]{2,1,0:T(8,128)S(1)}, u32[]{:S(2)}, u32[]{:S(2)}) %collective-permute-start.2) | collective-permute-done | bytes 163872 | tf_op jit(solution)/shard_map/ppermute | solution.py:714
  19.5 0.0 collective-permute-done.3.yhi
  19.5 0.7 copy-done.4
  20.2 0.7 copy-done.5
  20.8 3.6 %shard_map.29 = (f32[3,40,128]{2,1,0:T(8,128)}, f32[3,40,128]{2,1,0:T(8,128)}) custom-call(s32[3]{0:T(128)} %pad_add_fusion.pos, f32[32,32,128]{2,1,0:T(8,128)} %b.5, f32[32,32,128]{2,1,0:T(8,128)} %k.5, f32[8,32,128]{2,1,0:T(8,128)} %copy-done.2, f32[8,32,128]{2,1,0:T(8,128)} %copy-done.3, f32[40,8,128]{2,1,0:T(8,128)} %copy-done.4, f32[40,8,128]{2,1,0:T(8,128)} %copy-done.5), custom_call_target="tpu_custom_call" | custom-call | tf_op jit(solution)/shard_map/pallas_call | solution.py:700
  24.5 3.6 %collective-permute-start.4 = (f32[3,40,128]{2,1,0:T(8,128)}, f32[3,40,128]{2,1,0:T(8,128)S(1)}, u32[]{:S(2)}, u32[]{:S(2)}) collective-permute-start(f32[3,40,128]{2,1,0:T(8,128)} %get-tuple-element.33), channel_id=1, source_target_pairs={{0,1},{1,2},{2,3},{3,4},{4,5},{5,6},{6,7},{7,0},{8,9},{9,10},{10,1... | collective-permute-start | bytes 184328 | tf_op jit(solution)/shard_map/ppermute | solution.py:714
  28.1 0.0 collective-permute-start.5
  28.1 1.6 collective-permute-done.4.zlo
  29.7 2.2 collective-permute-done.5.zhi
  32.0 0.0 copy-done.10
  32.0 0.6 copy-done.11
  32.6 26.4 %shard_map.30 = (f32[16,16,128]{2,1,0:T(8,128)}, f32[2,40,56,128]{3,2,1,0:T(8,128)}, f32[2,40,56,128]{3,2,1,0:T(8,128)}, f32[2,40,56,128]{3,2,1,0:T(8,128)}, f32...) custom-call(s32[3]{0:T(128)} %pad_add_fusion.pos, f32[32,32,128]{2,1,0:T(8,128)} %b.5, ...), custom_call_target="tpu_custom_call" | custom-call | tf_op jit(solution)/shard_map/pallas_call | solution.py:700
  59.0 2.1 collective-permute-start.7
  61.1 0.0 collective-permute-start.6
  61.1 2.5 %collective-permute-done.7.xhi = f32[16,16,128]{2,1,0:T(8,128)S(1)} collective-permute-done((f32[16,16,128]{2,1,0:T(8,128)}, f32[16,16,128]{2,1,0:T(8,128)S(1)}, u32[]{:S(2)}, u32[]{:S(2)}) %collective-permute-start.7) | collective-permute-done | bytes 131104 | tf_op jit(solution)/shard_map/ppermute | solution.py:715
  63.6 2.7 %collective-permute-done.6.xlo = f32[16,16,128]{2,1,0:T(8,128)S(1)} collective-permute-done((f32[16,16,128]{2,1,0:T(8,128)}, f32[16,16,128]{2,1,0:T(8,128)S(1)}, u32[]{:S(2)}, u32[]{:S(2)}) %collective-permute-start.6) | collective-permute-done | bytes 131104 | tf_op jit(solution)/shard_map/ppermute | solution.py:714
  66.4 0.0 copy-done.8
  66.4 0.7 copy-done.9
  67.0 1.8 shard_map.31.own
  68.8 2.3 %collective-permute-start.9 = (f32[42,16,128]{2,1,0:T(8,128)}, f32[42,16,128]{2,1,0:T(8,128)S(1)}, u32[]{:S(2)}, u32[]{:S(2)}) collective-permute-start(f32[42,16,128]{2,1,0:T(8,128)} %shard_map.31.own), channel_id=1, source_target_pairs={{0,56},{8,0},{16,8},{24,16},{32,24},{40,32},{48,40},{56,48},{1,57}... | collective-permute-start | bytes 1032200 | tf_op jit(solution)/shard_map/ppermute | solution.py:715
  71.1 0.0 collective-permute-start.8
  71.1 5.6 %collective-permute-done.9.yhi = f32[42,16,128]{2,1,0:T(8,128)S(1)} collective-permute-done((f32[42,16,128]{2,1,0:T(8,128)}, f32[42,16,128]{2,1,0:T(8,128)S(1)}, u32[]{:S(2)}, u32[]{:S(2)}) %collective-permute-start.9) | collective-permute-done | bytes 344096 | tf_op jit(solution)/shard_map/ppermute | solution.py:715
  76.7 3.0 %collective-permute-done.8.ylo = f32[42,16,128]{2,1,0:T(8,128)S(1)} collective-permute-done((f32[42,16,128]{2,1,0:T(8,128)}, f32[42,16,128]{2,1,0:T(8,128)S(1)}, u32[]{:S(2)}, u32[]{:S(2)}) %collective-permute-start.8) | collective-permute-done | bytes 344096 | tf_op jit(solution)/shard_map/ppermute | solution.py:714
  79.7 0.0 copy-done
  79.7 0.8 copy-done.1
  80.5 4.1 %shard_map.32 = (f32[11,48,128]{2,1,0:T(8,128)}, f32[11,48,128]{2,1,0:T(8,128)}) custom-call(s32[3]{0:T(128)} %pad_add_fusion.pos, f32[42,16,128]{2,1,0:T(8,128)} %shard_map.31.own, f32[42,16,128]{2,1,0:T(8,128)} %copy-done.1, f32[42,16,128]{2,1,0:T(8,128)} %copy-done), custom_call_target="tpu_custom_call" | custom-call | tf_op jit(solution)/shard_map/pallas_call | solution.py:700
  84.6 6.0 %collective-permute-start.10 = (f32[11,48,128]{2,1,0:T(8,128)}, f32[11,48,128]{2,1,0:T(8,128)S(1)}, u32[]{:S(2)}, u32[]{:S(2)}) collective-permute-start(f32[11,48,128]{2,1,0:T(8,128)} %get-tuple-element.36), channel_id=1, source_target_pairs={{0,1},{1,2},{2,3},{3,4},{4,5},{5,6},{6,7},{7,0},{8,9},{9,10},{10,1... | collective-permute-start | bytes 811016 | tf_op jit(solution)/shard_map/ppermute | solution.py:714
  90.6 0.0 collective-permute-start.11
  90.6 3.7 %collective-permute-done.10.zlo = f32[11,48,128]{2,1,0:T(8,128)S(1)} collective-permute-done((f32[11,48,128]{2,1,0:T(8,128)}, f32[11,48,128]{2,1,0:T(8,128)S(1)}, u32[]{:S(2)}, u32[]{:S(2)}) %collective-permute-start.10) | collective-permute-done | bytes 270368 | tf_op jit(solution)/shard_map/ppermute | solution.py:714
  94.4 2.4 %collective-permute-done.11.zhi = f32[11,48,128]{2,1,0:T(8,128)S(1)} collective-permute-done((f32[11,48,128]{2,1,0:T(8,128)}, f32[11,48,128]{2,1,0:T(8,128)S(1)}, u32[]{:S(2)}, u32[]{:S(2)}) %collective-permute-start.11) | collective-permute-done | bytes 270368 | tf_op jit(solution)/shard_map/ppermute | solution.py:715
  96.7 0.0 copy-done.6
  96.7 0.7 copy-done.7
  97.5 34.5 %shard_map.33 = (f32[4,128]{1,0:T(4,128)}, f32[42,64,128]{2,1,0:T(8,128)}, f32[42,64,128]{2,1,0:T(8,128)}, f32[42,64,128]{2,1,0:T(8,128)}, f32[42,64,128]{2,1,0:...) custom-call(s32[3]{0:T(128)} %pad_add_fusion.pos, ...), custom_call_target="tpu_custom_call" | custom-call | tf_op jit(solution)/shard_map/pallas_call | solution.py:700
  131.9 0.8 broadcast_in_dim.2
  132.7 29.7 %all_to_all.5 = f32[256,4,128]{2,1,0:T(4,128)} all-to-all(f32[256,4,128]{2,1,0:T(4,128)S(1)} %broadcast_in_dim.2), channel_id=1, replica_groups=mesh['gx'=4,'gy'=8,'gz'=8] {'gx','gy','gz'}, dimensions={0} | all-to-all | bytes 1048576 | tf_op jit(solution)/shard_map/all_to_all | solution.py:751
  162.4 67.8 %shard_map.34 = f32[32,32,128]{2,1,0:T(8,128)} custom-call(s32[3]{0:T(128)} %pad_add_fusion.pos, f32[1024,128]{1,0:T(8,128)} %bitcast.4, f32[42,64,128]{2,1,0:T(8,128)} %get-tuple-element.39.b3, f32[42,64,128]{2,1,0:T(8,128)} %get-tuple-element.40.wx3, f32[42,64,128]{2,1,0:T(8,128)} %get-tuple-element.41.wy3, f32[42,64,128]{2,1,0:T(8,128)} %get-tuple-element.42.wz3, ...), custom_call_target="tpu_custom_call" | custom-call | tf_op jit(solution)/shard_map/pallas_call | solution.py:700
  (13 shorter events, 0.0 us)
Async XLA Ops:
  1.0 5.7 %collective-permute-start = (f32[8,32,128]{2,1,0:T(8,128)S(1)}, f32[8,32,128]{2,1,0:T(8,128)S(1)}, u32[]{:S(2)}, u32[]{:S(2)}) collective-permute-start(f32[8,32,128]{2,1,0:T(8,128)S(1)} %pad_maximum_fusion), channel_id=1, source_target_pairs={{0,64},{64,128},{128,192},{192,0},{1,65},{65,129},{129,193},{193,1... | collective-permute-start | bytes 393224 | tf_op jit(solution)/shard_map/ppermute | solution.py:714
  3.1 3.9 %collective-permute-start.1 = (f32[8,32,128]{2,1,0:T(8,128)S(1)}, f32[8,32,128]{2,1,0:T(8,128)S(1)}, u32[]{:S(2)}, u32[]{:S(2)}) collective-permute-start(f32[8,32,128]{2,1,0:T(8,128)S(1)} %pad_maximum_fusion.1), channel_id=1, source_target_pairs={{0,192},{64,0},{128,64},{192,128},{1,193},{65,1},{129,65},{193,129... | collective-permute-start | bytes 393224 | tf_op jit(solution)/shard_map/ppermute | solution.py:715
  6.7 0.7 copy-start.2
  7.4 0.7 copy-start.3
  10.3 9.2 %collective-permute-start.2 = (f32[40,8,128]{2,1,0:T(8,128)}, f32[40,8,128]{2,1,0:T(8,128)S(1)}, u32[]{:S(2)}, u32[]{:S(2)}) collective-permute-start(f32[40,8,128]{2,1,0:T(8,128)} %get-tuple-element.31), channel_id=1, source_target_pairs={{0,8},{8,16},{16,24},{24,32},{32,40},{40,48},{48,56},{56,0},{1,9},... | collective-permute-start | bytes 491528 | tf_op jit(solution)/shard_map/ppermute | solution.py:714
  12.7 6.9 %collective-permute-start.3 = (f32[40,8,128]{2,1,0:T(8,128)}, f32[40,8,128]{2,1,0:T(8,128)S(1)}, u32[]{:S(2)}, u32[]{:S(2)}) collective-permute-start(f32[40,8,128]{2,1,0:T(8,128)} %get-tuple-element.32), channel_id=1, source_target_pairs={{0,56},{8,0},{16,8},{24,16},{32,24},{40,32},{48,40},{56,48},{1,57}... | collective-permute-start | bytes 491528 | tf_op jit(solution)/shard_map/ppermute | solution.py:715
  19.5 0.7 copy-start.4
  20.2 0.7 copy-start.5
  24.5 5.2 %collective-permute-start.4 = (f32[3,40,128]{2,1,0:T(8,128)}, f32[3,40,128]{2,1,0:T(8,128)S(1)}, u32[]{:S(2)}, u32[]{:S(2)}) collective-permute-start(f32[3,40,128]{2,1,0:T(8,128)} %get-tuple-element.33), channel_id=1, source_target_pairs={{0,1},{1,2},{2,3},{3,4},{4,5},{5,6},{6,7},{7,0},{8,9},{9,10},{10,1... | collective-permute-start | bytes 184328 | tf_op jit(solution)/shard_map/ppermute | solution.py:714
  28.1 3.9 %collective-permute-start.5 = (f32[3,40,128]{2,1,0:T(8,128)}, f32[3,40,128]{2,1,0:T(8,128)S(1)}, u32[]{:S(2)}, u32[]{:S(2)}) collective-permute-start(f32[3,40,128]{2,1,0:T(8,128)} %get-tuple-element.34), channel_id=1, source_target_pairs={{0,7},{1,0},{2,1},{3,2},{4,3},{5,4},{6,5},{7,6},{8,15},{9,8},{10,9... | collective-permute-start | bytes 184328 | tf_op jit(solution)/shard_map/ppermute | solution.py:715
  29.7 2.2 copy-start.10
  32.0 0.6 copy-start.11
  59.0 4.6 %collective-permute-start.7 = (f32[16,16,128]{2,1,0:T(8,128)}, f32[16,16,128]{2,1,0:T(8,128)S(1)}, u32[]{:S(2)}, u32[]{:S(2)}) collective-permute-start(f32[16,16,128]{2,1,0:T(8,128)} %get-tuple-element.35.bk), channel_id=1, source_target_pairs={{0,192},{64,0},{128,64},{192,128},{1,193},{65,1},{129,65},{193,129... | collective-permute-start | bytes 393224 | tf_op jit(solution)/shard_map/ppermute | solution.py:715
  61.1 5.2 %collective-permute-start.6 = (f32[16,16,128]{2,1,0:T(8,128)}, f32[16,16,128]{2,1,0:T(8,128)S(1)}, u32[]{:S(2)}, u32[]{:S(2)}) collective-permute-start(f32[16,16,128]{2,1,0:T(8,128)} %get-tuple-element.35.bk), channel_id=1, source_target_pairs={{0,64},{64,128},{128,192},{192,0},{1,65},{65,129},{129,193},{193,1... | collective-permute-start | bytes 393224 | tf_op jit(solution)/shard_map/ppermute | solution.py:714
  63.6 2.7 %copy-start.8 = (f32[16,16,128]{2,1,0:T(8,128)}, f32[16,16,128]{2,1,0:T(8,128)S(1)}, u32[]{:S(2)}) copy-start(f32[16,16,128]{2,1,0:T(8,128)S(1)} %collective-permute-done.7.xhi) | copy-start | bytes 393220
  66.4 0.7 copy-start.9
  68.8 7.9 %collective-permute-start.9 = (f32[42,16,128]{2,1,0:T(8,128)}, f32[42,16,128]{2,1,0:T(8,128)S(1)}, u32[]{:S(2)}, u32[]{:S(2)}) collective-permute-start(f32[42,16,128]{2,1,0:T(8,128)} %shard_map.31.own), channel_id=1, source_target_pairs={{0,56},{8,0},{16,8},{24,16},{32,24},{40,32},{48,40},{56,48},{1,57}... | collective-permute-start | bytes 1032200 | tf_op jit(solution)/shard_map/ppermute | solution.py:715
  71.1 8.6 %collective-permute-start.8 = (f32[42,16,128]{2,1,0:T(8,128)}, f32[42,16,128]{2,1,0:T(8,128)S(1)}, u32[]{:S(2)}, u32[]{:S(2)}) collective-permute-start(f32[42,16,128]{2,1,0:T(8,128)} %shard_map.31.own), channel_id=1, source_target_pairs={{0,8},{8,16},{16,24},{24,32},{32,40},{40,48},{48,56},{56,0},{1,9},... | collective-permute-start | bytes 1032200 | tf_op jit(solution)/shard_map/ppermute | solution.py:714
  76.7 3.0 %copy-start = (f32[42,16,128]{2,1,0:T(8,128)}, f32[42,16,128]{2,1,0:T(8,128)S(1)}, u32[]{:S(2)}) copy-start(f32[42,16,128]{2,1,0:T(8,128)S(1)} %collective-permute-done.9.yhi) | copy-start | bytes 1032196
  79.7 0.8 copy-start.1
  84.6 9.7 %collective-permute-start.10 = (f32[11,48,128]{2,1,0:T(8,128)}, f32[11,48,128]{2,1,0:T(8,128)S(1)}, u32[]{:S(2)}, u32[]{:S(2)}) collective-permute-start(f32[11,48,128]{2,1,0:T(8,128)} %get-tuple-element.36), channel_id=1, source_target_pairs={{0,1},{1,2},{2,3},{3,4},{4,5},{5,6},{6,7},{7,0},{8,9},{9,10},{10,1... | collective-permute-start | bytes 811016 | tf_op jit(solution)/shard_map/ppermute | solution.py:714
  90.6 6.1 %collective-permute-start.11 = (f32[11,48,128]{2,1,0:T(8,128)}, f32[11,48,128]{2,1,0:T(8,128)S(1)}, u32[]{:S(2)}, u32[]{:S(2)}) collective-permute-start(f32[11,48,128]{2,1,0:T(8,128)} %get-tuple-element.37), channel_id=1, source_target_pairs={{0,7},{1,0},{2,1},{3,2},{4,3},{5,4},{6,5},{7,6},{8,15},{9,8},{10,9... | collective-permute-start | bytes 811016 | tf_op jit(solution)/shard_map/ppermute | solution.py:715
  94.4 2.4 %copy-start.6 = (f32[11,48,128]{2,1,0:T(8,128)}, f32[11,48,128]{2,1,0:T(8,128)S(1)}, u32[]{:S(2)}) copy-start(f32[11,48,128]{2,1,0:T(8,128)S(1)} %collective-permute-done.10.zlo) | copy-start | bytes 811012
  96.7 0.7 copy-start.7

commit v2 on v1

v2 whole, which is shorter than its diff:
```python
import math

import jax
import jax.numpy as jnp
from jax import lax
from jax.experimental import pallas as pl
from jax.experimental.pallas import tpu as pltpu
from jax.sharding import PartitionSpec as P

F32 = jnp.float32
AXES = ("gx", "gy", "gz")
DEV = (4, 8, 8)

center_eig = 1.25
half_width = 0.75
rho_first = half_width / center_eig
rho_second = 1.0 / (2.0 * center_eig / half_width - rho_first)
keep_coef = rho_second * rho_first
push_coef = 2.0 * rho_second / half_width
inv_center = 1.0 / center_eig

N2, R2, T2 = 40, 40, 56
N3, R3, T3 = 42, 48, 64
N4, R4, T4 = 20, 24, 40


def rcp(value):
    guess = pl.reciprocal(value, approx=True)
    return guess * (2.0 - value * guess)


def row_pairs(ref, planes, start, count):
    even = [ref[i, pl.ds(start, count, stride=2)] for i in planes]
    odd = [ref[i, pl.ds(start + 1, count, stride=2)] for i in planes]
    return jnp.concatenate(even, axis=0) + jnp.concatenate(odd, axis=0)


def spread_rows(ref, planes, start, count, value):
    for n, i in enumerate(planes):
        part = value[n * count : (n + 1) * count]
        ref[i, pl.ds(start, count, stride=2)] = part
        ref[i, pl.ds(start + 1, count, stride=2)] = part


def lanes_of(rows):
    return lax.broadcasted_iota(jnp.int32, (rows, 128), 1)


def rows_of(rows):
    return lax.broadcasted_iota(jnp.int32, (rows, 128), 0)


def rolled(value, shift):
    shift = shift % 128
    return value if shift == 0 else pltpu.roll(value, shift, 1)


def select_dot(value, matrix):
    high = value.astype(jnp.bfloat16)
    rest = value - high.astype(F32)
    middle = rest.astype(jnp.bfloat16)
    low = (rest - middle.astype(F32)).astype(jnp.bfloat16)
    parts = jnp.concatenate([high, middle, low], axis=1)
    return jnp.dot(parts, jnp.concatenate([matrix] * 3, axis=0), preferred_element_type=F32)


def square(condition, value):
    source = lax.broadcasted_iota(jnp.int32, (128, 128), 0)
    target = lax.broadcasted_iota(jnp.int32, (128, 128), 1)
    return jnp.where(condition(source, target), value, 0.0).astype(jnp.bfloat16)


def loop(low, high, body, unroll=1):
    blocks = (high - low) // unroll
    if blocks > 1:

        @pl.loop(0, blocks)
        def _(block):
            for j in range(unroll):
                body(low + block * unroll + j)

        low += blocks * unroll
    for index in range(low, high):
        body(index)


def copy_all(pairs, sems):
    copies = [
        pltpu.make_async_copy(source, target, sems.at[n]) for n, (source, target) in enumerate(pairs)
    ]
    for copy in copies:
        copy.start()
    for copy in copies:
        copy.wait()


def edge_kernel(b, k, low, high, sems):
    copy_all(
        (
            (b.at[pl.ds(0, 3)], low.at[pl.ds(0, 3)]),
            (k.at[pl.ds(0, 4)], low.at[pl.ds(3, 4)]),
            (b.at[pl.ds(29, 3)], high.at[pl.ds(0, 3)]),
            (k.at[pl.ds(28, 4)], high.at[pl.ds(3, 4)]),
        ),
        sems,
    )


def load_kernel(b, k, bv, kv, sems):
    parts = [pl.ds(8 * n, 8) for n in range(4)]
    copy_all([(x.at[part], y.at[part]) for part in parts for x, y in ((b, bv), (k, kv))], sems)


def outer_planes(pos, k, xlo, xhi, put):
    gx = pos[0]
    for j in range(4):
        kl = jnp.where(gx == 0, k[0], xlo[6]) if j == 3 else xlo[3 + j]
        kh = jnp.where(gx == DEV[0] - 1, k[31], xhi[3]) if j == 0 else xhi[3 + j]
        put(j, xlo[max(j - 1, 0)], kl)
        put(36 + j, xhi[min(j, 2)], kh)


def rows_kernel(pos, b, k, xlo, xhi, low, high):
    def put(plane, bv, kv):
        low[plane, 0:4] = bv[0:4]
        low[plane, 4:8] = kv[0:4]
        high[plane, 0:4] = bv[28:32]
        high[plane, 4:8] = kv[28:32]

    outer_planes(pos, k, xlo, xhi, put)
    loop(0, 32, lambda i: put(i + 4, b[i], k[i]), 4)


def assemble_two(pos, b, k, xlo, xhi, ylo, yhi, eb, ek):
    gy = pos[1]

    def put(plane, bv, kv):
        eb[plane, 12:44] = bv
        ek[plane, 12:44] = kv

    outer_planes(pos, k, xlo, xhi, put)
    loop(0, 32, lambda i: put(i + 4, b[i], k[i]), 4)
    row = rows_of(4)

    def edges(i):
        eb[i, 8:12] = ylo[i, 0:4]
        eb[i, 44:48] = yhi[i, 0:4]
        ek[i, 8:12] = jnp.where((row == 3) & (gy == 0), ek[i, 12:13], ylo[i, 4:8])
        ek[i, 44:48] = jnp.where((row == 0) & (gy == DEV[1] - 1), ek[i, 43:44], yhi[i, 4:8])

    loop(0, N2, edges, 4)


def lanes_kernel(pos, b, k, xlo, xhi, ylo, yhi, low, high, eb, ek):
    assemble_two(pos, b, k, xlo, xhi, ylo, yhi, eb, ek)
    group = lanes_of(R2) >> 2

    def column(col, slots):
        lo = jnp.zeros((R2, 128), F32)
        hi = jnp.zeros((R2, 128), F32)
        for s in range(slots):
            bv = eb[col * 16 + s, 8:48]
            kv = ek[col * 16 + s, 8:48]
            first, second = group == 2 * s, group == 2 * s + 1
            lo = jnp.where(first, rolled(bv, 8 * s), lo)
            lo = jnp.where(second, rolled(kv, 8 * s + 4), lo)
            hi = jnp.where(first, rolled(bv, 8 * s + 4), hi)
            hi = jnp.where(second, rolled(kv, 8 * s + 8), hi)
        low[col] = lo
        high[col] = hi

    loop(0, 2, lambda col: column(col, 16))
    column(2, 8)


def next_plane(parts):
    edge = lanes_of(parts[0].shape[0]) >= 120
    moved = [pltpu.roll(part, 120, 1) for part in parts]
    return [jnp.where(edge, moved[(c + 1) % 3], moved[c]) for c in range(3)]


def last_plane(parts):
    edge = lanes_of(parts[0].shape[0]) < 8
    moved = [pltpu.roll(part, 8, 1) for part in parts]
    return [jnp.where(edge, moved[c - 1], moved[c]) for c in range(3)]


def merge_faces(low, high):
    return jnp.where((lanes_of(low.shape[0]) & 7) == 3, high, pltpu.roll(low, 1, 1))


def flux_strips(v_ref, wx, wy, wz, faces):
    here, above, below = slice(8, 48), slice(9, 49), slice(7, 47)
    result, through = [], []
    for t in range(2):
        v = [v_ref[t, c, here] for c in range(3)]
        ahead = next_plane(v)
        fx = [wx[t, c, here] * (v[c] - ahead[c]) for c in range(3)]
        gx = last_plane(fx)
        total = []
        for c in range(3):
            fy = wy[t, c, here] * (v[c] - v_ref[t, c, above])
            gy = wy[t, c, below] * (v_ref[t, c, below] - v[c])
            fz = wz[t, c, here] * (v[c] - pltpu.roll(v[c], 127, 1))
            through.append(fz)
            total.append((fx[c] - gx[c]) + (fy - gy) + (fz - pltpu.roll(fz, 1, 1)))
        result.append(total)
    for c in range(3):
        faces[c, here] = merge_faces(through[c], through[3 + c])
    return result


def face_lanes(faces, p, here):
    return pltpu.roll(faces[p // 16, here], 124 - 8 * (p % 16), 1)


def flux_two(v_ref, wx, wy, wz, faces, p, start, rows):
    here = slice(start, start + rows)
    above = slice(start + 1, start + rows + 1)
    below = slice(start - 1, start + rows - 1)
    lane = lanes_of(rows)
    v = v_ref[p, here]
    through = face_lanes(faces, p, here)
    fx = wx[p, here] * (v - v_ref[p + 1, here])
    gx = wx[p - 1, here] * (v_ref[p - 1, here] - v)
    fy = wy[p, here] * (v - v_ref[p, above])
    gy = wy[p, below] * (v_ref[p, below] - v)
    fz = jnp.where(lane == 127, through, wz[p, here] * (v - pltpu.roll(v, 127, 1)))
    gz = jnp.where(lane == 0, through, pltpu.roll(fz, 1, 1))
    return (fx - gx) + (fy - gy) + (fz - gz)


def weights_kernel(pos, ek, wx, wy, wz, sums, q):
    here = slice(8, 48)

    def invert(p):
        q[p, here] = 0.5 * rcp(ek[p, here])

    loop(0, N2, invert, 8)
    wx[0, here] = rcp(q[0, here] + q[1, here])

    def body(p):
        v = q[p, here]
        face_x = rcp(v + q[p + 1, here])
        face_y = rcp(v + q[p, 9:49])
        wx[p, here] = face_x
        wy[p, here] = face_y
        wz[p, here] = rcp(v + pltpu.roll(v, 127, 1))
        sums[p, here] = rcp(v + q[p - 1, here]) + face_x + face_y + rcp(v + q[p, 7:47])

    loop(1, N2 - 1, body, 4)


def down_kernel(
    pos, eb, ek, wx, wy, wz, sums, low, high, zlo, zhi,
    bk3, low3, high3, inv, xs, tb, twx, twy, twz, tinv, tx,
    f, r1, s, tq, tf, ts, face_w, face_f, face_s, tmp,
):
    gx, gy, gz = pos[0], pos[1], pos[2]
    lane = lanes_of(R2)
    row = rows_of(R2) - 4
    here, above, below = slice(8, 48), slice(9, 49), slice(7, 47)
    inside_y = ((row >= 0) | (gy > 0)) & ((row < 32) | (gy < DEV[1] - 1))
    cell = lane & 7

    def inside_x(p):
        return ((p >= 4) | (gx > 0)) & ((p < 36) | (gx < DEV[0] - 1))

    for t, (first, second) in enumerate(((zlo, low), (high, zhi))):
        for c in range(3):
            one, two = first[c], second[c]
            tb[t, c, here] = jnp.where(cell < 4, one, pltpu.roll(two, 4, 1))
            k = jnp.where(cell < 4, pltpu.roll(one, 124, 1), two)
            if c == 2:
                k = jnp.where(lane < 64, k, 1.0)
            tq[t, c, here] = 0.5 * rcp(k)
    through = []
    for t in range(2):
        v = [tq[t, c, here] for c in range(3)]
        face_x = [rcp(a + b) for a, b in zip(v, next_plane(v))]
        below_x = last_plane(face_x)
        inside_z = ((cell >= 4) | (gz > 0)) if t == 0 else ((cell < 4) | (gz < DEV[2] - 1))
        for c in range(3):
            face_y = rcp(v[c] + tq[t, c, above])
            below_y = rcp(v[c] + tq[t, c, below])
            ahead = pltpu.roll(v[c], 127, 1)
            if t == 0:
                face_z = rcp(jnp.where((cell == 3) & (gz == 0), ahead, v[c]) + ahead)
            else:
                face_z = rcp(v[c] + jnp.where((cell == 3) & (gz == DEV[2] - 1), v[c], ahead))
            through.append(face_z)
            twx[t, c, here] = face_x[c]
            twy[t, c, here] = face_y
            twz[t, c, here] = face_z
            total = below_x[c] + face_x[c] + face_y + below_y + face_z + pltpu.roll(face_z, 1, 1)
            inside = inside_y & inside_z & inside_x(16 * c + (lane >> 3))
            value = jnp.where(inside, rcp(total), 0.0)
            tinv[t, c, here] = value
            tf[t, c, here] = value * tb[t, c, here] * inv_center
    for c in range(3):
        face_w[c, here] = merge_faces(through[c], through[3 + c])
    flux = flux_strips(tf, twx, twy, twz, face_f)
    for t in range(2):
        for c in range(3):
            rest = tb[t, c, here] - flux[t][c]
            step = keep_coef * tf[t, c, here] + push_coef * tinv[t, c, here] * rest
            ts[t, c, here] = step
            tx[t, c, here] = tf[t, c, here] + step
    through = [
        twz[t, c, here] * (ts[t, c, here] - pltpu.roll(ts[t, c, here], 127, 1))
        for t in range(2)
        for c in range(3)
    ]
    for c in range(3):
        face_s[c, here] = merge_faces(through[c], through[3 + c])

    mask = jnp.where(inside_y, 1.0, 0.0)

    def weigh(p):
        through = face_lanes(face_w, p, here)
        face_z = jnp.where(lane == 127, through, wz[p, here])
        below_z = jnp.where(lane == 0, through, pltpu.roll(face_z, 1, 1))
        scale = jnp.where(inside_x(p), 1.0, 0.0)
        value = jnp.where(mask * scale > 0.5, rcp(sums[p, here] + face_z + below_z), 0.0)
        inv[p, here] = value
        f[p, here] = value * eb[p, here] * inv_center

    loop(1, N2 - 1, weigh, 4)

    def smooth(p):
        rest = eb[p, here] - flux_two(f, wx, wy, wz, face_f, p, 8, R2)
        step = keep_coef * f[p, here] + push_coef * inv[p, here] * rest
        r1[p, here] = rest
        s[p, here] = step
        xs[p, here] = f[p, here] + step

    loop(2, N2 - 2, smooth, 6)

    to_b = square(lambda i, j: (i >> 1) == j, 0.125)
    to_k = square(lambda i, j: (i >> 1) + 64 == j, 0.125)

    def coarsen(i):
        p = 2 * i + 4
        total = r1[p, 12:44] + r1[p + 1, 12:44]
        total = total - flux_two(s, wx, wy, wz, face_s, p, 12, 32)
        tmp[0, i, 0:32] = total - flux_two(s, wx, wy, wz, face_s, p + 1, 12, 32)
        tmp[1, i, 0:32] = ek[p, 12:44] + ek[p + 1, 12:44]

    loop(0, 16, coarsen, 4)
    pairs = [row_pairs(tmp.at[j], range(16), 0, 16) for j in range(2)]
    both = select_dot(pairs[0], to_b) + select_dot(pairs[1], to_k)
    for i in range(16):
        part = both[16 * i : 16 * i + 16]
        bk3[i] = part
        if i < 13:
            low3[i] = part
        if i >= 3:
            high3[i - 3] = part


def planes_kernel(pos, bk, xlo, xhi, out, low, high):
    gx = pos[0]
    right = lanes_of(16) >= 64

    def put(p, value):
        out[p] = value
        low[p] = value[0:8]
        high[p] = value[8:16]
        if 9 <= p < 33:
            low[p + 33] = value[8:16]
            high[p + 33] = value[0:8]

    for j in range(13):
        lo, hi = xlo[j], xhi[j]
        if j == 12:
            lo = jnp.where(right & (gx == 0), bk[0], lo)
        if j == 0:
            hi = jnp.where(right & (gx == DEV[0] - 1), bk[15], hi)
        put(j, lo)
        put(29 + j, hi)
    for j in range(16):
        put(13 + j, bk[j])


def three_rows(pos, own, ylo, yhi, p):
    gy = pos[1]
    right = lanes_of(16) >= 64
    row = rows_of(16)
    far = jnp.where((p >= 9) & (p < 33), p + 33, p)
    lo = jnp.concatenate([ylo[far], ylo[p]], axis=0)
    hi = jnp.concatenate([yhi[p], yhi[far]], axis=0)
    lo = jnp.where(right & (row == 15) & (gy == 0), own[p, 0:1], lo)
    hi = jnp.where(right & (row == 0) & (gy == DEV[1] - 1), own[p, 15:16], hi)
    return lo, own[p], hi


def slots_kernel(pos, own, ylo, yhi, low, high):
    quarter = (lanes_of(16) & 63) >> 4

    def column(col):
        total_lo = [None] * 3
        total_hi = [None] * 3
        for slot in range(4):
            p = jnp.minimum(col * 4 + slot, N3 - 1)
            mine = quarter == slot
            for g, e in enumerate(three_rows(pos, own, ylo, yhi, p)):
                lo, hi = rolled(e, 16 * slot), rolled(e, 16 * slot - 48)
                total_lo[g] = lo if slot == 0 else jnp.where(mine, lo, total_lo[g])
                total_hi[g] = hi if slot == 0 else jnp.where(mine, hi, total_hi[g])
        for g in range(3):
            low[col, 16 * g : 16 * g + 16] = total_lo[g]
            high[col, 16 * g : 16 * g + 16] = total_hi[g]

    loop(0, 11, column, 4)


def flux_one(v_ref, wx, wy, wz, p, rows):
    here, above, below = slice(8, 8 + rows), slice(9, 9 + rows), slice(7, 7 + rows)
    v = v_ref[p, here]
    fx = wx[p, here] * (v - v_ref[p + 1, here])
    gx = wx[p - 1, here] * (v_ref[p - 1, here] - v)
    fy = wy[p, here] * (v - v_ref[p, above])
    gy = wy[p, below] * (v_ref[p, below] - v)
    fz = wz[p, here] * (v - pltpu.roll(v, 127, 1))
    return (fx - gx) + (fy - gy) + (fz - pltpu.roll(fz, 1, 1))


UNROLL = {48: 4, 24: 6, 32: 8, 16: 8, 8: 4}


def weigh_one(q, b, wx, wy, wz, inv, f, rows, low, high, first, last, inside):
    here = slice(8, 8 + rows)
    wx[low - 1, here] = rcp(q[low - 1, here] + q[low, here])

    def body(p):
        v = q[p, here]
        up = pltpu.roll(v, 127, 1)
        face_x = rcp(v + q[p + 1, here])
        face_y = rcp(v + q[p, 9 : 9 + rows])
        below_x = rcp(v + q[p - 1, here])
        below_y = rcp(v + q[p, 7 : 7 + rows])
        face_z = rcp(jnp.where(first, up, v) + jnp.where(last, v, up))
        lower_z = pltpu.roll(face_z, 1, 1)
        wx[p, here] = face_x
        wy[p, here] = face_y
        wz[p, here] = face_z
        total = below_x + face_x + face_y + below_y + face_z + lower_z
        value = jnp.where(inside(p), rcp(total), 0.0)
        inv[p, here] = value
        f[p, here] = value * b[p, here] * inv_center

    loop(low, high, body, UNROLL[rows])


def smooth_one(b, wx, wy, wz, inv, f, r1, s, xs, rows, low, high):
    here = slice(8, 8 + rows)

    def body(p):
        rest = b[p, here] - flux_one(f, wx, wy, wz, p, rows)
        step = keep_coef * f[p, here] + push_coef * inv[p, here] * rest
        r1[p, here] = rest
        s[p, here] = step
        xs[p, here] = f[p, here] + step

    loop(low, high, body, UNROLL[rows])


def finish_one(b, wx, wy, wz, inv, xs, f, r0, out, shift, rows, ranges):
    here = slice(8, 8 + rows)

    def start(p):
        rest = b[p, here] - flux_one(xs, wx, wy, wz, p, rows)
        r0[p, here] = rest
        f[p, here] = inv[p, here] * rest * inv_center

    loop(*ranges[0], start, UNROLL[rows])

    def end(p):
        rest = r0[p, here] - flux_one(f, wx, wy, wz, p, rows)
        step = keep_coef * f[p, here] + push_coef * inv[p, here] * rest
        out[p + shift, here] = xs[p, here] + f[p, here] + step

    loop(*ranges[1], end, UNROLL[rows])


def signed(lane, limit):
    return jnp.where(lane < limit, lane, lane - 128)


def middle_kernel(
    pos, own, ylo, yhi, zlo, zhi,
    payload, b3, wx3, wy3, wz3, inv3, x3, b4, wx4, wy4, wz4, inv4, x4,
    k3, q3, f3, r3, s3, k4, q4, f4, r4, s4, tmp,
):
    gx, gy, gz = pos[0], pos[1], pos[2]
    lane = lanes_of(16)

    def unpack(p, lo, hi, slot):
        for g, e in enumerate(three_rows(pos, own, ylo, yhi, p)):
            rows = slice(8 + 16 * g, 24 + 16 * g)
            part = slice(16 * g, 16 * g + 16)
            up, dn = rolled(hi[part], 64 - 16 * slot), rolled(lo[part], 112 - 16 * slot)
            bv = jnp.where((lane >= 64) & (lane < 80), up, e)
            b3[p, rows] = jnp.where(lane >= 112, dn, bv)
            kv = jnp.where(lane < 16, up, jnp.where((lane >= 48) & (lane < 64), dn, e))
            kv = pltpu.roll(kv, 64, 1)
            kv = jnp.where((lane >= 80) & (lane < 112), 1.0, kv)
            k3[p, rows] = kv
            q3[p, rows] = 2.0 * rcp(kv)

    def column(col, slots):
        lo, hi = zlo[col], zhi[col]
        for slot in range(slots):
            unpack(col * 4 + slot, lo, hi, slot)

    loop(0, 10, lambda col: column(col, 4), 2)
    column(10, 2)

    def region(rows, y_first, x_first, nx, ny, nz):
        y = rows_of(rows) + y_first
        z = signed(lanes_of(rows), 96)
        inside_y = ((y >= 0) | (gy > 0)) & ((y < ny) | (gy < DEV[1] - 1))
        inside_z = ((z >= 0) | (gz > 0)) & ((z < nz) | (gz < DEV[2] - 1))
        inside_yz = jnp.where(inside_y & inside_z, 1.0, 0.0)

        def inside(p):
            x = p + x_first
            inside_x = ((x >= 0) | (gx > 0)) & ((x < nx) | (gx < DEV[0] - 1))
            return inside_yz * jnp.where(inside_x, 1.0, 0.0) > 0.5

        return inside

    def edges(rows, cells):
        lane = lanes_of(rows)
        return (lane == 127) & (gz == 0), (lane == cells - 1) & (gz == DEV[2] - 1)

    inside = region(R3, -16, -13, 16, 16, 64)
    weigh_one(q3, b3, wx3, wy3, wz3, inv3, f3, R3, 1, N3 - 1, *edges(R3, 64), inside)
    smooth_one(b3, wx3, wy3, wz3, inv3, f3, r3, s3, x3, R3, 2, N3 - 2)

    def pick(i, j):
        target = signed(j, 64)
        return ((signed(i, 96) >> 1) == target) & (target >= -6) & (target < 38)

    narrow = square(pick, 0.125)
    valid = (lanes_of(R4) < 38) | (lanes_of(R4) >= 122)
    row = rows_of(R4)

    def coarse_k(i):
        p = 2 * i + 1
        tmp[0, i, 8:56] = k3[p, 8:56] + k3[p + 1, 8:56]

    def coarse_b(i):
        p = 2 * i + 1
        total = r3[p, 8:56] + r3[p + 1, 8:56] - flux_one(s3, wx3, wy3, wz3, p, R3)
        tmp[1, i, 8:56] = total - flux_one(s3, wx3, wy3, wz3, p + 1, R3)

    loop(0, N4, coarse_k, 5)
    loop(1, N4 - 1, coarse_b, 3)
    value = select_dot(row_pairs(tmp.at[0], range(N4), 12, R4), narrow)
    for i in range(N4):
        part = jnp.where(valid, value[R4 * i : R4 * i + R4], 1.0)
        part = jnp.where((row == 5) & (gy == 0), pltpu.roll(part, R4 - 1, 0), part)
        part = jnp.where((row == 14) & (gy == DEV[1] - 1), pltpu.roll(part, 1, 0), part)
        k4[i, 8:32] = part
    value = select_dot(row_pairs(tmp.at[1], range(1, N4 - 1), 12, R4), narrow)
    for i in range(1, N4 - 1):
        b4[i, 8:32] = value[R4 * (i - 1) : R4 * i]
    k4[5, 8:32] = jnp.where(gx == 0, k4[6, 8:32], k4[5, 8:32])
    k4[14, 8:32] = jnp.where(gx == DEV[0] - 1, k4[13, 8:32], k4[14, 8:32])

    def invert(i):
        q4[i, 8:32] = 8.0 * rcp(k4[i, 8:32])

    loop(0, N4, invert, 5)
    inside = region(R4, -6, -6, 8, 8, 32)
    weigh_one(q4, b4, wx4, wy4, wz4, inv4, f4, R4, 1, N4 - 1, *edges(R4, 32), inside)
    smooth_one(b4, wx4, wy4, wz4, inv4, f4, r4, s4, x4, R4, 2, N4 - 2)

    spread = square(lambda i, j: (i < 32) & ((i >> 1) == (j & 15)), 0.125)
    slot = lanes_of(4) >> 4
    quad = rows_of(4)
    parts = [[None, None], [None, None]]
    for i in range(4):
        p = 2 * i + 6
        total = r4[p, 8:32] + r4[p + 1, 8:32] - flux_one(s4, wx4, wy4, wz4, p, R4)
        tmp[0, i, 8:32] = total - flux_one(s4, wx4, wy4, wz4, p + 1, R4)
        tmp[1, i, 8:32] = k4[p, 8:32] + k4[p + 1, 8:32]
    for i in range(4):
        mine = slot == (i % 2) * 4 + quad
        for a in range(2):
            value = row_pairs(tmp.at[a], [i], 14, 4)
            value = jnp.where(mine, select_dot(value, spread), 0.0)
            value = jnp.sum(value, axis=0, keepdims=True)
            old = parts[a][i // 2]
            parts[a][i // 2] = value if old is None else old + value
    value = jnp.concatenate(parts[0] + parts[1], axis=0)
    for d in range(32):
        payload[d] = value


def exchange_blocks(value):
    row = rows_of(8)
    group = lanes_of(8) >> 4
    for bit in (1, 2):
        upper = pltpu.roll(pltpu.roll(value, 8 - bit, 0), 16 * bit, 1)
        lower = pltpu.roll(pltpu.roll(value, bit, 0), 128 - 16 * bit, 1)
        moved = jnp.where((row & bit) == 0, upper, lower)
        value = jnp.where((row & bit) == (group & bit), value, moved)
    moved = pltpu.roll(pltpu.roll(value, 4, 0), 64, 1)
    return jnp.where((row & 4) == (group & 4), value, moved)


WHOLE = ((16, 32, 128), (8, 16, 64), (4, 8, 32))


def up_kernel(
    pos, own, up1, up2, down2, down1, b3, wx3, wy3, wz3, inv3, x3, b4, wx4, wy4, wz4, inv4, x4,
    eb, wx, wy, wz, inv, xs, tb, twx, twy, twz, tinv, tx,
    out, *scratch,
):
    gx, gy, gz = pos[0], pos[1], pos[2]
    levels = [scratch[12 * i : 12 * i + 12] for i in range(3)]
    e5, e6, raw, f4, r4, e4, y4, f3, r3, e3, y3, f2, r2, y2, tf, ty, face_x, face_f, tmp = scratch[36:]

    for level, (nx, ny, nz) in enumerate(WHOLE):
        b, k, q, wx_, wy_, wz_, inv_, f, r, s, x, r0 = levels[level]
        for ref in (f, s, x):
            ref[0] = jnp.zeros(ref.shape[1:], F32)
            ref[nx + 1] = jnp.zeros(ref.shape[1:], F32)

            def clear(p, ref=ref, ny=ny):
                ref[p, 0:8] = jnp.zeros((8, 128), F32)
                ref[p, 8 + ny : 16 + ny] = jnp.zeros((8, 128), F32)

            loop(1, nx + 1, clear)
    for p in (0, 1, 2, 19, 20, 21):
        e5[p] = jnp.zeros(e5.shape[1:], F32)

    def clear(p):
        e5[p, 0:8] = jnp.zeros((8, 128), F32)
        e5[p, 40:48] = jnp.zeros((8, 128), F32)

    loop(3, 19, clear)

    b5, k5 = levels[0][0], levels[0][1]

    unused = jnp.ones((128, 128), F32)
    parts = (own[...], up1[...], up2[...], unused, unused, unused, down2[...], down1[...])
    for n, part in enumerate(parts):
        raw[pl.ds(n, 128, stride=8)] = part

    def unpack(d):
        dx, dy = d // 8, d % 8
        rows = pl.ds(8 + 4 * dy, 4)
        for kind in range(4):
            value = exchange_blocks(raw[pl.ds(pl.multiple_of(d * 32 + kind * 8, 8), 8)])
            target = (b5, k5)[kind // 2]
            p = 1 + 4 * dx + 2 * (kind % 2)
            target[p, rows] = value[0:4]
            target[p + 1, rows] = value[4:8]

    loop(0, 32, unpack, 4)

    def ends(level):
        nx, ny, nz = WHOLE[level]
        k, q = levels[level][1], levels[level][2]
        factor = 0.5 * 4.0 ** (level + 3)

        def invert(p):
            value = factor * rcp(k[p, 8 : 8 + ny])
            q[p, 8 : 8 + ny] = value
            q[p, 7:8] = value[0:1]
            q[p, 8 + ny : 9 + ny] = value[ny - 1 : ny]

        loop(1, nx + 1, invert, 4)
        q[0] = q[1]
        q[nx + 1] = q[nx]

    def down(level):
        nx, ny, nz = WHOLE[level]
        b, k, q, wx_, wy_, wz_, inv_, f, r, s, x, r0 = levels[level]
        ends(level)

        def below(p):
            wy_[p, 7:8] = rcp(q[p, 7:8] + q[p, 8:9])

        loop(1, nx + 1, below, 4)
        z = signed(lanes_of(ny), 72) + gz * (nz // DEV[2])
        weigh_one(
            q, b, wx_, wy_, wz_, inv_, f, ny, 1, nx + 1, z == -1, z == nz - 1,
            lambda p: (z >= 0) & (z < nz),
        )
        smooth_one(b, wx_, wy_, wz_, inv_, f, r, s, x, ny, 1, nx + 1)
        if level == 2:
            return
        nb, nk = levels[level + 1][0], levels[level + 1][1]
        low, high = ((-9, 17), (-4, 8))[level]

        def kept(lane):
            return (signed(lane, 64) >= low) & (signed(lane, 64) < high)

        narrow = square(lambda i, j: ((signed(i, 72) >> 1) == signed(j, 64)) & kept(j), 0.125)
        valid = kept(lanes_of(ny // 2))

        def coarsen(i):
            p = 2 * i - 1
            here = slice(8, 8 + ny)
            total = r[p, here] + r[p + 1, here] - flux_one(s, wx_, wy_, wz_, p, ny)
            tmp[0, i, here] = total - flux_one(s, wx_, wy_, wz_, p + 1, ny)
            tmp[1, i, here] = k[p, here] + k[p + 1, here]

        count = ny // 2
        planes = range(1, nx // 2 + 1)
        loop(1, nx // 2 + 1, coarsen, 64 // ny)
        for a, target in enumerate((nb, nk)):
            value = select_dot(row_pairs(tmp.at[a], planes, 8, count), narrow)
            for n, i in enumerate(planes):
                part = value[count * n : count * n + count]
                target[i, 8 : 8 + count] = jnp.where(valid, part, 1.0) if a == 1 else part

    for level in range(3):
        down(level)

    def up(level, coarse, target, shift):
        nx, ny, nz = WHOLE[level]
        b, k, q, wx_, wy_, wz_, inv_, f, r, s, x, r0 = levels[level]
        widen = square(lambda i, j: signed(i, 64) == (signed(j, 64) >> 1), 1.0)
        count = ny // 2

        planes = range(1, nx // 2 + 1)
        value = jnp.concatenate([coarse[i, 8 : 8 + count] for i in planes], axis=0)
        spread_rows(tmp.at[0], planes, 8, count, select_dot(value, widen))

        def add(i):
            wide = tmp[0, i, 8 : 8 + ny]
            x[2 * i - 1, 8 : 8 + ny] += wide
            x[2 * i, 8 : 8 + ny] += wide

        loop(1, nx // 2 + 1, add, 64 // ny)
        span = (1, nx + 1)
        finish_one(b, wx_, wy_, wz_, inv_, x, f, r0, target, shift, ny, (span, span))

    up(1, levels[2][10], e6, 0)
    up(0, e6, e5, 2)

    widen = square(lambda i, j: signed(i, 64) == (signed(j, 64) >> 1), 1.0)

    planes = range(1, 9)
    value = [e5[gx * 4 + i, pl.ds(pl.multiple_of(4 * gy, 4), 24)] for i in planes]
    value = select_dot(jnp.concatenate(value, axis=0), widen)
    for n, i in enumerate(planes):
        spread_rows(tmp.at[0], [i], 8, 12, value[24 * n + 5 : 24 * n + 17])

    def add_four(i):
        wide = tmp[0, i, 8:32]
        y4[2 * i, 8:32] = x4[2 * i, 8:32] + wide
        y4[2 * i + 1, 8:32] = x4[2 * i + 1, 8:32] + wide

    loop(1, 9, add_four, 4)
    finish_one(b4, wx4, wy4, wz4, inv4, y4, f4, r4, e4, 0, R4, ((3, 17), (4, 16)))

    widen3 = square(lambda i, j: signed(i, 64) == (signed(j, 96) >> 1), 1.0)

    planes = range(4, 16)
    value = jnp.concatenate([e4[i, 8:32] for i in planes], axis=0)
    spread_rows(tmp.at[0], planes, 12, 24, select_dot(value, widen3))

    def add_three(i):
        wide = tmp[0, i, 8:56]
        y3[2 * i + 1, 8:56] = x3[2 * i + 1, 8:56] + wide
        y3[2 * i + 2, 8:56] = x3[2 * i + 2, 8:56] + wide

    loop(4, 16, add_three, 3)
    finish_one(b3, wx3, wy3, wz3, inv3, y3, f3, r3, e3, 0, R3, ((11, 31), (12, 30)))

    wide = square(lambda i, j: i == (j >> 1), 1.0)
    planes = range(1, 19)
    value = jnp.concatenate([e3[i + 11, 22:46] for i in planes], axis=0)
    spread_rows(tmp.at[0], planes, 8, 24, select_dot(value, wide))
    here = slice(8, 48)
    group = lanes_of(24) >> 4
    for t in range(2):
        wide = square(lambda i, j: signed(i, 96) == ((j & 7) + 128 * t - 4) >> 1, 1.0)
        parts = select_dot(value, wide)
        for c in range(3):
            total = jnp.zeros((24, 128), F32)
            for n, i in enumerate(planes):
                if i // 8 == c:
                    total = jnp.where(group == i % 8, parts[24 * n : 24 * n + 24], total)
            spread_rows(tmp.at[1], [3 * t + c], 8, 24, total)
            ty[t, c, here] = tx[t, c, here] + tmp[1, 3 * t + c, here]
    flux = flux_strips(ty, twx, twy, twz, face_x)
    for t in range(2):
        for c in range(3):
            tf[t, c, here] = tinv[t, c, here] * (tb[t, c, here] - flux[t][c]) * inv_center
    through = [
        twz[t, c, here] * (tf[t, c, here] - pltpu.roll(tf[t, c, here], 127, 1))
        for t in range(2)
        for c in range(3)
    ]
    for c in range(3):
        face_f[c, here] = merge_faces(through[c], through[3 + c])

    def add_two(i):
        part = tmp[0, i, here]
        y2[2 * i, here] = xs[2 * i, here] + part
        y2[2 * i + 1, here] = xs[2 * i + 1, here] + part

    loop(1, 19, add_two, 3)

    def start(p):
        rest = eb[p, here] - flux_two(y2, wx, wy, wz, face_x, p, 8, R2)
        r2[p, here] = rest
        f2[p, here] = inv[p, here] * rest * inv_center

    loop(3, 37, start, 5)
    core = slice(12, 44)

    def end(i):
        p = i + 4
        rest = r2[p, core] - flux_two(f2, wx, wy, wz, face_f, p, 12, 32)
        first = f2[p, core]
        step = keep_coef * first + push_coef * inv[p, core] * rest
        out[i] = y2[p, core] + first + step

    loop(0, 32, end, 8)


def vmem(array):
    return pltpu.with_memory_space_constraint(array, pltpu.VMEM)


def call(kernel, args, outs, scratch=(), final=False):
    size = sum(4 * math.prod(shape) for shape in scratch) + sum(4 * math.prod(shape) for shape in outs)
    out_type = jax.ShapeDtypeStruct if final else pltpu.VMEM
    held = args[1:]
    return pl.pallas_call(
        kernel,
        out_shape=[out_type(shape, F32) for shape in outs],
        in_specs=[pl.BlockSpec(memory_space=pltpu.SMEM)]
        + [pl.BlockSpec(memory_space=pltpu.VMEM)] * len(held),
        out_specs=[pl.BlockSpec(memory_space=pltpu.VMEM)] * len(outs),
        scratch_shapes=[pltpu.VMEM(shape, F32) for shape in scratch],
        compiler_params=pltpu.CompilerParams(vmem_limit_bytes=size + (4 << 20)),
    )(args[0], *held)


def load(kernel, b, k, shape, count):
    return pl.pallas_call(
        kernel,
        out_shape=[pltpu.VMEM(shape, F32)] * 2,
        in_specs=[pl.BlockSpec(memory_space=pl.ANY)] * 2,
        out_specs=[pl.BlockSpec(memory_space=pltpu.VMEM)] * 2,
        scratch_shapes=[pltpu.SemaphoreType.DMA((count,))],
    )(b, k)


def swap(low, high, axis):
    count = lax.axis_size(axis)
    ring = range(count)
    before = lax.ppermute(high, axis, [(i, (i + 1) % count) for i in ring])
    after = lax.ppermute(low, axis, [(i, (i - 1) % count) for i in ring])
    return vmem(before), vmem(after)


def shards(b, k):
    pos = jnp.stack([lax.axis_index(axis) for axis in AXES]).astype(jnp.int32)
    low, high = load(edge_kernel, b, k, (7, 32, 128), 4)
    xlo, xhi = swap(low, high, "gx")
    b, k = load(load_kernel, b, k, (32, 32, 128), 8)
    low, high = call(rows_kernel, (pos, b, k, xlo, xhi), [(N2, 8, 128)] * 2)
    ylo, yhi = swap(low, high, "gy")
    ext2, strip, face = (N2, T2, 128), (2, 3, T2, 128), (3, T2, 128)
    low, high, eb, ek = call(
        lanes_kernel, (pos, b, k, xlo, xhi, ylo, yhi), [(3, R2, 128)] * 2 + [ext2] * 2
    )
    zlo, zhi = swap(low, high, "gz")
    wx, wy, wz, sums = call(weights_kernel, (pos, ek), [ext2] * 4, [ext2])
    bk3, low, high, *rest = call(
        down_kernel,
        (pos, eb, ek, wx, wy, wz, sums, low, high, zlo, zhi),
        [(16, 16, 128)] + [(13, 16, 128)] * 2 + [ext2] * 2 + [strip] * 6,
        [ext2] * 3 + [strip] * 3 + [face] * 3 + [(2, 16, 32, 128)],
    )
    state2 = [eb, wx, wy, wz, *rest]
    xlo, xhi = swap(low, high, "gx")
    own, low, high = call(
        planes_kernel, (pos, bk3, xlo, xhi), [(N3, 16, 128)] + [(N3 + 24, 8, 128)] * 2
    )
    ylo, yhi = swap(low, high, "gy")
    low, high = call(slots_kernel, (pos, own, ylo, yhi), [(11, 48, 128)] * 2)
    zlo, zhi = swap(low, high, "gz")
    three, four = (N3, T3, 128), (N4, T4, 128)
    payload, *state = call(
        middle_kernel,
        (pos, own, ylo, yhi, zlo, zhi),
        [(32, 4, 128)] + [three] * 6 + [four] * 6,
        [three] * 5 + [four] * 5 + [(2, N4, T3, 128)],
    )
    recv = lax.all_to_all(payload, AXES[:2], 0, 0, tiled=True).reshape(128, 128)
    ring = range(DEV[2])
    recv = [recv] + [
        lax.ppermute(recv, "gz", [(i, (i - d) % DEV[2]) for i in ring]) for d in (1, 2, -2, -1)
    ]
    recv = [vmem(part) for part in recv]
    scratch = []
    for nx, ny, _ in WHOLE:
        scratch += [(nx + 2, ny + 16, 128)] * 12
    scratch += [(22, 56, 128), (10, 32, 128), (1024, 128)]
    scratch += [four] * 4 + [three] * 4 + [ext2] * 3 + [strip] * 2 + [face] * 2
    scratch += [(2, 20, T3, 128)]
    (out,) = call(up_kernel, (pos, *recv, *state, *state2), [(32, 32, 128)], scratch, True)
    return out


def solution(mesh):
    spec = P(*AXES)
    return jax.shard_map(shards, mesh=mesh, in_specs=(spec, spec), out_specs=spec, check_vma=False)
```

time: 231 us -> 104 us (0.45)
  Pallas kernels: 140 us -> 37.8 us
  blocking collectives: 29.7 us -> 17.2 us
  waiting for transfers between devices: 28.6 us -> 18.4 us
  local copies, waits for them, and re-layouts: 6.86 us -> 0 us
  starting transfers between devices: 23.8 us -> 30 us
    pallas_call x7 -> x10, Pallas kernels: 140 us -> 37.8 us  [the longest x8 35.5 us: call(): pl.pallas_call(kernel, out_shape=[out_type(shape, F32) for shape in outs]...]
    all_to_all x1, blocking collectives: 29.7 us -> 17.2 us  [shards(): recv = lax.all_to_all(payload, AXES[:2], 0, 0, tiled=True).reshape(128, 128)]
    ppermute x6, waiting for transfers between devices: 13 us -> 2.81 us  [swap(): after = lax.ppermute(low, axis, [(i, (i - 1) % count) for i in ring])]
    unnamed x24 -> x0, local copies, waits for them, and re-layouts: 5.15 us -> none
    ppermute x0 -> x4, starting transfers between devices: none -> 4.94 us  [shards(): lax.ppermute(recv, 'gz', [(i, (i - d) % DEV[2]) for i in ring])]
    ppermute x0 -> x4, waiting for transfers between devices: none -> 3.19 us  [shards(): lax.ppermute(recv, 'gz', [(i, (i - d) % DEV[2]) for i in ring])]
    ppermute x6, waiting for transfers between devices: 15.6 us -> 12.4 us  [swap(): before = lax.ppermute(high, axis, [(i, (i + 1) % count) for i in ring])]
    ppermute x6, starting transfers between devices: 9.7 us -> 12.7 us  [swap(): after = lax.ppermute(low, axis, [(i, (i - 1) % count) for i in ring])]
  transfers between devices with their start and end apart: 12 -> 16, of which waited for: 11 -> 10; matrix products, arithmetic and copies ran while one was open for 0% -> 0% of each run, Pallas kernels for 0% -> 3%
where the time goes in v2:
time: 104 us
  Pallas kernels  37.8 us (36%)
  starting transfers between devices  30 us (29%)
  waiting for transfers between devices  18.4 us (18%)
  blocking collectives  17.2 us (17%)
    pallas_call x8, Pallas kernels, call(): pl.pallas_call(kernel, out_shape=[out_type(shape, F32) for shape in outs]...  35.5 us
    all_to_all x1, blocking collectives, shards(): recv = lax.all_to_all(payload, AXES[:2], 0, 0, tiled=True).reshape(128, 128)  17.2 us
    ppermute x6, starting transfers between devices, swap(): after = lax.ppermute(low, axis, [(i, (i - 1) % count) for i in ring])  12.7 us
    ppermute x6, waiting for transfers between devices, swap(): before = lax.ppermute(high, axis, [(i, (i + 1) % count) for i in ring])  12.4 us
    ppermute x6, starting transfers between devices, swap(): before = lax.ppermute(high, axis, [(i, (i + 1) % count) for i in ring])  12.4 us
    ppermute x4, starting transfers between devices, shards(): lax.ppermute(recv, 'gz', [(i, (i - d) % DEV[2]) for i in ring])  4.94 us
    ppermute x4, waiting for transfers between devices, shards(): lax.ppermute(recv, 'gz', [(i, (i - d) % DEV[2]) for i in ring])  3.19 us
    ppermute x6, waiting for transfers between devices, swap(): after = lax.ppermute(low, axis, [(i, (i - 1) % count) for i in ring])  2.81 us
  transfers between devices with their start and end apart: 16, of which 10 were waited for; matrix products, arithmetic and copies ran while one was open for 0% of the time, Pallas kernels for 3%

profile of v2, /device:TPU:1, one launch (start us, length us, event | category | flops | bytes accessed | tf_op | source)
XLA Modules:
  0.0 103.6 jit_solution(13192039363502579466)
XLA Ops:
  0.0 1.0 shard_map.29
  1.0 2.1 %collective-permute-start = (f32[7,32,128]{2,1,0:T(8,128)S(1)}, f32[7,32,128]{2,1,0:T(8,128)S(1)}, u32[]{:S(2)}, u32[]{:S(2)}) collective-permute-start(f32[7,32,128]{2,1,0:T(8,128)S(1)} %get-tuple-element.50), channel_id=1, source_target_pairs={{0,64},{64,128},{128,192},{192,0},{1,65},{65,129},{129,193},{193,1... | collective-permute-start | bytes 344072 | tf_op jit(solution)/shard_map/ppermute | solution.py:862
  3.1 1.4 %collective-permute-start.1 = (f32[7,32,128]{2,1,0:T(8,128)S(1)}, f32[7,32,128]{2,1,0:T(8,128)S(1)}, u32[]{:S(2)}, u32[]{:S(2)}) collective-permute-start(f32[7,32,128]{2,1,0:T(8,128)S(1)} %get-tuple-element.51), channel_id=1, source_target_pairs={{0,192},{64,0},{128,64},{192,128},{1,193},{65,1},{129,65},{193,129... | collective-permute-start | bytes 344072 | tf_op jit(solution)/shard_map/ppermute | solution.py:863
  4.4 1.3 %shard_map.28 = (f32[32,32,128]{2,1,0:T(8,128)S(1)}, f32[32,32,128]{2,1,0:T(8,128)S(1)}) custom-call(f32[32,32,128]{2,1,0:T(8,128)} %b.3, f32[32,32,128]{2,1,0:T(8,128)} %k.3), custom_call_target="tpu_custom_call" | custom-call | tf_op jit(solution)/shard_map/pallas_call | solution.py:850
  5.8 0.1 pad_add_fusion.pos
  5.9 0.7 collective-permute-done.xlo
  6.5 0.2 collective-permute-done.1.xhi
  6.7 0.6 shard_map.30
  7.4 2.1 %collective-permute-start.2 = (f32[40,8,128]{2,1,0:T(8,128)S(1)}, f32[40,8,128]{2,1,0:T(8,128)S(1)}, u32[]{:S(2)}, u32[]{:S(2)}) collective-permute-start(f32[40,8,128]{2,1,0:T(8,128)S(1)} %get-tuple-element.52), channel_id=1, source_target_pairs={{0,8},{8,16},{16,24},{24,32},{32,40},{40,48},{48,56},{56,0},{1,9},... | collective-permute-start | bytes 491528 | tf_op jit(solution)/shard_map/ppermute | solution.py:862
  9.5 4.0 %collective-permute-start.3 = (f32[40,8,128]{2,1,0:T(8,128)S(1)}, f32[40,8,128]{2,1,0:T(8,128)S(1)}, u32[]{:S(2)}, u32[]{:S(2)}) collective-permute-start(f32[40,8,128]{2,1,0:T(8,128)S(1)} %get-tuple-element.53), channel_id=1, source_target_pairs={{0,56},{8,0},{16,8},{24,16},{32,24},{40,32},{48,40},{56,48},{1,57}... | collective-permute-start | bytes 491528 | tf_op jit(solution)/shard_map/ppermute | solution.py:863
  13.5 2.6 %collective-permute-done.2.ylo = f32[40,8,128]{2,1,0:T(8,128)S(1)} collective-permute-done((f32[40,8,128]{2,1,0:T(8,128)S(1)}, f32[40,8,128]{2,1,0:T(8,128)S(1)}, u32[]{:S(2)}, u32[]{:S(2)}) %collective-permute-start.2) | collective-permute-done | bytes 163872 | tf_op jit(solution)/shard_map/ppermute | solution.py:862
  16.1 0.0 collective-permute-done.3.yhi
  16.1 1.8 %shard_map.31 = (f32[3,40,128]{2,1,0:T(8,128)S(1)}, f32[3,40,128]{2,1,0:T(8,128)S(1)}, f32[40,56,128]{2,1,0:T(8,128)S(1)}, f32[40,56,128]{2,1,0:T(8,128)S(1)}) custom-call(s32[3]{0:T(128)S(1)} %pad_add_fusion.pos, f32[32,32,128]{2,1,0:T(8,128)S(1)} %get-tuple-element.48.b, f32[32,32,128]{2,1,0:T(8,128)S(1)} %get-tuple-element.49.k, ...), custom_call_target="tpu_custom_call" | custom-call | tf_op jit(solution)/shard_map/pallas_call | solution.py:838
  17.9 2.6 %collective-permute-start.5 = (f32[3,40,128]{2,1,0:T(8,128)S(1)}, f32[3,40,128]{2,1,0:T(8,128)S(1)}, u32[]{:S(2)}, u32[]{:S(2)}) collective-permute-start(f32[3,40,128]{2,1,0:T(8,128)S(1)} %get-tuple-element.60.low), channel_id=1, source_target_pairs={{0,7},{1,0},{2,1},{3,2},{4,3},{5,4},{6,5},{7,6},{8,15},{9,8},{10,9... | collective-permute-start | bytes 184328 | tf_op jit(solution)/shard_map/ppermute | solution.py:863
  20.5 1.2 %collective-permute-start.4 = (f32[3,40,128]{2,1,0:T(8,128)S(1)}, f32[3,40,128]{2,1,0:T(8,128)S(1)}, u32[]{:S(2)}, u32[]{:S(2)}) collective-permute-start(f32[3,40,128]{2,1,0:T(8,128)S(1)} %get-tuple-element.61.high), channel_id=1, source_target_pairs={{0,1},{1,2},{2,3},{3,4},{4,5},{5,6},{6,7},{7,0},{8,9},{9,10},{10,1... | collective-permute-start | bytes 184328 | tf_op jit(solution)/shard_map/ppermute | solution.py:862
  21.7 1.7 %shard_map.32 = (f32[40,56,128]{2,1,0:T(8,128)S(1)}, f32[40,56,128]{2,1,0:T(8,128)S(1)}, f32[40,56,128]{2,1,0:T(8,128)S(1)}, f32[40,56,128]{2,1,0:T(8,128)S(1)}) custom-call(s32[3]{0:T(128)S(1)} %pad_add_fusion.pos, f32[40,56,128]{2,1,0:T(8,128)S(1)} %get-tuple-element.55.ek), custom_call_target="tpu_custom_call" | custom-call | tf_op jit(solution)/shard_map/pallas_call | solution.py:838
  23.5 0.1 collective-permute-done.5.zhi
  23.6 0.0 collective-permute-done.4.zlo
  23.6 5.8 %shard_map.33 = (f32[16,16,128]{2,1,0:T(8,128)S(1)}, f32[13,16,128]{2,1,0:T(8,128)S(1)}, f32[13,16,128]{2,1,0:T(8,128)S(1)}, f32[40,56,128]{2,1,0:T(8,128)S(1)},...) custom-call(s32[3]{0:T(128)S(1)} %pad_add_fusion.pos, ...), custom_call_target="tpu_custom_call" | custom-call | tf_op jit(solution)/shard_map/pallas_call | solution.py:838
  29.4 1.3 %collective-permute-start.6 = (f32[13,16,128]{2,1,0:T(8,128)S(1)}, f32[13,16,128]{2,1,0:T(8,128)S(1)}, u32[]{:S(2)}, u32[]{:S(2)}) collective-permute-start(f32[13,16,128]{2,1,0:T(8,128)S(1)} %get-tuple-element.63), channel_id=1, source_target_pairs={{0,64},{64,128},{128,192},{192,0},{1,65},{65,129},{129,193},{193,1... | collective-permute-start | bytes 319496 | tf_op jit(solution)/shard_map/ppermute | solution.py:862
  30.7 1.6 %collective-permute-start.7 = (f32[13,16,128]{2,1,0:T(8,128)S(1)}, f32[13,16,128]{2,1,0:T(8,128)S(1)}, u32[]{:S(2)}, u32[]{:S(2)}) collective-permute-start(f32[13,16,128]{2,1,0:T(8,128)S(1)} %get-tuple-element.64), channel_id=1, source_target_pairs={{0,192},{64,0},{128,64},{192,128},{1,193},{65,1},{129,65},{193,129... | collective-permute-start | bytes 319496 | tf_op jit(solution)/shard_map/ppermute | solution.py:863
  32.2 2.0 %collective-permute-done.6.xlo = f32[13,16,128]{2,1,0:T(8,128)S(1)} collective-permute-done((f32[13,16,128]{2,1,0:T(8,128)S(1)}, f32[13,16,128]{2,1,0:T(8,128)S(1)}, u32[]{:S(2)}, u32[]{:S(2)}) %collective-permute-start.6) | collective-permute-done | bytes 106528 | tf_op jit(solution)/shard_map/ppermute | solution.py:862
  34.2 0.0 collective-permute-done.7.xhi
  34.2 0.6 shard_map.34
  34.8 0.1 collective-permute-start.8
  34.9 3.1 %collective-permute-start.9 = (f32[66,8,128]{2,1,0:T(8,128)S(1)}, f32[66,8,128]{2,1,0:T(8,128)S(1)}, u32[]{:S(2)}, u32[]{:S(2)}) collective-permute-start(f32[66,8,128]{2,1,0:T(8,128)S(1)} %get-tuple-element.67), channel_id=1, source_target_pairs={{0,56},{8,0},{16,8},{24,16},{32,24},{40,32},{48,40},{56,48},{1,57}... | collective-permute-start | bytes 811016 | tf_op jit(solution)/shard_map/ppermute | solution.py:863
  38.0 3.8 %collective-permute-done.8.ylo = f32[66,8,128]{2,1,0:T(8,128)S(1)} collective-permute-done((f32[66,8,128]{2,1,0:T(8,128)S(1)}, f32[66,8,128]{2,1,0:T(8,128)S(1)}, u32[]{:S(2)}, u32[]{:S(2)}) %collective-permute-start.8) | collective-permute-done | bytes 270368 | tf_op jit(solution)/shard_map/ppermute | solution.py:862
  41.8 0.0 collective-permute-done.9.yhi
  41.8 1.2 %shard_map.35 = (f32[11,48,128]{2,1,0:T(8,128)S(1)}, f32[11,48,128]{2,1,0:T(8,128)S(1)}) custom-call(s32[3]{0:T(128)S(1)} %pad_add_fusion.pos, f32[42,16,128]{2,1,0:T(8,128)S(1)} %get-tuple-element.65.own, f32[66,8,128]{2,1,0:T(8,128)S(1)} %collective-permute-done.8.ylo, f32[66,8,128]{2,1,0:T(8,128)S(1)} %collective-permute-done.9.yhi), custom_call_target="tpu_custom_call" | custom-call | tf_op jit(solution)/shard_map/pallas_call | solution.py:838
  43.0 5.6 %collective-permute-start.10 = (f32[11,48,128]{2,1,0:T(8,128)S(1)}, f32[11,48,128]{2,1,0:T(8,128)S(1)}, u32[]{:S(2)}, u32[]{:S(2)}) collective-permute-start(f32[11,48,128]{2,1,0:T(8,128)S(1)} %get-tuple-element.68), channel_id=1, source_target_pairs={{0,1},{1,2},{2,3},{3,4},{4,5},{5,6},{6,7},{7,0},{8,9},{9,10},{10,1... | collective-permute-start | bytes 811016 | tf_op jit(solution)/shard_map/ppermute | solution.py:862
  48.6 0.0 collective-permute-start.11
  48.6 3.4 %collective-permute-done.10.zlo = f32[11,48,128]{2,1,0:T(8,128)S(1)} collective-permute-done((f32[11,48,128]{2,1,0:T(8,128)S(1)}, f32[11,48,128]{2,1,0:T(8,128)S(1)}, u32[]{:S(2)}, u32[]{:S(2)}) %collective-permute-start.10) | collective-permute-done | bytes 270368 | tf_op jit(solution)/shard_map/ppermute | solution.py:862
  52.0 2.5 %collective-permute-done.11.zhi = f32[11,48,128]{2,1,0:T(8,128)S(1)} collective-permute-done((f32[11,48,128]{2,1,0:T(8,128)S(1)}, f32[11,48,128]{2,1,0:T(8,128)S(1)}, u32[]{:S(2)}, u32[]{:S(2)}) %collective-permute-start.11) | collective-permute-done | bytes 270368 | tf_op jit(solution)/shard_map/ppermute | solution.py:863
  54.4 9.2 %shard_map.36 = (f32[32,4,128]{2,1,0:T(4,128)S(1)}, f32[42,64,128]{2,1,0:T(8,128)S(1)}, f32[42,64,128]{2,1,0:T(8,128)S(1)}, f32[42,64,128]{2,1,0:T(8,128)S(1)}, ...) custom-call(s32[3]{0:T(128)S(1)} %pad_add_fusion.pos, ...), custom_call_target="tpu_custom_call" | custom-call | tf_op jit(solution)/shard_map/pallas_call | solution.py:838
  63.6 17.2 %all_to_all.5 = f32[32,4,128]{2,1,0:T(4,128)S(1)} all-to-all(f32[32,4,128]{2,1,0:T(4,128)S(1)} %get-tuple-element.70), channel_id=1, replica_groups=mesh['gx'=4,'gy'=8,'gz'=8] {'gx','gy'}, dimensions={0} | all-to-all | bytes 131072 | tf_op jit(solution)/shard_map/all_to_all | solution.py:901
  80.8 1.8 %collective-permute-start.15 = (f32[128,128]{1,0:T(8,128)S(1)}, f32[128,128]{1,0:T(8,128)S(1)}, u32[]{:S(2)}, u32[]{:S(2)}) collective-permute-start(f32[128,128]{1,0:T(8,128)S(1)} %bitcast.4), channel_id=1, source_target_pairs={{0,1},{1,2},{2,3},{3,4},{4,5},{5,6},{6,7},{7,0},{8,9},{9,10},{10,1... | collective-permute-start | bytes 196616 | tf_op jit(solution)/shard_map/ppermute | solution.py:904
  82.6 0.7 collective-permute-start.14
  83.3 2.0 %collective-permute-start.13 = (f32[128,128]{1,0:T(8,128)S(1)}, f32[128,128]{1,0:T(8,128)S(1)}, u32[]{:S(2)}, u32[]{:S(2)}) collective-permute-start(f32[128,128]{1,0:T(8,128)S(1)} %bitcast.6), channel_id=1, source_target_pairs={{0,6},{1,7},{2,0},{3,1},{4,2},{5,3},{6,4},{7,5},{8,14},{9,15},{10,... | collective-permute-start | bytes 196616 | tf_op jit(solution)/shard_map/ppermute | solution.py:904
  85.3 0.5 collective-permute-start.12
  85.8 0.0 collective-permute-done.15.down1
  85.8 2.5 %collective-permute-done.14.down2 = f32[128,128]{1,0:T(8,128)S(1)} collective-permute-done((f32[128,128]{1,0:T(8,128)S(1)}, f32[128,128]{1,0:T(8,128)S(1)}, u32[]{:S(2)}, u32[]{:S(2)}) %collective-permute-start.14) | collective-permute-done | bytes 65568 | tf_op jit(solution)/shard_map/ppermute | solution.py:904
  88.3 0.0 collective-permute-done.13.up2
  88.3 0.7 collective-permute-done.12.up1
  89.0 14.7 %shard_map.37 = f32[32,32,128]{2,1,0:T(8,128)} custom-call(s32[3]{0:T(128)S(1)} %pad_add_fusion.pos, f32[128,128]{1,0:T(8,128)S(1)} %bitcast.8, f32[128,128]{1,0:T(8,128)S(1)} %collective-permute-done.12.up1, f32[128,128]{1,0:T(8,128)S(1)} %collective-permute-done.13.up2, f32[128,128]{1,0:T(8,128)S(1)} %collective-permute-done.14.down2, ...), custom_call_target="tpu_custom_call" | custom-call | tf_op jit(solution)/shard_map/pallas_call | solution.py:838
Async XLA Ops:
  1.0 5.6 %collective-permute-start = (f32[7,32,128]{2,1,0:T(8,128)S(1)}, f32[7,32,128]{2,1,0:T(8,128)S(1)}, u32[]{:S(2)}, u32[]{:S(2)}) collective-permute-start(f32[7,32,128]{2,1,0:T(8,128)S(1)} %get-tuple-element.50), channel_id=1, source_target_pairs={{0,64},{64,128},{128,192},{192,0},{1,65},{65,129},{129,193},{193,1... | collective-permute-start | bytes 344072 | tf_op jit(solution)/shard_map/ppermute | solution.py:862
  3.1 3.6 %collective-permute-start.1 = (f32[7,32,128]{2,1,0:T(8,128)S(1)}, f32[7,32,128]{2,1,0:T(8,128)S(1)}, u32[]{:S(2)}, u32[]{:S(2)}) collective-permute-start(f32[7,32,128]{2,1,0:T(8,128)S(1)} %get-tuple-element.51), channel_id=1, source_target_pairs={{0,192},{64,0},{128,64},{192,128},{1,193},{65,1},{129,65},{193,129... | collective-permute-start | bytes 344072 | tf_op jit(solution)/shard_map/ppermute | solution.py:863
  7.4 8.7 %collective-permute-start.2 = (f32[40,8,128]{2,1,0:T(8,128)S(1)}, f32[40,8,128]{2,1,0:T(8,128)S(1)}, u32[]{:S(2)}, u32[]{:S(2)}) collective-permute-start(f32[40,8,128]{2,1,0:T(8,128)S(1)} %get-tuple-element.52), channel_id=1, source_target_pairs={{0,8},{8,16},{16,24},{24,32},{32,40},{40,48},{48,56},{56,0},{1,9},... | collective-permute-start | bytes 491528 | tf_op jit(solution)/shard_map/ppermute | solution.py:862
  9.5 6.7 %collective-permute-start.3 = (f32[40,8,128]{2,1,0:T(8,128)S(1)}, f32[40,8,128]{2,1,0:T(8,128)S(1)}, u32[]{:S(2)}, u32[]{:S(2)}) collective-permute-start(f32[40,8,128]{2,1,0:T(8,128)S(1)} %get-tuple-element.53), channel_id=1, source_target_pairs={{0,56},{8,0},{16,8},{24,16},{32,24},{40,32},{48,40},{56,48},{1,57}... | collective-permute-start | bytes 491528 | tf_op jit(solution)/shard_map/ppermute | solution.py:863
  17.9 5.7 %collective-permute-start.5 = (f32[3,40,128]{2,1,0:T(8,128)S(1)}, f32[3,40,128]{2,1,0:T(8,128)S(1)}, u32[]{:S(2)}, u32[]{:S(2)}) collective-permute-start(f32[3,40,128]{2,1,0:T(8,128)S(1)} %get-tuple-element.60.low), channel_id=1, source_target_pairs={{0,7},{1,0},{2,1},{3,2},{4,3},{5,4},{6,5},{7,6},{8,15},{9,8},{10,9... | collective-permute-start | bytes 184328 | tf_op jit(solution)/shard_map/ppermute | solution.py:863
  20.5 3.1 %collective-permute-start.4 = (f32[3,40,128]{2,1,0:T(8,128)S(1)}, f32[3,40,128]{2,1,0:T(8,128)S(1)}, u32[]{:S(2)}, u32[]{:S(2)}) collective-permute-start(f32[3,40,128]{2,1,0:T(8,128)S(1)} %get-tuple-element.61.high), channel_id=1, source_target_pairs={{0,1},{1,2},{2,3},{3,4},{4,5},{5,6},{6,7},{7,0},{8,9},{9,10},{10,1... | collective-permute-start | bytes 184328 | tf_op jit(solution)/shard_map/ppermute | solution.py:862
  29.4 4.8 %collective-permute-start.6 = (f32[13,16,128]{2,1,0:T(8,128)S(1)}, f32[13,16,128]{2,1,0:T(8,128)S(1)}, u32[]{:S(2)}, u32[]{:S(2)}) collective-permute-start(f32[13,16,128]{2,1,0:T(8,128)S(1)} %get-tuple-element.63), channel_id=1, source_target_pairs={{0,64},{64,128},{128,192},{192,0},{1,65},{65,129},{129,193},{193,1... | collective-permute-start | bytes 319496 | tf_op jit(solution)/shard_map/ppermute | solution.py:862
  30.7 3.6 %collective-permute-start.7 = (f32[13,16,128]{2,1,0:T(8,128)S(1)}, f32[13,16,128]{2,1,0:T(8,128)S(1)}, u32[]{:S(2)}, u32[]{:S(2)}) collective-permute-start(f32[13,16,128]{2,1,0:T(8,128)S(1)} %get-tuple-element.64), channel_id=1, source_target_pairs={{0,192},{64,0},{128,64},{192,128},{1,193},{65,1},{129,65},{193,129... | collective-permute-start | bytes 319496 | tf_op jit(solution)/shard_map/ppermute | solution.py:863
  34.8 7.0 %collective-permute-start.8 = (f32[66,8,128]{2,1,0:T(8,128)S(1)}, f32[66,8,128]{2,1,0:T(8,128)S(1)}, u32[]{:S(2)}, u32[]{:S(2)}) collective-permute-start(f32[66,8,128]{2,1,0:T(8,128)S(1)} %get-tuple-element.66), channel_id=1, source_target_pairs={{0,8},{8,16},{16,24},{24,32},{32,40},{40,48},{48,56},{56,0},{1,9},... | collective-permute-start | bytes 811016 | tf_op jit(solution)/shard_map/ppermute | solution.py:862
  34.9 6.9 %collective-permute-start.9 = (f32[66,8,128]{2,1,0:T(8,128)S(1)}, f32[66,8,128]{2,1,0:T(8,128)S(1)}, u32[]{:S(2)}, u32[]{:S(2)}) collective-permute-start(f32[66,8,128]{2,1,0:T(8,128)S(1)} %get-tuple-element.67), channel_id=1, source_target_pairs={{0,56},{8,0},{16,8},{24,16},{32,24},{40,32},{48,40},{56,48},{1,57}... | collective-permute-start | bytes 811016 | tf_op jit(solution)/shard_map/ppermute | solution.py:863
  43.0 9.0 %collective-permute-start.10 = (f32[11,48,128]{2,1,0:T(8,128)S(1)}, f32[11,48,128]{2,1,0:T(8,128)S(1)}, u32[]{:S(2)}, u32[]{:S(2)}) collective-permute-start(f32[11,48,128]{2,1,0:T(8,128)S(1)} %get-tuple-element.68), channel_id=1, source_target_pairs={{0,1},{1,2},{2,3},{3,4},{4,5},{5,6},{6,7},{7,0},{8,9},{9,10},{10,1... | collective-permute-start | bytes 811016 | tf_op jit(solution)/shard_map/ppermute | solution.py:862
  48.6 5.9 %collective-permute-start.11 = (f32[11,48,128]{2,1,0:T(8,128)S(1)}, f32[11,48,128]{2,1,0:T(8,128)S(1)}, u32[]{:S(2)}, u32[]{:S(2)}) collective-permute-start(f32[11,48,128]{2,1,0:T(8,128)S(1)} %get-tuple-element.69), channel_id=1, source_target_pairs={{0,7},{1,0},{2,1},{3,2},{4,3},{5,4},{6,5},{7,6},{8,15},{9,8},{10,9... | collective-permute-start | bytes 811016 | tf_op jit(solution)/shard_map/ppermute | solution.py:863
  80.8 4.9 %collective-permute-start.15 = (f32[128,128]{1,0:T(8,128)S(1)}, f32[128,128]{1,0:T(8,128)S(1)}, u32[]{:S(2)}, u32[]{:S(2)}) collective-permute-start(f32[128,128]{1,0:T(8,128)S(1)} %bitcast.4), channel_id=1, source_target_pairs={{0,1},{1,2},{2,3},{3,4},{4,5},{5,6},{6,7},{7,0},{8,9},{9,10},{10,1... | collective-permute-start | bytes 196616 | tf_op jit(solution)/shard_map/ppermute | solution.py:904
  82.6 5.7 %collective-permute-start.14 = (f32[128,128]{1,0:T(8,128)S(1)}, f32[128,128]{1,0:T(8,128)S(1)}, u32[]{:S(2)}, u32[]{:S(2)}) collective-permute-start(f32[128,128]{1,0:T(8,128)S(1)} %bitcast.5), channel_id=1, source_target_pairs={{0,2},{1,3},{2,4},{3,5},{4,6},{5,7},{6,0},{7,1},{8,10},{9,11},{10,... | collective-permute-start | bytes 196616 | tf_op jit(solution)/shard_map/ppermute | solution.py:904
  83.3 5.0 %collective-permute-start.13 = (f32[128,128]{1,0:T(8,128)S(1)}, f32[128,128]{1,0:T(8,128)S(1)}, u32[]{:S(2)}, u32[]{:S(2)}) collective-permute-start(f32[128,128]{1,0:T(8,128)S(1)} %bitcast.6), channel_id=1, source_target_pairs={{0,6},{1,7},{2,0},{3,1},{4,2},{5,3},{6,4},{7,5},{8,14},{9,15},{10,... | collective-permute-start | bytes 196616 | tf_op jit(solution)/shard_map/ppermute | solution.py:904
  85.3 3.7 %collective-permute-start.12 = (f32[128,128]{1,0:T(8,128)S(1)}, f32[128,128]{1,0:T(8,128)S(1)}, u32[]{:S(2)}, u32[]{:S(2)}) collective-permute-start(f32[128,128]{1,0:T(8,128)S(1)} %bitcast.7), channel_id=1, source_target_pairs={{0,7},{1,0},{2,1},{3,2},{4,3},{5,4},{6,5},{7,6},{8,15},{9,8},{10,9... | collective-permute-start | bytes 196616 | tf_op jit(solution)/shard_map/ppermute | solution.py:904

commit v3 on v2

--- a/solution.py
+++ b/solution.py
@@ -248,13 +248,23 @@
         wz[p, here] = rcp(v + pltpu.roll(v, 127, 1))
         sums[p, here] = rcp(v + q[p - 1, here]) + face_x + face_y + rcp(v + q[p, 7:47])
 
-    loop(1, N2 - 1, body, 4)
+    loop(1, N2 - 1, body, 8)
+
+
+def add_kernel(pos, first, second, out):
+    planes, rows = out.shape[0], out.shape[1] - 16
+    here = slice(8, 8 + rows)
+
+    def add(p):
+        out[p, here] = first[p, here] + second[p, here]
+
+    loop(0, planes, add, 8)
 
 
 def down_kernel(
     pos, eb, ek, wx, wy, wz, sums, low, high, zlo, zhi,
-    bk3, low3, high3, inv, xs, tb, twx, twy, twz, tinv, tx,
-    f, r1, s, tq, tf, ts, face_w, face_f, face_s, tmp,
+    bk3, low3, high3, inv, f, s, tb, twx, twy, twz, tinv, tx,
+    r1, tq, tf, ts, face_w, face_f, face_s, tmp,
 ):
     gx, gy, gz = pos[0], pos[1], pos[2]
     lane = lanes_of(R2)
@@ -325,14 +335,13 @@
         inv[p, here] = value
         f[p, here] = value * eb[p, here] * inv_center
 
-    loop(1, N2 - 1, weigh, 4)
+    loop(1, N2 - 1, weigh, 13)
 
     def smooth(p):
         rest = eb[p, here] - flux_two(f, wx, wy, wz, face_f, p, 8, R2)
         step = keep_coef * f[p, here] + push_coef * inv[p, here] * rest
         r1[p, here] = rest
         s[p, here] = step
-        xs[p, here] = f[p, here] + step
 
     loop(2, N2 - 2, smooth, 6)
 
@@ -425,7 +434,7 @@
     return (fx - gx) + (fy - gy) + (fz - pltpu.roll(fz, 1, 1))
 
 
-UNROLL = {48: 4, 24: 6, 32: 8, 16: 8, 8: 4}
+UNROLL = {48: 10, 24: 9, 32: 8, 16: 8, 8: 4}
 
 
 def weigh_one(q, b, wx, wy, wz, inv, f, rows, low, high, first, last, inside):
@@ -460,7 +469,8 @@
         step = keep_coef * f[p, here] + push_coef * inv[p, here] * rest
         r1[p, here] = rest
         s[p, here] = step
-        xs[p, here] = f[p, here] + step
+        if xs is not None:
+            xs[p, here] = f[p, here] + step
 
     loop(low, high, body, UNROLL[rows])
 
@@ -489,8 +499,8 @@
 
 def middle_kernel(
     pos, own, ylo, yhi, zlo, zhi,
-    payload, b3, wx3, wy3, wz3, inv3, x3, b4, wx4, wy4, wz4, inv4, x4,
-    k3, q3, f3, r3, s3, k4, q4, f4, r4, s4, tmp,
+    payload, b3, wx3, wy3, wz3, inv3, f3, s3, b4, wx4, wy4, wz4, inv4, f4, s4,
+    k3, q3, r3, k4, q4, r4, tmp,
 ):
     gx, gy, gz = pos[0], pos[1], pos[2]
     lane = lanes_of(16)
@@ -536,14 +546,14 @@
 
     inside = region(R3, -16, -13, 16, 16, 64)
     weigh_one(q3, b3, wx3, wy3, wz3, inv3, f3, R3, 1, N3 - 1, *edges(R3, 64), inside)
-    smooth_one(b3, wx3, wy3, wz3, inv3, f3, r3, s3, x3, R3, 2, N3 - 2)
+    smooth_one(b3, wx3, wy3, wz3, inv3, f3, r3, s3, None, R3, 2, N3 - 2)
 
     def pick(i, j):
         target = signed(j, 64)
-        return ((signed(i, 96) >> 1) == target) & (target >= -6) & (target < 38)
+        return ((signed(i, 96) >> 1) == target) & (target >= -7) & (target < 39)
 
     narrow = square(pick, 0.125)
-    valid = (lanes_of(R4) < 38) | (lanes_of(R4) >= 122)
+    valid = (lanes_of(R4) < 39) | (lanes_of(R4) >= 121)
     row = rows_of(R4)
 
     def coarse_k(i):
@@ -575,12 +585,19 @@
     loop(0, N4, invert, 5)
     inside = region(R4, -6, -6, 8, 8, 32)
     weigh_one(q4, b4, wx4, wy4, wz4, inv4, f4, R4, 1, N4 - 1, *edges(R4, 32), inside)
-    smooth_one(b4, wx4, wy4, wz4, inv4, f4, r4, s4, x4, R4, 2, N4 - 2)
-
-    spread = square(lambda i, j: (i < 32) & ((i >> 1) == (j & 15)), 0.125)
+    smooth_one(b4, wx4, wy4, wz4, inv4, f4, r4, s4, None, R4, 2, N4 - 2)
+
+    cell = lanes_of(4) & 15
+    spread = square(lambda i, j: (signed(i, 64) >> 1) == (j & 15), 0.125)
+    spread_halo = square(
+        lambda i, j: ((signed(i, 64) >> 1) == ((j & 15) ^ 16) - ((j & 8) << 2))
+        & (((j & 15) < 4) | ((j & 15) >= 12)),
+        0.125,
+    )
+    between = (cell >= 4) & (cell < 12)
     slot = lanes_of(4) >> 4
     quad = rows_of(4)
-    parts = [[None, None], [None, None]]
+    parts = [[[None, None], [None, None]] for _ in range(2)]
     for i in range(4):
         p = 2 * i + 6
         total = r4[p, 8:32] + r4[p + 1, 8:32] - flux_one(s4, wx4, wy4, wz4, p, R4)
@@ -589,12 +606,15 @@
     for i in range(4):
         mine = slot == (i % 2) * 4 + quad
         for a in range(2):
-            value = row_pairs(tmp.at[a], [i], 14, 4)
-            value = jnp.where(mine, select_dot(value, spread), 0.0)
-            value = jnp.sum(value, axis=0, keepdims=True)
-            old = parts[a][i // 2]
-            parts[a][i // 2] = value if old is None else old + value
-    value = jnp.concatenate(parts[0] + parts[1], axis=0)
+            pair = row_pairs(tmp.at[a], [i], 14, 4)
+            for h, matrix in enumerate((spread, spread_halo)):
+                value = select_dot(pair, matrix)
+                if h == 1:
+                    value = jnp.where(between, 1.0, value)
+                value = jnp.sum(jnp.where(mine, value, 0.0), axis=0, keepdims=True)
+                old = parts[h][a][i // 2]
+                parts[h][a][i // 2] = value if old is None else old + value
+    value = jnp.concatenate([row for h in parts for a in h for row in a], axis=0)
     for d in range(32):
         payload[d] = value
 
@@ -615,13 +635,13 @@
 
 
 def up_kernel(
-    pos, own, up1, up2, down2, down1, b3, wx3, wy3, wz3, inv3, x3, b4, wx4, wy4, wz4, inv4, x4,
+    pos, own, up, down, b3, wx3, wy3, wz3, inv3, x3, b4, wx4, wy4, wz4, inv4, x4,
     eb, wx, wy, wz, inv, xs, tb, twx, twy, twz, tinv, tx,
     out, *scratch,
 ):
     gx, gy, gz = pos[0], pos[1], pos[2]
     levels = [scratch[12 * i : 12 * i + 12] for i in range(3)]
-    e5, e6, raw, f4, r4, e4, y4, f3, r3, e3, y3, f2, r2, y2, tf, ty, face_x, face_f, tmp = scratch[36:]
+    e5, e6, raw, f4, r4, e4, y4, f3, r3, e3, y3, f2, r2, y2, tf, ty, face_x, face_f, ob, tmp, sems = scratch[36:]
 
     for level, (nx, ny, nz) in enumerate(WHOLE):
         b, k, q, wx_, wy_, wz_, inv_, f, r, s, x, r0 = levels[level]
@@ -645,10 +665,11 @@
 
     b5, k5 = levels[0][0], levels[0][1]
 
-    unused = jnp.ones((128, 128), F32)
-    parts = (own[...], up1[...], up2[...], unused, unused, unused, down2[...], down1[...])
-    for n, part in enumerate(parts):
-        raw[pl.ds(n, 128, stride=8)] = part
+    for n in (3, 4, 5):
+        raw[pl.ds(n, 128, stride=8)] = jnp.ones((128, 128), F32)
+    for n, part, first in ((0, own, 0), (1, up, 0), (2, up, 4), (6, down, 4), (7, down, 0)):
+        for kind in range(4):
+            raw[pl.ds(8 * kind + n, 32, stride=32)] = part[pl.ds(first + kind, 32, stride=8)]
 
     def unpack(d):
         dx, dy = d // 8, d % 8
@@ -660,7 +681,7 @@
             target[p, rows] = value[0:4]
             target[p + 1, rows] = value[4:8]
 
-    loop(0, 32, unpack, 4)
+    loop(0, 32, unpack, 8)
 
     def ends(level):
         nx, ny, nz = WHOLE[level]
@@ -722,7 +743,7 @@
     for level in range(3):
         down(level)
 
-    def up(level, coarse, target, shift):
+    def rise(level, coarse, target, shift):
         nx, ny, nz = WHOLE[level]
         b, k, q, wx_, wy_, wz_, inv_, f, r, s, x, r0 = levels[level]
         widen = square(lambda i, j: signed(i, 64) == (signed(j, 64) >> 1), 1.0)
@@ -741,8 +762,8 @@
         span = (1, nx + 1)
         finish_one(b, wx_, wy_, wz_, inv_, x, f, r0, target, shift, ny, (span, span))
 
-    up(1, levels[2][10], e6, 0)
-    up(0, e6, e5, 2)
+    rise(1, levels[2][10], e6, 0)
+    rise(0, e6, e5, 2)
 
     widen = square(lambda i, j: signed(i, 64) == (signed(j, 64) >> 1), 1.0)
 
@@ -814,7 +835,7 @@
         r2[p, here] = rest
         f2[p, here] = inv[p, here] * rest * inv_center
 
-    loop(3, 37, start, 5)
+    loop(3, 37, start, 7)
     core = slice(12, 44)
 
     def end(i):
@@ -822,9 +843,20 @@
         rest = r2[p, core] - flux_two(f2, wx, wy, wz, face_f, p, 12, 32)
         first = f2[p, core]
         step = keep_coef * first + push_coef * inv[p, core] * rest
-        out[i] = y2[p, core] + first + step
-
-    loop(0, 32, end, 8)
+        ob[i] = y2[p, core] + first + step
+
+    def leave(n):
+        part = pl.ds(pl.multiple_of(8 * n, 8), 8)
+        return pltpu.make_async_copy(ob.at[part], out.at[part], sems.at[n])
+
+    @pl.loop(0, 4)
+    def _(n):
+        for j in range(8):
+            end(8 * n + j)
+        leave(n).start()
+
+    for n in range(4):
+        leave(n).wait()
 
 
 def vmem(array):
@@ -840,8 +872,9 @@
         out_shape=[out_type(shape, F32) for shape in outs],
         in_specs=[pl.BlockSpec(memory_space=pltpu.SMEM)]
         + [pl.BlockSpec(memory_space=pltpu.VMEM)] * len(held),
-        out_specs=[pl.BlockSpec(memory_space=pltpu.VMEM)] * len(outs),
-        scratch_shapes=[pltpu.VMEM(shape, F32) for shape in scratch],
+        out_specs=[pl.BlockSpec(memory_space=pl.ANY if final else pltpu.VMEM)] * len(outs),
+        scratch_shapes=[pltpu.VMEM(shape, F32) for shape in scratch]
+        + [pltpu.SemaphoreType.DMA((4,))] * final,
         compiler_params=pltpu.CompilerParams(vmem_limit_bytes=size + (4 << 20)),
     )(args[0], *held)
 
@@ -877,13 +910,14 @@
     )
     zlo, zhi = swap(low, high, "gz")
     wx, wy, wz, sums = call(weights_kernel, (pos, ek), [ext2] * 4, [ext2])
-    bk3, low, high, *rest = call(
+    bk3, low, high, inv, first, second, *rest = call(
         down_kernel,
         (pos, eb, ek, wx, wy, wz, sums, low, high, zlo, zhi),
-        [(16, 16, 128)] + [(13, 16, 128)] * 2 + [ext2] * 2 + [strip] * 6,
-        [ext2] * 3 + [strip] * 3 + [face] * 3 + [(2, 16, 32, 128)],
+        [(16, 16, 128)] + [(13, 16, 128)] * 2 + [ext2] * 3 + [strip] * 6,
+        [ext2] + [strip] * 3 + [face] * 3 + [(2, 16, 32, 128)],
     )
-    state2 = [eb, wx, wy, wz, *rest]
+    (xs,) = call(add_kernel, (pos, first, second), [ext2])
+    state2 = [eb, wx, wy, wz, inv, xs, *rest]
     xlo, xhi = swap(low, high, "gx")
     own, low, high = call(
         planes_kernel, (pos, bk3, xlo, xhi), [(N3, 16, 128)] + [(N3 + 24, 8, 128)] * 2
@@ -895,20 +929,23 @@
     payload, *state = call(
         middle_kernel,
         (pos, own, ylo, yhi, zlo, zhi),
-        [(32, 4, 128)] + [three] * 6 + [four] * 6,
-        [three] * 5 + [four] * 5 + [(2, N4, T3, 128)],
+        [(32, 8, 128)] + [three] * 7 + [four] * 7,
+        [three] * 3 + [four] * 3 + [(2, N4, T3, 128)],
     )
-    recv = lax.all_to_all(payload, AXES[:2], 0, 0, tiled=True).reshape(128, 128)
+    (x3,) = call(add_kernel, (pos, *state[5:7]), [three])
+    (x4,) = call(add_kernel, (pos, *state[12:14]), [four])
+    state = [*state[:5], x3, *state[7:12], x4]
+    recv = lax.all_to_all(payload, AXES[:2], 0, 0, tiled=True).reshape(256, 128)
     ring = range(DEV[2])
     recv = [recv] + [
-        lax.ppermute(recv, "gz", [(i, (i - d) % DEV[2]) for i in ring]) for d in (1, 2, -2, -1)
+        lax.ppermute(recv, "gz", [(i, (i - d) % DEV[2]) for i in ring]) for d in (1, -1)
     ]
     recv = [vmem(part) for part in recv]
     scratch = []
     for nx, ny, _ in WHOLE:
         scratch += [(nx + 2, ny + 16, 128)] * 12
     scratch += [(22, 56, 128), (10, 32, 128), (1024, 128)]
-    scratch += [four] * 4 + [three] * 4 + [ext2] * 3 + [strip] * 2 + [face] * 2
+    scratch += [four] * 4 + [three] * 4 + [ext2] * 3 + [strip] * 2 + [face] * 2 + [(32, 32, 128)]
     scratch += [(2, 20, T3, 128)]
     (out,) = call(up_kernel, (pos, *recv, *state, *state2), [(32, 32, 128)], scratch, True)
     return out

time: 104 us -> 99.5 us (0.957)
  starting transfers between devices: 30 us -> 27.1 us
  Pallas kernels: 37.8 us -> 36.3 us
    ppermute x4 -> x2, starting transfers between devices: 4.94 us -> 2.11 us  [shards(): lax.ppermute(recv, 'gz', [(i, (i - d) % DEV[2]) for i in ring])]
    pallas_call x8 -> x11, Pallas kernels: 35.5 us -> 34 us  [call(): pl.pallas_call(kernel, out_shape=[out_type(shape, F32) for shape in outs]...]
    ppermute x4 -> x2, waiting for transfers between devices: 3.19 us -> 2.63 us  [shards(): lax.ppermute(recv, 'gz', [(i, (i - d) % DEV[2]) for i in ring])]
  transfers between devices with their start and end apart: 16 -> 14, of which waited for: 10 -> 9; matrix products, arithmetic and copies ran while one was open for 0% -> 0% of each run, Pallas kernels for 3% -> 5%
where the time goes in v3:
time: 99.5 us; the launch traced here: 99.2 us
  Pallas kernels  36.3 us (36%)
  starting transfers between devices  27.1 us (27%)
  waiting for transfers between devices  18 us (18%)
  blocking collectives  17.4 us (17%)
    pallas_call x11, Pallas kernels, call(): pl.pallas_call(kernel, out_shape=[out_type(shape, F32) for shape in outs]...  34 us
    all_to_all x1, blocking collectives, shards(): recv = lax.all_to_all(payload, AXES[:2], 0, 0, tiled=True).reshape(256, 128)  17.4 us
    ppermute x6, starting transfers between devices, swap(): after = lax.ppermute(low, axis, [(i, (i - 1) % count) for i in ring])  12.7 us
    ppermute x6, waiting for transfers between devices, swap(): before = lax.ppermute(high, axis, [(i, (i + 1) % count) for i in ring])  12.4 us
    ppermute x6, starting transfers between devices, swap(): before = lax.ppermute(high, axis, [(i, (i + 1) % count) for i in ring])  12.4 us
    ppermute x6, waiting for transfers between devices, swap(): after = lax.ppermute(low, axis, [(i, (i - 1) % count) for i in ring])  2.97 us
    ppermute x2, waiting for transfers between devices, shards(): lax.ppermute(recv, 'gz', [(i, (i - d) % DEV[2]) for i in ring])  2.63 us
    pallas_call x2, Pallas kernels, load(): pl.pallas_call(kernel, out_shape=[pltpu.VMEM(shape, F32)] * 2, in_specs=[...  2.31 us
  transfers between devices with their start and end apart: 14, of which 9 were waited for; matrix products, arithmetic and copies ran while one was open for 0% of the time, Pallas kernels for 5%

profile of v3, /device:TPU:1, one launch (start us, length us, event | category | flops | bytes accessed | tf_op | source)
XLA Modules:
  0.0 99.2 jit_solution(6065140830584073496)
XLA Ops:
  0.0 1.0 shard_map.29
  1.0 2.1 %collective-permute-start = (f32[7,32,128]{2,1,0:T(8,128)S(1)}, f32[7,32,128]{2,1,0:T(8,128)S(1)}, u32[]{:S(2)}, u32[]{:S(2)}) collective-permute-start(f32[7,32,128]{2,1,0:T(8,128)S(1)} %get-tuple-element.53), channel_id=1, source_target_pairs={{0,64},{64,128},{128,192},{192,0},{1,65},{65,129},{129,193},{193,1... | collective-permute-start | bytes 344072 | tf_op jit(solution)/shard_map/ppermute | solution.py:895
  3.1 1.4 %collective-permute-start.1 = (f32[7,32,128]{2,1,0:T(8,128)S(1)}, f32[7,32,128]{2,1,0:T(8,128)S(1)}, u32[]{:S(2)}, u32[]{:S(2)}) collective-permute-start(f32[7,32,128]{2,1,0:T(8,128)S(1)} %get-tuple-element.54), channel_id=1, source_target_pairs={{0,192},{64,0},{128,64},{192,128},{1,193},{65,1},{129,65},{193,129... | collective-permute-start | bytes 344072 | tf_op jit(solution)/shard_map/ppermute | solution.py:896
  4.4 1.3 %shard_map.28 = (f32[32,32,128]{2,1,0:T(8,128)S(1)}, f32[32,32,128]{2,1,0:T(8,128)S(1)}) custom-call(f32[32,32,128]{2,1,0:T(8,128)} %b.3, f32[32,32,128]{2,1,0:T(8,128)} %k.3), custom_call_target="tpu_custom_call" | custom-call | tf_op jit(solution)/shard_map/pallas_call | solution.py:883
  5.8 0.1 pad_add_fusion.pos
  5.9 0.7 collective-permute-done.xlo
  6.5 0.2 collective-permute-done.1.xhi
  6.7 0.6 shard_map.30
  7.4 2.1 %collective-permute-start.2 = (f32[40,8,128]{2,1,0:T(8,128)S(1)}, f32[40,8,128]{2,1,0:T(8,128)S(1)}, u32[]{:S(2)}, u32[]{:S(2)}) collective-permute-start(f32[40,8,128]{2,1,0:T(8,128)S(1)} %get-tuple-element.55), channel_id=1, source_target_pairs={{0,8},{8,16},{16,24},{24,32},{32,40},{40,48},{48,56},{56,0},{1,9},... | collective-permute-start | bytes 491528 | tf_op jit(solution)/shard_map/ppermute | solution.py:895
  9.5 4.0 %collective-permute-start.3 = (f32[40,8,128]{2,1,0:T(8,128)S(1)}, f32[40,8,128]{2,1,0:T(8,128)S(1)}, u32[]{:S(2)}, u32[]{:S(2)}) collective-permute-start(f32[40,8,128]{2,1,0:T(8,128)S(1)} %get-tuple-element.56), channel_id=1, source_target_pairs={{0,56},{8,0},{16,8},{24,16},{32,24},{40,32},{48,40},{56,48},{1,57}... | collective-permute-start | bytes 491528 | tf_op jit(solution)/shard_map/ppermute | solution.py:896
  13.5 2.6 %collective-permute-done.2.ylo = f32[40,8,128]{2,1,0:T(8,128)S(1)} collective-permute-done((f32[40,8,128]{2,1,0:T(8,128)S(1)}, f32[40,8,128]{2,1,0:T(8,128)S(1)}, u32[]{:S(2)}, u32[]{:S(2)}) %collective-permute-start.2) | collective-permute-done | bytes 163872 | tf_op jit(solution)/shard_map/ppermute | solution.py:895
  16.1 0.0 collective-permute-done.3.yhi
  16.1 1.8 %shard_map.31 = (f32[3,40,128]{2,1,0:T(8,128)S(1)}, f32[3,40,128]{2,1,0:T(8,128)S(1)}, f32[40,56,128]{2,1,0:T(8,128)S(1)}, f32[40,56,128]{2,1,0:T(8,128)S(1)}) custom-call(s32[3]{0:T(128)S(1)} %pad_add_fusion.pos, f32[32,32,128]{2,1,0:T(8,128)S(1)} %get-tuple-element.51.b, f32[32,32,128]{2,1,0:T(8,128)S(1)} %get-tuple-element.52.k, ...), custom_call_target="tpu_custom_call" | custom-call | tf_op jit(solution)/shard_map/pallas_call | solution.py:870
  17.9 2.6 %collective-permute-start.5 = (f32[3,40,128]{2,1,0:T(8,128)S(1)}, f32[3,40,128]{2,1,0:T(8,128)S(1)}, u32[]{:S(2)}, u32[]{:S(2)}) collective-permute-start(f32[3,40,128]{2,1,0:T(8,128)S(1)} %get-tuple-element.63.low), channel_id=1, source_target_pairs={{0,7},{1,0},{2,1},{3,2},{4,3},{5,4},{6,5},{7,6},{8,15},{9,8},{10,9... | collective-permute-start | bytes 184328 | tf_op jit(solution)/shard_map/ppermute | solution.py:896
  20.5 1.2 %collective-permute-start.4 = (f32[3,40,128]{2,1,0:T(8,128)S(1)}, f32[3,40,128]{2,1,0:T(8,128)S(1)}, u32[]{:S(2)}, u32[]{:S(2)}) collective-permute-start(f32[3,40,128]{2,1,0:T(8,128)S(1)} %get-tuple-element.64.high), channel_id=1, source_target_pairs={{0,1},{1,2},{2,3},{3,4},{4,5},{5,6},{6,7},{7,0},{8,9},{9,10},{10,1... | collective-permute-start | bytes 184328 | tf_op jit(solution)/shard_map/ppermute | solution.py:895
  21.7 1.6 %shard_map.32 = (f32[40,56,128]{2,1,0:T(8,128)S(1)}, f32[40,56,128]{2,1,0:T(8,128)S(1)}, f32[40,56,128]{2,1,0:T(8,128)S(1)}, f32[40,56,128]{2,1,0:T(8,128)S(1)}) custom-call(s32[3]{0:T(128)S(1)} %pad_add_fusion.pos, f32[40,56,128]{2,1,0:T(8,128)S(1)} %get-tuple-element.58.ek), custom_call_target="tpu_custom_call" | custom-call | tf_op jit(solution)/shard_map/pallas_call | solution.py:870
  23.3 0.3 collective-permute-done.5.zhi
  23.6 0.0 collective-permute-done.4.zlo
  23.6 4.6 %shard_map.33 = (f32[16,16,128]{2,1,0:T(8,128)S(1)}, f32[13,16,128]{2,1,0:T(8,128)S(1)}, f32[13,16,128]{2,1,0:T(8,128)S(1)}, f32[40,56,128]{2,1,0:T(8,128)S(1)},...) custom-call(s32[3]{0:T(128)S(1)} %pad_add_fusion.pos, ...), custom_call_target="tpu_custom_call" | custom-call | tf_op jit(solution)/shard_map/pallas_call | solution.py:870
  28.3 1.3 %collective-permute-start.6 = (f32[13,16,128]{2,1,0:T(8,128)S(1)}, f32[13,16,128]{2,1,0:T(8,128)S(1)}, u32[]{:S(2)}, u32[]{:S(2)}) collective-permute-start(f32[13,16,128]{2,1,0:T(8,128)S(1)} %get-tuple-element.66), channel_id=1, source_target_pairs={{0,64},{64,128},{128,192},{192,0},{1,65},{65,129},{129,193},{193,1... | collective-permute-start | bytes 319496 | tf_op jit(solution)/shard_map/ppermute | solution.py:895
  29.5 1.6 %collective-permute-start.7 = (f32[13,16,128]{2,1,0:T(8,128)S(1)}, f32[13,16,128]{2,1,0:T(8,128)S(1)}, u32[]{:S(2)}, u32[]{:S(2)}) collective-permute-start(f32[13,16,128]{2,1,0:T(8,128)S(1)} %get-tuple-element.67), channel_id=1, source_target_pairs={{0,192},{64,0},{128,64},{192,128},{1,193},{65,1},{129,65},{193,129... | collective-permute-start | bytes 319496 | tf_op jit(solution)/shard_map/ppermute | solution.py:896
  31.1 2.0 %collective-permute-done.6.xlo = f32[13,16,128]{2,1,0:T(8,128)S(1)} collective-permute-done((f32[13,16,128]{2,1,0:T(8,128)S(1)}, f32[13,16,128]{2,1,0:T(8,128)S(1)}, u32[]{:S(2)}, u32[]{:S(2)}) %collective-permute-start.6) | collective-permute-done | bytes 106528 | tf_op jit(solution)/shard_map/ppermute | solution.py:895
  33.1 0.0 collective-permute-done.7.xhi
  33.1 0.6 shard_map.34
  33.7 0.1 collective-permute-start.8
  33.8 3.1 %collective-permute-start.9 = (f32[66,8,128]{2,1,0:T(8,128)S(1)}, f32[66,8,128]{2,1,0:T(8,128)S(1)}, u32[]{:S(2)}, u32[]{:S(2)}) collective-permute-start(f32[66,8,128]{2,1,0:T(8,128)S(1)} %get-tuple-element.70), channel_id=1, source_target_pairs={{0,56},{8,0},{16,8},{24,16},{32,24},{40,32},{48,40},{56,48},{1,57}... | collective-permute-start | bytes 811016 | tf_op jit(solution)/shard_map/ppermute | solution.py:896
  36.9 3.8 %collective-permute-done.8.ylo = f32[66,8,128]{2,1,0:T(8,128)S(1)} collective-permute-done((f32[66,8,128]{2,1,0:T(8,128)S(1)}, f32[66,8,128]{2,1,0:T(8,128)S(1)}, u32[]{:S(2)}, u32[]{:S(2)}) %collective-permute-start.8) | collective-permute-done | bytes 270368 | tf_op jit(solution)/shard_map/ppermute | solution.py:895
  40.7 0.0 collective-permute-done.9.yhi
  40.7 1.2 %shard_map.35 = (f32[11,48,128]{2,1,0:T(8,128)S(1)}, f32[11,48,128]{2,1,0:T(8,128)S(1)}) custom-call(s32[3]{0:T(128)S(1)} %pad_add_fusion.pos, f32[42,16,128]{2,1,0:T(8,128)S(1)} %get-tuple-element.68.own, f32[66,8,128]{2,1,0:T(8,128)S(1)} %collective-permute-done.8.ylo, f32[66,8,128]{2,1,0:T(8,128)S(1)} %collective-permute-done.9.yhi), custom_call_target="tpu_custom_call" | custom-call | tf_op jit(solution)/shard_map/pallas_call | solution.py:870
  41.9 5.6 %collective-permute-start.10 = (f32[11,48,128]{2,1,0:T(8,128)S(1)}, f32[11,48,128]{2,1,0:T(8,128)S(1)}, u32[]{:S(2)}, u32[]{:S(2)}) collective-permute-start(f32[11,48,128]{2,1,0:T(8,128)S(1)} %get-tuple-element.71), channel_id=1, source_target_pairs={{0,1},{1,2},{2,3},{3,4},{4,5},{5,6},{6,7},{7,0},{8,9},{9,10},{10,1... | collective-permute-start | bytes 811016 | tf_op jit(solution)/shard_map/ppermute | solution.py:895
  47.4 0.0 collective-permute-start.11
  47.4 3.4 %collective-permute-done.10.zlo = f32[11,48,128]{2,1,0:T(8,128)S(1)} collective-permute-done((f32[11,48,128]{2,1,0:T(8,128)S(1)}, f32[11,48,128]{2,1,0:T(8,128)S(1)}, u32[]{:S(2)}, u32[]{:S(2)}) %collective-permute-start.10) | collective-permute-done | bytes 270368 | tf_op jit(solution)/shard_map/ppermute | solution.py:895
  50.8 2.5 %collective-permute-done.11.zhi = f32[11,48,128]{2,1,0:T(8,128)S(1)} collective-permute-done((f32[11,48,128]{2,1,0:T(8,128)S(1)}, f32[11,48,128]{2,1,0:T(8,128)S(1)}, u32[]{:S(2)}, u32[]{:S(2)}) %collective-permute-start.11) | collective-permute-done | bytes 270368 | tf_op jit(solution)/shard_map/ppermute | solution.py:896
  53.3 8.0 %shard_map.36 = (f32[32,8,128]{2,1,0:T(8,128)S(1)}, f32[42,64,128]{2,1,0:T(8,128)S(1)}, f32[42,64,128]{2,1,0:T(8,128)S(1)}, f32[42,64,128]{2,1,0:T(8,128)S(1)}, ...) custom-call(s32[3]{0:T(128)S(1)} %pad_add_fusion.pos, ...), custom_call_target="tpu_custom_call" | custom-call | tf_op jit(solution)/shard_map/pallas_call | solution.py:870
  61.3 17.4 %all_to_all.5 = f32[32,8,128]{2,1,0:T(8,128)S(1)} all-to-all(f32[32,8,128]{2,1,0:T(8,128)S(1)} %get-tuple-element.73), channel_id=1, replica_groups=mesh['gx'=4,'gy'=8,'gz'=8] {'gx','gy'}, dimensions={0} | all-to-all | bytes 262144 | tf_op jit(solution)/shard_map/all_to_all | solution.py:938
  78.8 2.0 %collective-permute-start.13 = (f32[256,128]{1,0:T(8,128)S(1)}, f32[256,128]{1,0:T(8,128)S(1)}, u32[]{:S(2)}, u32[]{:S(2)}) collective-permute-start(f32[256,128]{1,0:T(8,128)S(1)} %bitcast.4), channel_id=1, source_target_pairs={{0,1},{1,2},{2,3},{3,4},{4,5},{5,6},{6,7},{7,0},{8,9},{9,10},{10,1... | collective-permute-start | bytes 393224 | tf_op jit(solution)/shard_map/ppermute | solution.py:941
  80.7 0.2 collective-permute-start.12
  80.9 0.6 shard_map.39.xs
  81.5 0.6 shard_map.38.x4
  82.1 0.7 shard_map.37.x3
  82.8 0.0 collective-permute-done.13.down
  82.8 2.6 %collective-permute-done.12.up = f32[256,128]{1,0:T(8,128)S(1)} collective-permute-done((f32[256,128]{1,0:T(8,128)S(1)}, f32[256,128]{1,0:T(8,128)S(1)}, u32[]{:S(2)}, u32[]{:S(2)}) %collective-permute-start.12) | collective-permute-done | bytes 131104 | tf_op jit(solution)/shard_map/ppermute | solution.py:941
  85.4 13.7 %shard_map.40 = f32[32,32,128]{2,1,0:T(8,128)} custom-call(s32[3]{0:T(128)S(1)} %pad_add_fusion.pos, f32[256,128]{1,0:T(8,128)S(1)} %bitcast.6, f32[256,128]{1,0:T(8,128)S(1)} %collective-permute-done.12.up, f32[256,128]{1,0:T(8,128)S(1)} %collective-permute-done.13.down, f32[42,64,128]{2,1,0:T(8,128)S(1)} %get-tuple-element.74.b3, ...), custom_call_target="tpu_custom_call" | custom-call | tf_op jit(solution)/shard_map/pallas_call | solution.py:870
Async XLA Ops:
  1.0 5.6 %collective-permute-start = (f32[7,32,128]{2,1,0:T(8,128)S(1)}, f32[7,32,128]{2,1,0:T(8,128)S(1)}, u32[]{:S(2)}, u32[]{:S(2)}) collective-permute-start(f32[7,32,128]{2,1,0:T(8,128)S(1)} %get-tuple-element.53), channel_id=1, source_target_pairs={{0,64},{64,128},{128,192},{192,0},{1,65},{65,129},{129,193},{193,1... | collective-permute-start | bytes 344072 | tf_op jit(solution)/shard_map/ppermute | solution.py:895
  3.1 3.6 %collective-permute-start.1 = (f32[7,32,128]{2,1,0:T(8,128)S(1)}, f32[7,32,128]{2,1,0:T(8,128)S(1)}, u32[]{:S(2)}, u32[]{:S(2)}) collective-permute-start(f32[7,32,128]{2,1,0:T(8,128)S(1)} %get-tuple-element.54), channel_id=1, source_target_pairs={{0,192},{64,0},{128,64},{192,128},{1,193},{65,1},{129,65},{193,129... | collective-permute-start | bytes 344072 | tf_op jit(solution)/shard_map/ppermute | solution.py:896
  7.4 8.7 %collective-permute-start.2 = (f32[40,8,128]{2,1,0:T(8,128)S(1)}, f32[40,8,128]{2,1,0:T(8,128)S(1)}, u32[]{:S(2)}, u32[]{:S(2)}) collective-permute-start(f32[40,8,128]{2,1,0:T(8,128)S(1)} %get-tuple-element.55), channel_id=1, source_target_pairs={{0,8},{8,16},{16,24},{24,32},{32,40},{40,48},{48,56},{56,0},{1,9},... | collective-permute-start | bytes 491528 | tf_op jit(solution)/shard_map/ppermute | solution.py:895
  9.5 6.7 %collective-permute-start.3 = (f32[40,8,128]{2,1,0:T(8,128)S(1)}, f32[40,8,128]{2,1,0:T(8,128)S(1)}, u32[]{:S(2)}, u32[]{:S(2)}) collective-permute-start(f32[40,8,128]{2,1,0:T(8,128)S(1)} %get-tuple-element.56), channel_id=1, source_target_pairs={{0,56},{8,0},{16,8},{24,16},{32,24},{40,32},{48,40},{56,48},{1,57}... | collective-permute-start | bytes 491528 | tf_op jit(solution)/shard_map/ppermute | solution.py:896
  17.9 5.7 %collective-permute-start.5 = (f32[3,40,128]{2,1,0:T(8,128)S(1)}, f32[3,40,128]{2,1,0:T(8,128)S(1)}, u32[]{:S(2)}, u32[]{:S(2)}) collective-permute-start(f32[3,40,128]{2,1,0:T(8,128)S(1)} %get-tuple-element.63.low), channel_id=1, source_target_pairs={{0,7},{1,0},{2,1},{3,2},{4,3},{5,4},{6,5},{7,6},{8,15},{9,8},{10,9... | collective-permute-start | bytes 184328 | tf_op jit(solution)/shard_map/ppermute | solution.py:896
  20.5 3.1 %collective-permute-start.4 = (f32[3,40,128]{2,1,0:T(8,128)S(1)}, f32[3,40,128]{2,1,0:T(8,128)S(1)}, u32[]{:S(2)}, u32[]{:S(2)}) collective-permute-start(f32[3,40,128]{2,1,0:T(8,128)S(1)} %get-tuple-element.64.high), channel_id=1, source_target_pairs={{0,1},{1,2},{2,3},{3,4},{4,5},{5,6},{6,7},{7,0},{8,9},{9,10},{10,1... | collective-permute-start | bytes 184328 | tf_op jit(solution)/shard_map/ppermute | solution.py:895
  28.3 4.8 %collective-permute-start.6 = (f32[13,16,128]{2,1,0:T(8,128)S(1)}, f32[13,16,128]{2,1,0:T(8,128)S(1)}, u32[]{:S(2)}, u32[]{:S(2)}) collective-permute-start(f32[13,16,128]{2,1,0:T(8,128)S(1)} %get-tuple-element.66), channel_id=1, source_target_pairs={{0,64},{64,128},{128,192},{192,0},{1,65},{65,129},{129,193},{193,1... | collective-permute-start | bytes 319496 | tf_op jit(solution)/shard_map/ppermute | solution.py:895
  29.5 3.6 %collective-permute-start.7 = (f32[13,16,128]{2,1,0:T(8,128)S(1)}, f32[13,16,128]{2,1,0:T(8,128)S(1)}, u32[]{:S(2)}, u32[]{:S(2)}) collective-permute-start(f32[13,16,128]{2,1,0:T(8,128)S(1)} %get-tuple-element.67), channel_id=1, source_target_pairs={{0,192},{64,0},{128,64},{192,128},{1,193},{65,1},{129,65},{193,129... | collective-permute-start | bytes 319496 | tf_op jit(solution)/shard_map/ppermute | solution.py:896
  33.7 7.0 %collective-permute-start.8 = (f32[66,8,128]{2,1,0:T(8,128)S(1)}, f32[66,8,128]{2,1,0:T(8,128)S(1)}, u32[]{:S(2)}, u32[]{:S(2)}) collective-permute-start(f32[66,8,128]{2,1,0:T(8,128)S(1)} %get-tuple-element.69), channel_id=1, source_target_pairs={{0,8},{8,16},{16,24},{24,32},{32,40},{40,48},{48,56},{56,0},{1,9},... | collective-permute-start | bytes 811016 | tf_op jit(solution)/shard_map/ppermute | solution.py:895
  33.8 6.9 %collective-permute-start.9 = (f32[66,8,128]{2,1,0:T(8,128)S(1)}, f32[66,8,128]{2,1,0:T(8,128)S(1)}, u32[]{:S(2)}, u32[]{:S(2)}) collective-permute-start(f32[66,8,128]{2,1,0:T(8,128)S(1)} %get-tuple-element.70), channel_id=1, source_target_pairs={{0,56},{8,0},{16,8},{24,16},{32,24},{40,32},{48,40},{56,48},{1,57}... | collective-permute-start | bytes 811016 | tf_op jit(solution)/shard_map/ppermute | solution.py:896
  41.9 9.0 %collective-permute-start.10 = (f32[11,48,128]{2,1,0:T(8,128)S(1)}, f32[11,48,128]{2,1,0:T(8,128)S(1)}, u32[]{:S(2)}, u32[]{:S(2)}) collective-permute-start(f32[11,48,128]{2,1,0:T(8,128)S(1)} %get-tuple-element.71), channel_id=1, source_target_pairs={{0,1},{1,2},{2,3},{3,4},{4,5},{5,6},{6,7},{7,0},{8,9},{9,10},{10,1... | collective-permute-start | bytes 811016 | tf_op jit(solution)/shard_map/ppermute | solution.py:895
  47.4 5.9 %collective-permute-start.11 = (f32[11,48,128]{2,1,0:T(8,128)S(1)}, f32[11,48,128]{2,1,0:T(8,128)S(1)}, u32[]{:S(2)}, u32[]{:S(2)}) collective-permute-start(f32[11,48,128]{2,1,0:T(8,128)S(1)} %get-tuple-element.72), channel_id=1, source_target_pairs={{0,7},{1,0},{2,1},{3,2},{4,3},{5,4},{6,5},{7,6},{8,15},{9,8},{10,9... | collective-permute-start | bytes 811016 | tf_op jit(solution)/shard_map/ppermute | solution.py:896
  78.8 4.0 %collective-permute-start.13 = (f32[256,128]{1,0:T(8,128)S(1)}, f32[256,128]{1,0:T(8,128)S(1)}, u32[]{:S(2)}, u32[]{:S(2)}) collective-permute-start(f32[256,128]{1,0:T(8,128)S(1)} %bitcast.4), channel_id=1, source_target_pairs={{0,1},{1,2},{2,3},{3,4},{4,5},{5,6},{6,7},{7,0},{8,9},{9,10},{10,1... | collective-permute-start | bytes 393224 | tf_op jit(solution)/shard_map/ppermute | solution.py:941
  80.7 4.7 %collective-permute-start.12 = (f32[256,128]{1,0:T(8,128)S(1)}, f32[256,128]{1,0:T(8,128)S(1)}, u32[]{:S(2)}, u32[]{:S(2)}) collective-permute-start(f32[256,128]{1,0:T(8,128)S(1)} %bitcast.5), channel_id=1, source_target_pairs={{0,7},{1,0},{2,1},{3,2},{4,3},{5,4},{6,5},{7,6},{8,15},{9,8},{10,9... | collective-permute-start | bytes 393224 | tf_op jit(solution)/shard_map/ppermute | solution.py:941

commit v4 on v3

--- a/solution.py
+++ b/solution.py
@@ -214,7 +214,7 @@
     return pltpu.roll(faces[p // 16, here], 124 - 8 * (p % 16), 1)
 
 
-def flux_two(v_ref, wx, wy, wz, faces, p, start, rows):
+def flux_two(v_ref, wx, wy, wz, wm, faces, p, start, rows):
     here = slice(start, start + rows)
     above = slice(start + 1, start + rows + 1)
     below = slice(start - 1, start + rows - 1)
@@ -226,11 +226,11 @@
     fy = wy[p, here] * (v - v_ref[p, above])
     gy = wy[p, below] * (v_ref[p, below] - v)
     fz = jnp.where(lane == 127, through, wz[p, here] * (v - pltpu.roll(v, 127, 1)))
-    gz = jnp.where(lane == 0, through, pltpu.roll(fz, 1, 1))
+    gz = jnp.where(lane == 0, through, wm[p, here] * (pltpu.roll(v, 1, 1) - v))
     return (fx - gx) + (fy - gy) + (fz - gz)
 
 
-def weights_kernel(pos, ek, wx, wy, wz, sums, q):
+def weights_kernel(pos, ek, wx, wy, wz, wm, sums, q):
     here = slice(8, 48)
 
     def invert(p):
@@ -245,7 +245,9 @@
         face_y = rcp(v + q[p, 9:49])
         wx[p, here] = face_x
         wy[p, here] = face_y
-        wz[p, here] = rcp(v + pltpu.roll(v, 127, 1))
+        face_z = rcp(v + pltpu.roll(v, 127, 1))
+        wz[p, here] = face_z
+        wm[p, here] = pltpu.roll(face_z, 1, 1)
         sums[p, here] = rcp(v + q[p - 1, here]) + face_x + face_y + rcp(v + q[p, 7:47])
 
     loop(1, N2 - 1, body, 8)
@@ -262,7 +264,7 @@
 
 
 def down_kernel(
-    pos, eb, ek, wx, wy, wz, sums, low, high, zlo, zhi,
+    pos, eb, ek, wx, wy, wz, wm, sums, low, high, zlo, zhi,
     bk3, low3, high3, inv, f, s, tb, twx, twy, twz, tinv, tx,
     r1, tq, tf, ts, face_w, face_f, face_s, tmp,
 ):
@@ -329,7 +331,7 @@
     def weigh(p):
         through = face_lanes(face_w, p, here)
         face_z = jnp.where(lane == 127, through, wz[p, here])
-        below_z = jnp.where(lane == 0, through, pltpu.roll(face_z, 1, 1))
+        below_z = jnp.where(lane == 0, through, wm[p, here])
         scale = jnp.where(inside_x(p), 1.0, 0.0)
         value = jnp.where(mask * scale > 0.5, rcp(sums[p, here] + face_z + below_z), 0.0)
         inv[p, here] = value
@@ -338,7 +340,7 @@
     loop(1, N2 - 1, weigh, 13)
 
     def smooth(p):
-        rest = eb[p, here] - flux_two(f, wx, wy, wz, face_f, p, 8, R2)
+        rest = eb[p, here] - flux_two(f, wx, wy, wz, wm, face_f, p, 8, R2)
         step = keep_coef * f[p, here] + push_coef * inv[p, here] * rest
         r1[p, here] = rest
         s[p, here] = step
@@ -351,8 +353,8 @@
     def coarsen(i):
         p = 2 * i + 4
         total = r1[p, 12:44] + r1[p + 1, 12:44]
-        total = total - flux_two(s, wx, wy, wz, face_s, p, 12, 32)
-        tmp[0, i, 0:32] = total - flux_two(s, wx, wy, wz, face_s, p + 1, 12, 32)
+        total = total - flux_two(s, wx, wy, wz, wm, face_s, p, 12, 32)
+        tmp[0, i, 0:32] = total - flux_two(s, wx, wy, wz, wm, face_s, p + 1, 12, 32)
         tmp[1, i, 0:32] = ek[p, 12:44] + ek[p + 1, 12:44]
 
     loop(0, 16, coarsen, 4)
@@ -423,7 +425,7 @@
     loop(0, 11, column, 4)
 
 
-def flux_one(v_ref, wx, wy, wz, p, rows):
+def flux_one(v_ref, wx, wy, wz, wm, p, rows):
     here, above, below = slice(8, 8 + rows), slice(9, 9 + rows), slice(7, 7 + rows)
     v = v_ref[p, here]
     fx = wx[p, here] * (v - v_ref[p + 1, here])
@@ -431,13 +433,14 @@
     fy = wy[p, here] * (v - v_ref[p, above])
     gy = wy[p, below] * (v_ref[p, below] - v)
     fz = wz[p, here] * (v - pltpu.roll(v, 127, 1))
-    return (fx - gx) + (fy - gy) + (fz - pltpu.roll(fz, 1, 1))
+    gz = wm[p, here] * (pltpu.roll(v, 1, 1) - v)
+    return (fx - gx) + (fy - gy) + (fz - gz)
 
 
 UNROLL = {48: 10, 24: 9, 32: 8, 16: 8, 8: 4}
 
 
-def weigh_one(q, b, wx, wy, wz, inv, f, rows, low, high, first, last, inside):
+def weigh_one(q, b, wx, wy, wz, wm, inv, f, rows, low, high, first, last, inside):
     here = slice(8, 8 + rows)
     wx[low - 1, here] = rcp(q[low - 1, here] + q[low, here])
 
@@ -453,6 +456,7 @@
         wx[p, here] = face_x
         wy[p, here] = face_y
         wz[p, here] = face_z
+        wm[p, here] = lower_z
         total = below_x + face_x + face_y + below_y + face_z + lower_z
         value = jnp.where(inside(p), rcp(total), 0.0)
         inv[p, here] = value
@@ -461,11 +465,11 @@
     loop(low, high, body, UNROLL[rows])
 
 
-def smooth_one(b, wx, wy, wz, inv, f, r1, s, xs, rows, low, high):
+def smooth_one(b, wx, wy, wz, wm, inv, f, r1, s, xs, rows, low, high):
     here = slice(8, 8 + rows)
 
     def body(p):
-        rest = b[p, here] - flux_one(f, wx, wy, wz, p, rows)
+        rest = b[p, here] - flux_one(f, wx, wy, wz, wm, p, rows)
         step = keep_coef * f[p, here] + push_coef * inv[p, here] * rest
         r1[p, here] = rest
         s[p, here] = step
@@ -475,18 +479,18 @@
     loop(low, high, body, UNROLL[rows])
 
 
-def finish_one(b, wx, wy, wz, inv, xs, f, r0, out, shift, rows, ranges):
+def finish_one(b, wx, wy, wz, wm, inv, xs, f, r0, out, shift, rows, ranges):
     here = slice(8, 8 + rows)
 
     def start(p):
-        rest = b[p, here] - flux_one(xs, wx, wy, wz, p, rows)
+        rest = b[p, here] - flux_one(xs, wx, wy, wz, wm, p, rows)
         r0[p, here] = rest
         f[p, here] = inv[p, here] * rest * inv_center
 
     loop(*ranges[0], start, UNROLL[rows])
 
     def end(p):
-        rest = r0[p, here] - flux_one(f, wx, wy, wz, p, rows)
+        rest = r0[p, here] - flux_one(f, wx, wy, wz, wm, p, rows)
         step = keep_coef * f[p, here] + push_coef * inv[p, here] * rest
         out[p + shift, here] = xs[p, here] + f[p, here] + step
 
@@ -499,7 +503,7 @@
 
 def middle_kernel(
     pos, own, ylo, yhi, zlo, zhi,
-    payload, b3, wx3, wy3, wz3, inv3, f3, s3, b4, wx4, wy4, wz4, inv4, f4, s4,
+    payload, b3, wx3, wy3, wz3, wm3, inv3, f3, s3, b4, wx4, wy4, wz4, wm4, inv4, f4, s4,
     k3, q3, r3, k4, q4, r4, tmp,
 ):
     gx, gy, gz = pos[0], pos[1], pos[2]
@@ -545,8 +549,8 @@
         return (lane == 127) & (gz == 0), (lane == cells - 1) & (gz == DEV[2] - 1)
 
     inside = region(R3, -16, -13, 16, 16, 64)
-    weigh_one(q3, b3, wx3, wy3, wz3, inv3, f3, R3, 1, N3 - 1, *edges(R3, 64), inside)
-    smooth_one(b3, wx3, wy3, wz3, inv3, f3, r3, s3, None, R3, 2, N3 - 2)
+    weigh_one(q3, b3, wx3, wy3, wz3, wm3, inv3, f3, R3, 1, N3 - 1, *edges(R3, 64), inside)
+    smooth_one(b3, wx3, wy3, wz3, wm3, inv3, f3, r3, s3, None, R3, 2, N3 - 2)
 
     def pick(i, j):
         target = signed(j, 64)
@@ -562,8 +566,8 @@
 
     def coarse_b(i):
         p = 2 * i + 1
-        total = r3[p, 8:56] + r3[p + 1, 8:56] - flux_one(s3, wx3, wy3, wz3, p, R3)
-        tmp[1, i, 8:56] = total - flux_one(s3, wx3, wy3, wz3, p + 1, R3)
+        total = r3[p, 8:56] + r3[p + 1, 8:56] - flux_one(s3, wx3, wy3, wz3, wm3, p, R3)
+        tmp[1, i, 8:56] = total - flux_one(s3, wx3, wy3, wz3, wm3, p + 1, R3)
 
     loop(0, N4, coarse_k, 5)
     loop(1, N4 - 1, coarse_b, 3)
@@ -584,8 +588,8 @@
 
     loop(0, N4, invert, 5)
     inside = region(R4, -6, -6, 8, 8, 32)
-    weigh_one(q4, b4, wx4, wy4, wz4, inv4, f4, R4, 1, N4 - 1, *edges(R4, 32), inside)
-    smooth_one(b4, wx4, wy4, wz4, inv4, f4, r4, s4, None, R4, 2, N4 - 2)
+    weigh_one(q4, b4, wx4, wy4, wz4, wm4, inv4, f4, R4, 1, N4 - 1, *edges(R4, 32), inside)
+    smooth_one(b4, wx4, wy4, wz4, wm4, inv4, f4, r4, s4, None, R4, 2, N4 - 2)
 
     cell = lanes_of(4) & 15
     spread = square(lambda i, j: (signed(i, 64) >> 1) == (j & 15), 0.125)
@@ -600,8 +604,8 @@
     parts = [[[None, None], [None, None]] for _ in range(2)]
     for i in range(4):
         p = 2 * i + 6
-        total = r4[p, 8:32] + r4[p + 1, 8:32] - flux_one(s4, wx4, wy4, wz4, p, R4)
-        tmp[0, i, 8:32] = total - flux_one(s4, wx4, wy4, wz4, p + 1, R4)
+        total = r4[p, 8:32] + r4[p + 1, 8:32] - flux_one(s4, wx4, wy4, wz4, wm4, p, R4)
+        tmp[0, i, 8:32] = total - flux_one(s4, wx4, wy4, wz4, wm4, p + 1, R4)
         tmp[1, i, 8:32] = k4[p, 8:32] + k4[p + 1, 8:32]
     for i in range(4):
         mine = slot == (i % 2) * 4 + quad
@@ -635,16 +639,16 @@
 
 
 def up_kernel(
-    pos, own, up, down, b3, wx3, wy3, wz3, inv3, x3, b4, wx4, wy4, wz4, inv4, x4,
-    eb, wx, wy, wz, inv, xs, tb, twx, twy, twz, tinv, tx,
+    pos, own, up, down, b3, wx3, wy3, wz3, wm3, inv3, x3, b4, wx4, wy4, wz4, wm4, inv4, x4,
+    eb, wx, wy, wz, wm, inv, xs, tb, twx, twy, twz, tinv, tx,
     out, *scratch,
 ):
     gx, gy, gz = pos[0], pos[1], pos[2]
-    levels = [scratch[12 * i : 12 * i + 12] for i in range(3)]
-    e5, e6, raw, f4, r4, e4, y4, f3, r3, e3, y3, f2, r2, y2, tf, ty, face_x, face_f, ob, tmp, sems = scratch[36:]
+    levels = [scratch[13 * i : 13 * i + 13] for i in range(3)]
+    e5, e6, raw, f4, r4, e4, y4, f3, r3, e3, y3, f2, r2, y2, tf, ty, face_x, face_f, ob, tmp, sems = scratch[39:]
 
     for level, (nx, ny, nz) in enumerate(WHOLE):
-        b, k, q, wx_, wy_, wz_, inv_, f, r, s, x, r0 = levels[level]
+        b, k, q, wx_, wy_, wz_, wm_, inv_, f, r, s, x, r0 = levels[level]
         for ref in (f, s, x):
             ref[0] = jnp.zeros(ref.shape[1:], F32)
             ref[nx + 1] = jnp.zeros(ref.shape[1:], F32)
@@ -700,7 +704,7 @@
 
     def down(level):
         nx, ny, nz = WHOLE[level]
-        b, k, q, wx_, wy_, wz_, inv_, f, r, s, x, r0 = levels[level]
+        b, k, q, wx_, wy_, wz_, wm_, inv_, f, r, s, x, r0 = levels[level]
         ends(level)
 
         def below(p):
@@ -709,10 +713,10 @@
         loop(1, nx + 1, below, 4)
         z = signed(lanes_of(ny), 72) + gz * (nz // DEV[2])
         weigh_one(
-            q, b, wx_, wy_, wz_, inv_, f, ny, 1, nx + 1, z == -1, z == nz - 1,
+            q, b, wx_, wy_, wz_, wm_, inv_, f, ny, 1, nx + 1, z == -1, z == nz - 1,
             lambda p: (z >= 0) & (z < nz),
         )
-        smooth_one(b, wx_, wy_, wz_, inv_, f, r, s, x, ny, 1, nx + 1)
+        smooth_one(b, wx_, wy_, wz_, wm_, inv_, f, r, s, x, ny, 1, nx + 1)
         if level == 2:
             return
         nb, nk = levels[level + 1][0], levels[level + 1][1]
@@ -727,8 +731,8 @@
         def coarsen(i):
             p = 2 * i - 1
             here = slice(8, 8 + ny)
-            total = r[p, here] + r[p + 1, here] - flux_one(s, wx_, wy_, wz_, p, ny)
-            tmp[0, i, here] = total - flux_one(s, wx_, wy_, wz_, p + 1, ny)
+            total = r[p, here] + r[p + 1, here] - flux_one(s, wx_, wy_, wz_, wm_, p, ny)
+            tmp[0, i, here] = total - flux_one(s, wx_, wy_, wz_, wm_, p + 1, ny)
             tmp[1, i, here] = k[p, here] + k[p + 1, here]
 
         count = ny // 2
@@ -745,7 +749,7 @@
 
     def rise(level, coarse, target, shift):
         nx, ny, nz = WHOLE[level]
-        b, k, q, wx_, wy_, wz_, inv_, f, r, s, x, r0 = levels[level]
+        b, k, q, wx_, wy_, wz_, wm_, inv_, f, r, s, x, r0 = levels[level]
         widen = square(lambda i, j: signed(i, 64) == (signed(j, 64) >> 1), 1.0)
         count = ny // 2
 
@@ -760,9 +764,9 @@
 
         loop(1, nx // 2 + 1, add, 64 // ny)
         span = (1, nx + 1)
-        finish_one(b, wx_, wy_, wz_, inv_, x, f, r0, target, shift, ny, (span, span))
-
-    rise(1, levels[2][10], e6, 0)
+        finish_one(b, wx_, wy_, wz_, wm_, inv_, x, f, r0, target, shift, ny, (span, span))
+
+    rise(1, levels[2][11], e6, 0)
     rise(0, e6, e5, 2)
 
     widen = square(lambda i, j: signed(i, 64) == (signed(j, 64) >> 1), 1.0)
@@ -779,7 +783,7 @@
         y4[2 * i + 1, 8:32] = x4[2 * i + 1, 8:32] + wide
 
     loop(1, 9, add_four, 4)
-    finish_one(b4, wx4, wy4, wz4, inv4, y4, f4, r4, e4, 0, R4, ((3, 17), (4, 16)))
+    finish_one(b4, wx4, wy4, wz4, wm4, inv4, y4, f4, r4, e4, 0, R4, ((3, 17), (4, 16)))
 
     widen3 = square(lambda i, j: signed(i, 64) == (signed(j, 96) >> 1), 1.0)
 
@@ -793,7 +797,7 @@
         y3[2 * i + 2, 8:56] = x3[2 * i + 2, 8:56] + wide
 
     loop(4, 16, add_three, 3)
-    finish_one(b3, wx3, wy3, wz3, inv3, y3, f3, r3, e3, 0, R3, ((11, 31), (12, 30)))
+    finish_one(b3, wx3, wy3, wz3, wm3, inv3, y3, f3, r3, e3, 0, R3, ((11, 31), (12, 30)))
 
     wide = square(lambda i, j: i == (j >> 1), 1.0)
     planes = range(1, 19)
@@ -831,7 +835,7 @@
     loop(1, 19, add_two, 3)
 
     def start(p):
-        rest = eb[p, here] - flux_two(y2, wx, wy, wz, face_x, p, 8, R2)
+        rest = eb[p, here] - flux_two(y2, wx, wy, wz, wm, face_x, p, 8, R2)
         r2[p, here] = rest
         f2[p, here] = inv[p, here] * rest * inv_center
 
@@ -840,7 +844,7 @@
 
     def end(i):
         p = i + 4
-        rest = r2[p, core] - flux_two(f2, wx, wy, wz, face_f, p, 12, 32)
+        rest = r2[p, core] - flux_two(f2, wx, wy, wz, wm, face_f, p, 12, 32)
         first = f2[p, core]
         step = keep_coef * first + push_coef * inv[p, core] * rest
         ob[i] = y2[p, core] + first + step
@@ -909,15 +913,15 @@
         lanes_kernel, (pos, b, k, xlo, xhi, ylo, yhi), [(3, R2, 128)] * 2 + [ext2] * 2
     )
     zlo, zhi = swap(low, high, "gz")
-    wx, wy, wz, sums = call(weights_kernel, (pos, ek), [ext2] * 4, [ext2])
+    wx, wy, wz, wm, sums = call(weights_kernel, (pos, ek), [ext2] * 5, [ext2])
     bk3, low, high, inv, first, second, *rest = call(
         down_kernel,
-        (pos, eb, ek, wx, wy, wz, sums, low, high, zlo, zhi),
+        (pos, eb, ek, wx, wy, wz, wm, sums, low, high, zlo, zhi),
         [(16, 16, 128)] + [(13, 16, 128)] * 2 + [ext2] * 3 + [strip] * 6,
         [ext2] + [strip] * 3 + [face] * 3 + [(2, 16, 32, 128)],
     )
     (xs,) = call(add_kernel, (pos, first, second), [ext2])
-    state2 = [eb, wx, wy, wz, inv, xs, *rest]
+    state2 = [eb, wx, wy, wz, wm, inv, xs, *rest]
     xlo, xhi = swap(low, high, "gx")
     own, low, high = call(
         planes_kernel, (pos, bk3, xlo, xhi), [(N3, 16, 128)] + [(N3 + 24, 8, 128)] * 2
@@ -929,12 +933,12 @@
     payload, *state = call(
         middle_kernel,
         (pos, own, ylo, yhi, zlo, zhi),
-        [(32, 8, 128)] + [three] * 7 + [four] * 7,
+        [(32, 8, 128)] + [three] * 8 + [four] * 8,
         [three] * 3 + [four] * 3 + [(2, N4, T3, 128)],
     )
-    (x3,) = call(add_kernel, (pos, *state[5:7]), [three])
-    (x4,) = call(add_kernel, (pos, *state[12:14]), [four])
-    state = [*state[:5], x3, *state[7:12], x4]
+    (x3,) = call(add_kernel, (pos, *state[6:8]), [three])
+    (x4,) = call(add_kernel, (pos, *state[14:16]), [four])
+    state = [*state[:6], x3, *state[8:14], x4]
     recv = lax.all_to_all(payload, AXES[:2], 0, 0, tiled=True).reshape(256, 128)
     ring = range(DEV[2])
     recv = [recv] + [
@@ -943,7 +947,7 @@
     recv = [vmem(part) for part in recv]
     scratch = []
     for nx, ny, _ in WHOLE:
-        scratch += [(nx + 2, ny + 16, 128)] * 12
+        scratch += [(nx + 2, ny + 16, 128)] * 13
     scratch += [(22, 56, 128), (10, 32, 128), (1024, 128)]
     scratch += [four] * 4 + [three] * 4 + [ext2] * 3 + [strip] * 2 + [face] * 2 + [(32, 32, 128)]
     scratch += [(2, 20, T3, 128)]

time: 99.5 us -> 96.4 us (0.969)
  Pallas kernels: 36.3 us -> 33.6 us
    pallas_call x11, Pallas kernels: 34 us -> 31.2 us  [call(): pl.pallas_call(kernel, out_shape=[out_type(shape, F32) for shape in outs]...]
  transfers between devices with their start and end apart: 14 -> 14, of which waited for: 9 -> 8; matrix products, arithmetic and copies ran while one was open for 0% -> 0% of each run, Pallas kernels for 5% -> 5%
where the time goes in v4:
time: 96.4 us; the launch traced here: 96.1 us
  Pallas kernels  33.6 us (35%)
  starting transfers between devices  27 us (28%)
  waiting for transfers between devices  17.7 us (18%)
  blocking collectives  17.4 us (18%)
    pallas_call x11, Pallas kernels, call(): pl.pallas_call(kernel, out_shape=[out_type(shape, F32) for shape in outs]...  31.2 us
    all_to_all x1, blocking collectives, shards(): recv = lax.all_to_all(payload, AXES[:2], 0, 0, tiled=True).reshape(256, 128)  17.4 us
    ppermute x6, starting transfers between devices, swap(): after = lax.ppermute(low, axis, [(i, (i - 1) % count) for i in ring])  12.7 us
    ppermute x6, waiting for transfers between devices, swap(): before = lax.ppermute(high, axis, [(i, (i + 1) % count) for i in ring])  12.4 us
    ppermute x6, starting transfers between devices, swap(): before = lax.ppermute(high, axis, [(i, (i + 1) % count) for i in ring])  12.2 us
    ppermute x6, waiting for transfers between devices, swap(): after = lax.ppermute(low, axis, [(i, (i - 1) % count) for i in ring])  2.68 us
    ppermute x2, waiting for transfers between devices, shards(): lax.ppermute(recv, 'gz', [(i, (i - d) % DEV[2]) for i in ring])  2.62 us
    pallas_call x2, Pallas kernels, load(): pl.pallas_call(kernel, out_shape=[pltpu.VMEM(shape, F32)] * 2, in_specs=[...  2.31 us
  transfers between devices with their start and end apart: 14, of which 8 were waited for; matrix products, arithmetic and copies ran while one was open for 0% of the time, Pallas kernels for 5%

profile of v4, /device:TPU:1, one launch (start us, length us, event | category | flops | bytes accessed | tf_op | source)
XLA Modules:
  0.0 96.1 jit_solution(8277394479259342118)
XLA Ops:
  0.0 1.0 shard_map.29
  1.0 2.1 %collective-permute-start = (f32[7,32,128]{2,1,0:T(8,128)S(1)}, f32[7,32,128]{2,1,0:T(8,128)S(1)}, u32[]{:S(2)}, u32[]{:S(2)}) collective-permute-start(f32[7,32,128]{2,1,0:T(8,128)S(1)} %get-tuple-element.56), channel_id=1, source_target_pairs={{0,64},{64,128},{128,192},{192,0},{1,65},{65,129},{129,193},{193,1... | collective-permute-start | bytes 344072 | tf_op jit(solution)/shard_map/ppermute | solution.py:899
  3.1 1.4 %collective-permute-start.1 = (f32[7,32,128]{2,1,0:T(8,128)S(1)}, f32[7,32,128]{2,1,0:T(8,128)S(1)}, u32[]{:S(2)}, u32[]{:S(2)}) collective-permute-start(f32[7,32,128]{2,1,0:T(8,128)S(1)} %get-tuple-element.57), channel_id=1, source_target_pairs={{0,192},{64,0},{128,64},{192,128},{1,193},{65,1},{129,65},{193,129... | collective-permute-start | bytes 344072 | tf_op jit(solution)/shard_map/ppermute | solution.py:900
  4.4 1.3 %shard_map.28 = (f32[32,32,128]{2,1,0:T(8,128)S(1)}, f32[32,32,128]{2,1,0:T(8,128)S(1)}) custom-call(f32[32,32,128]{2,1,0:T(8,128)} %b.3, f32[32,32,128]{2,1,0:T(8,128)} %k.3), custom_call_target="tpu_custom_call" | custom-call | tf_op jit(solution)/shard_map/pallas_call | solution.py:887
  5.8 0.1 pad_add_fusion.pos
  5.9 0.7 collective-permute-done.xlo
  6.5 0.2 collective-permute-done.1.xhi
  6.7 0.6 shard_map.30
  7.4 2.1 %collective-permute-start.2 = (f32[40,8,128]{2,1,0:T(8,128)S(1)}, f32[40,8,128]{2,1,0:T(8,128)S(1)}, u32[]{:S(2)}, u32[]{:S(2)}) collective-permute-start(f32[40,8,128]{2,1,0:T(8,128)S(1)} %get-tuple-element.58), channel_id=1, source_target_pairs={{0,8},{8,16},{16,24},{24,32},{32,40},{40,48},{48,56},{56,0},{1,9},... | collective-permute-start | bytes 491528 | tf_op jit(solution)/shard_map/ppermute | solution.py:899
  9.5 4.0 %collective-permute-start.3 = (f32[40,8,128]{2,1,0:T(8,128)S(1)}, f32[40,8,128]{2,1,0:T(8,128)S(1)}, u32[]{:S(2)}, u32[]{:S(2)}) collective-permute-start(f32[40,8,128]{2,1,0:T(8,128)S(1)} %get-tuple-element.59), channel_id=1, source_target_pairs={{0,56},{8,0},{16,8},{24,16},{32,24},{40,32},{48,40},{56,48},{1,57}... | collective-permute-start | bytes 491528 | tf_op jit(solution)/shard_map/ppermute | solution.py:900
  13.5 2.6 %collective-permute-done.2.ylo = f32[40,8,128]{2,1,0:T(8,128)S(1)} collective-permute-done((f32[40,8,128]{2,1,0:T(8,128)S(1)}, f32[40,8,128]{2,1,0:T(8,128)S(1)}, u32[]{:S(2)}, u32[]{:S(2)}) %collective-permute-start.2) | collective-permute-done | bytes 163872 | tf_op jit(solution)/shard_map/ppermute | solution.py:899
  16.1 0.0 collective-permute-done.3.yhi
  16.1 1.8 %shard_map.31 = (f32[3,40,128]{2,1,0:T(8,128)S(1)}, f32[3,40,128]{2,1,0:T(8,128)S(1)}, f32[40,56,128]{2,1,0:T(8,128)S(1)}, f32[40,56,128]{2,1,0:T(8,128)S(1)}) custom-call(s32[3]{0:T(128)S(1)} %pad_add_fusion.pos, f32[32,32,128]{2,1,0:T(8,128)S(1)} %get-tuple-element.54.b, f32[32,32,128]{2,1,0:T(8,128)S(1)} %get-tuple-element.55.k, ...), custom_call_target="tpu_custom_call" | custom-call | tf_op jit(solution)/shard_map/pallas_call | solution.py:874
  17.9 2.6 %collective-permute-start.5 = (f32[3,40,128]{2,1,0:T(8,128)S(1)}, f32[3,40,128]{2,1,0:T(8,128)S(1)}, u32[]{:S(2)}, u32[]{:S(2)}) collective-permute-start(f32[3,40,128]{2,1,0:T(8,128)S(1)} %get-tuple-element.67.low), channel_id=1, source_target_pairs={{0,7},{1,0},{2,1},{3,2},{4,3},{5,4},{6,5},{7,6},{8,15},{9,8},{10,9... | collective-permute-start | bytes 184328 | tf_op jit(solution)/shard_map/ppermute | solution.py:900
  20.5 1.2 %collective-permute-start.4 = (f32[3,40,128]{2,1,0:T(8,128)S(1)}, f32[3,40,128]{2,1,0:T(8,128)S(1)}, u32[]{:S(2)}, u32[]{:S(2)}) collective-permute-start(f32[3,40,128]{2,1,0:T(8,128)S(1)} %get-tuple-element.68.high), channel_id=1, source_target_pairs={{0,1},{1,2},{2,3},{3,4},{4,5},{5,6},{6,7},{7,0},{8,9},{9,10},{10,1... | collective-permute-start | bytes 184328 | tf_op jit(solution)/shard_map/ppermute | solution.py:899
  21.7 2.0 %shard_map.32 = (f32[40,56,128]{2,1,0:T(8,128)S(1)}, f32[40,56,128]{2,1,0:T(8,128)S(1)}, f32[40,56,128]{2,1,0:T(8,128)S(1)}, f32[40,56,128]{2,1,0:T(8,128)S(1)}, f32[40,56,128]{2,1,0:T(8,128)S(1)}) custom-call(s32[3]{0:T(128)S(1)} %pad_add_fusion.pos, f32[40,56,128]{2,1,0:T(8,128)S(1)} %get-tuple-element.61.ek), custom_call_target="tpu_custom_call" | custom-call | tf_op jit(solution)/shard_map/pallas_call | solution.py:874
  23.7 0.0 collective-permute-done.5.zhi
  23.7 0.0 collective-permute-done.4.zlo
  23.7 4.1 %shard_map.33 = (f32[16,16,128]{2,1,0:T(8,128)S(1)}, f32[13,16,128]{2,1,0:T(8,128)S(1)}, f32[13,16,128]{2,1,0:T(8,128)S(1)}, f32[40,56,128]{2,1,0:T(8,128)S(1)},...) custom-call(s32[3]{0:T(128)S(1)} %pad_add_fusion.pos, ...), custom_call_target="tpu_custom_call" | custom-call | tf_op jit(solution)/shard_map/pallas_call | solution.py:874
  27.9 1.3 %collective-permute-start.6 = (f32[13,16,128]{2,1,0:T(8,128)S(1)}, f32[13,16,128]{2,1,0:T(8,128)S(1)}, u32[]{:S(2)}, u32[]{:S(2)}) collective-permute-start(f32[13,16,128]{2,1,0:T(8,128)S(1)} %get-tuple-element.70), channel_id=1, source_target_pairs={{0,64},{64,128},{128,192},{192,0},{1,65},{65,129},{129,193},{193,1... | collective-permute-start | bytes 319496 | tf_op jit(solution)/shard_map/ppermute | solution.py:899
  29.2 1.6 %collective-permute-start.7 = (f32[13,16,128]{2,1,0:T(8,128)S(1)}, f32[13,16,128]{2,1,0:T(8,128)S(1)}, u32[]{:S(2)}, u32[]{:S(2)}) collective-permute-start(f32[13,16,128]{2,1,0:T(8,128)S(1)} %get-tuple-element.71), channel_id=1, source_target_pairs={{0,192},{64,0},{128,64},{192,128},{1,193},{65,1},{129,65},{193,129... | collective-permute-start | bytes 319496 | tf_op jit(solution)/shard_map/ppermute | solution.py:900
  30.7 2.0 %collective-permute-done.6.xlo = f32[13,16,128]{2,1,0:T(8,128)S(1)} collective-permute-done((f32[13,16,128]{2,1,0:T(8,128)S(1)}, f32[13,16,128]{2,1,0:T(8,128)S(1)}, u32[]{:S(2)}, u32[]{:S(2)}) %collective-permute-start.6) | collective-permute-done | bytes 106528 | tf_op jit(solution)/shard_map/ppermute | solution.py:899
  32.7 0.0 collective-permute-done.7.xhi
  32.7 0.6 shard_map.34
  33.3 0.1 collective-permute-start.8
  33.4 3.1 %collective-permute-start.9 = (f32[66,8,128]{2,1,0:T(8,128)S(1)}, f32[66,8,128]{2,1,0:T(8,128)S(1)}, u32[]{:S(2)}, u32[]{:S(2)}) collective-permute-start(f32[66,8,128]{2,1,0:T(8,128)S(1)} %get-tuple-element.74), channel_id=1, source_target_pairs={{0,56},{8,0},{16,8},{24,16},{32,24},{40,32},{48,40},{56,48},{1,57}... | collective-permute-start | bytes 811016 | tf_op jit(solution)/shard_map/ppermute | solution.py:900
  36.5 3.8 %collective-permute-done.8.ylo = f32[66,8,128]{2,1,0:T(8,128)S(1)} collective-permute-done((f32[66,8,128]{2,1,0:T(8,128)S(1)}, f32[66,8,128]{2,1,0:T(8,128)S(1)}, u32[]{:S(2)}, u32[]{:S(2)}) %collective-permute-start.8) | collective-permute-done | bytes 270368 | tf_op jit(solution)/shard_map/ppermute | solution.py:899
  40.3 0.0 collective-permute-done.9.yhi
  40.3 1.2 %shard_map.35 = (f32[11,48,128]{2,1,0:T(8,128)S(1)}, f32[11,48,128]{2,1,0:T(8,128)S(1)}) custom-call(s32[3]{0:T(128)S(1)} %pad_add_fusion.pos, f32[42,16,128]{2,1,0:T(8,128)S(1)} %get-tuple-element.72.own, f32[66,8,128]{2,1,0:T(8,128)S(1)} %collective-permute-done.8.ylo, f32[66,8,128]{2,1,0:T(8,128)S(1)} %collective-permute-done.9.yhi), custom_call_target="tpu_custom_call" | custom-call | tf_op jit(solution)/shard_map/pallas_call | solution.py:874
  41.5 5.5 %collective-permute-start.10 = (f32[11,48,128]{2,1,0:T(8,128)S(1)}, f32[11,48,128]{2,1,0:T(8,128)S(1)}, u32[]{:S(2)}, u32[]{:S(2)}) collective-permute-start(f32[11,48,128]{2,1,0:T(8,128)S(1)} %get-tuple-element.75), channel_id=1, source_target_pairs={{0,1},{1,2},{2,3},{3,4},{4,5},{5,6},{6,7},{7,0},{8,9},{9,10},{10,1... | collective-permute-start | bytes 811016 | tf_op jit(solution)/shard_map/ppermute | solution.py:899
  46.9 0.0 collective-permute-start.11
  46.9 3.4 %collective-permute-done.10.zlo = f32[11,48,128]{2,1,0:T(8,128)S(1)} collective-permute-done((f32[11,48,128]{2,1,0:T(8,128)S(1)}, f32[11,48,128]{2,1,0:T(8,128)S(1)}, u32[]{:S(2)}, u32[]{:S(2)}) %collective-permute-start.10) | collective-permute-done | bytes 270368 | tf_op jit(solution)/shard_map/ppermute | solution.py:899
  50.3 2.5 %collective-permute-done.11.zhi = f32[11,48,128]{2,1,0:T(8,128)S(1)} collective-permute-done((f32[11,48,128]{2,1,0:T(8,128)S(1)}, f32[11,48,128]{2,1,0:T(8,128)S(1)}, u32[]{:S(2)}, u32[]{:S(2)}) %collective-permute-start.11) | collective-permute-done | bytes 270368 | tf_op jit(solution)/shard_map/ppermute | solution.py:900
  52.8 7.7 %shard_map.36 = (f32[32,8,128]{2,1,0:T(8,128)S(1)}, f32[42,64,128]{2,1,0:T(8,128)S(1)}, f32[42,64,128]{2,1,0:T(8,128)S(1)}, f32[42,64,128]{2,1,0:T(8,128)S(1)}, ...) custom-call(s32[3]{0:T(128)S(1)} %pad_add_fusion.pos, ...), custom_call_target="tpu_custom_call" | custom-call | tf_op jit(solution)/shard_map/pallas_call | solution.py:874
  60.6 17.4 %all_to_all.5 = f32[32,8,128]{2,1,0:T(8,128)S(1)} all-to-all(f32[32,8,128]{2,1,0:T(8,128)S(1)} %get-tuple-element.77), channel_id=1, replica_groups=mesh['gx'=4,'gy'=8,'gz'=8] {'gx','gy'}, dimensions={0} | all-to-all | bytes 262144 | tf_op jit(solution)/shard_map/all_to_all | solution.py:942
  78.0 1.9 %collective-permute-start.13 = (f32[256,128]{1,0:T(8,128)S(1)}, f32[256,128]{1,0:T(8,128)S(1)}, u32[]{:S(2)}, u32[]{:S(2)}) collective-permute-start(f32[256,128]{1,0:T(8,128)S(1)} %bitcast.4), channel_id=1, source_target_pairs={{0,1},{1,2},{2,3},{3,4},{4,5},{5,6},{6,7},{7,0},{8,9},{9,10},{10,1... | collective-permute-start | bytes 393224 | tf_op jit(solution)/shard_map/ppermute | solution.py:945
  79.9 0.2 collective-permute-start.12
  80.1 0.6 shard_map.39.xs
  80.8 0.6 shard_map.38.x4
  81.3 0.7 shard_map.37.x3
  82.0 0.0 collective-permute-done.13.down
  82.0 2.6 %collective-permute-done.12.up = f32[256,128]{1,0:T(8,128)S(1)} collective-permute-done((f32[256,128]{1,0:T(8,128)S(1)}, f32[256,128]{1,0:T(8,128)S(1)}, u32[]{:S(2)}, u32[]{:S(2)}) %collective-permute-start.12) | collective-permute-done | bytes 131104 | tf_op jit(solution)/shard_map/ppermute | solution.py:945
  84.6 11.3 %shard_map.40 = f32[32,32,128]{2,1,0:T(8,128)} custom-call(s32[3]{0:T(128)S(1)} %pad_add_fusion.pos, f32[256,128]{1,0:T(8,128)S(1)} %bitcast.6, f32[256,128]{1,0:T(8,128)S(1)} %collective-permute-done.12.up, f32[256,128]{1,0:T(8,128)S(1)} %collective-permute-done.13.down, f32[42,64,128]{2,1,0:T(8,128)S(1)} %get-tuple-element.78.b3, ...), custom_call_target="tpu_custom_call" | custom-call | tf_op jit(solution)/shard_map/pallas_call | solution.py:874
Async XLA Ops:
  1.0 5.6 %collective-permute-start = (f32[7,32,128]{2,1,0:T(8,128)S(1)}, f32[7,32,128]{2,1,0:T(8,128)S(1)}, u32[]{:S(2)}, u32[]{:S(2)}) collective-permute-start(f32[7,32,128]{2,1,0:T(8,128)S(1)} %get-tuple-element.56), channel_id=1, source_target_pairs={{0,64},{64,128},{128,192},{192,0},{1,65},{65,129},{129,193},{193,1... | collective-permute-start | bytes 344072 | tf_op jit(solution)/shard_map/ppermute | solution.py:899
  3.1 3.6 %collective-permute-start.1 = (f32[7,32,128]{2,1,0:T(8,128)S(1)}, f32[7,32,128]{2,1,0:T(8,128)S(1)}, u32[]{:S(2)}, u32[]{:S(2)}) collective-permute-start(f32[7,32,128]{2,1,0:T(8,128)S(1)} %get-tuple-element.57), channel_id=1, source_target_pairs={{0,192},{64,0},{128,64},{192,128},{1,193},{65,1},{129,65},{193,129... | collective-permute-start | bytes 344072 | tf_op jit(solution)/shard_map/ppermute | solution.py:900
  7.4 8.7 %collective-permute-start.2 = (f32[40,8,128]{2,1,0:T(8,128)S(1)}, f32[40,8,128]{2,1,0:T(8,128)S(1)}, u32[]{:S(2)}, u32[]{:S(2)}) collective-permute-start(f32[40,8,128]{2,1,0:T(8,128)S(1)} %get-tuple-element.58), channel_id=1, source_target_pairs={{0,8},{8,16},{16,24},{24,32},{32,40},{40,48},{48,56},{56,0},{1,9},... | collective-permute-start | bytes 491528 | tf_op jit(solution)/shard_map/ppermute | solution.py:899
  9.5 6.7 %collective-permute-start.3 = (f32[40,8,128]{2,1,0:T(8,128)S(1)}, f32[40,8,128]{2,1,0:T(8,128)S(1)}, u32[]{:S(2)}, u32[]{:S(2)}) collective-permute-start(f32[40,8,128]{2,1,0:T(8,128)S(1)} %get-tuple-element.59), channel_id=1, source_target_pairs={{0,56},{8,0},{16,8},{24,16},{32,24},{40,32},{48,40},{56,48},{1,57}... | collective-permute-start | bytes 491528 | tf_op jit(solution)/shard_map/ppermute | solution.py:900
  17.9 5.8 %collective-permute-start.5 = (f32[3,40,128]{2,1,0:T(8,128)S(1)}, f32[3,40,128]{2,1,0:T(8,128)S(1)}, u32[]{:S(2)}, u32[]{:S(2)}) collective-permute-start(f32[3,40,128]{2,1,0:T(8,128)S(1)} %get-tuple-element.67.low), channel_id=1, source_target_pairs={{0,7},{1,0},{2,1},{3,2},{4,3},{5,4},{6,5},{7,6},{8,15},{9,8},{10,9... | collective-permute-start | bytes 184328 | tf_op jit(solution)/shard_map/ppermute | solution.py:900
  20.5 3.2 %collective-permute-start.4 = (f32[3,40,128]{2,1,0:T(8,128)S(1)}, f32[3,40,128]{2,1,0:T(8,128)S(1)}, u32[]{:S(2)}, u32[]{:S(2)}) collective-permute-start(f32[3,40,128]{2,1,0:T(8,128)S(1)} %get-tuple-element.68.high), channel_id=1, source_target_pairs={{0,1},{1,2},{2,3},{3,4},{4,5},{5,6},{6,7},{7,0},{8,9},{9,10},{10,1... | collective-permute-start | bytes 184328 | tf_op jit(solution)/shard_map/ppermute | solution.py:899
  27.9 4.8 %collective-permute-start.6 = (f32[13,16,128]{2,1,0:T(8,128)S(1)}, f32[13,16,128]{2,1,0:T(8,128)S(1)}, u32[]{:S(2)}, u32[]{:S(2)}) collective-permute-start(f32[13,16,128]{2,1,0:T(8,128)S(1)} %get-tuple-element.70), channel_id=1, source_target_pairs={{0,64},{64,128},{128,192},{192,0},{1,65},{65,129},{129,193},{193,1... | collective-permute-start | bytes 319496 | tf_op jit(solution)/shard_map/ppermute | solution.py:899
  29.2 3.6 %collective-permute-start.7 = (f32[13,16,128]{2,1,0:T(8,128)S(1)}, f32[13,16,128]{2,1,0:T(8,128)S(1)}, u32[]{:S(2)}, u32[]{:S(2)}) collective-permute-start(f32[13,16,128]{2,1,0:T(8,128)S(1)} %get-tuple-element.71), channel_id=1, source_target_pairs={{0,192},{64,0},{128,64},{192,128},{1,193},{65,1},{129,65},{193,129... | collective-permute-start | bytes 319496 | tf_op jit(solution)/shard_map/ppermute | solution.py:900
  33.3 7.0 %collective-permute-start.8 = (f32[66,8,128]{2,1,0:T(8,128)S(1)}, f32[66,8,128]{2,1,0:T(8,128)S(1)}, u32[]{:S(2)}, u32[]{:S(2)}) collective-permute-start(f32[66,8,128]{2,1,0:T(8,128)S(1)} %get-tuple-element.73), channel_id=1, source_target_pairs={{0,8},{8,16},{16,24},{24,32},{32,40},{40,48},{48,56},{56,0},{1,9},... | collective-permute-start | bytes 811016 | tf_op jit(solution)/shard_map/ppermute | solution.py:899
  33.4 6.9 %collective-permute-start.9 = (f32[66,8,128]{2,1,0:T(8,128)S(1)}, f32[66,8,128]{2,1,0:T(8,128)S(1)}, u32[]{:S(2)}, u32[]{:S(2)}) collective-permute-start(f32[66,8,128]{2,1,0:T(8,128)S(1)} %get-tuple-element.74), channel_id=1, source_target_pairs={{0,56},{8,0},{16,8},{24,16},{32,24},{40,32},{48,40},{56,48},{1,57}... | collective-permute-start | bytes 811016 | tf_op jit(solution)/shard_map/ppermute | solution.py:900
  41.5 8.9 %collective-permute-start.10 = (f32[11,48,128]{2,1,0:T(8,128)S(1)}, f32[11,48,128]{2,1,0:T(8,128)S(1)}, u32[]{:S(2)}, u32[]{:S(2)}) collective-permute-start(f32[11,48,128]{2,1,0:T(8,128)S(1)} %get-tuple-element.75), channel_id=1, source_target_pairs={{0,1},{1,2},{2,3},{3,4},{4,5},{5,6},{6,7},{7,0},{8,9},{9,10},{10,1... | collective-permute-start | bytes 811016 | tf_op jit(solution)/shard_map/ppermute | solution.py:899
  46.9 5.9 %collective-permute-start.11 = (f32[11,48,128]{2,1,0:T(8,128)S(1)}, f32[11,48,128]{2,1,0:T(8,128)S(1)}, u32[]{:S(2)}, u32[]{:S(2)}) collective-permute-start(f32[11,48,128]{2,1,0:T(8,128)S(1)} %get-tuple-element.76), channel_id=1, source_target_pairs={{0,7},{1,0},{2,1},{3,2},{4,3},{5,4},{6,5},{7,6},{8,15},{9,8},{10,9... | collective-permute-start | bytes 811016 | tf_op jit(solution)/shard_map/ppermute | solution.py:900
  78.0 4.0 %collective-permute-start.13 = (f32[256,128]{1,0:T(8,128)S(1)}, f32[256,128]{1,0:T(8,128)S(1)}, u32[]{:S(2)}, u32[]{:S(2)}) collective-permute-start(f32[256,128]{1,0:T(8,128)S(1)} %bitcast.4), channel_id=1, source_target_pairs={{0,1},{1,2},{2,3},{3,4},{4,5},{5,6},{6,7},{7,0},{8,9},{9,10},{10,1... | collective-permute-start | bytes 393224 | tf_op jit(solution)/shard_map/ppermute | solution.py:945
  79.9 4.7 %collective-permute-start.12 = (f32[256,128]{1,0:T(8,128)S(1)}, f32[256,128]{1,0:T(8,128)S(1)}, u32[]{:S(2)}, u32[]{:S(2)}) collective-permute-start(f32[256,128]{1,0:T(8,128)S(1)} %bitcast.5), channel_id=1, source_target_pairs={{0,7},{1,0},{2,1},{3,2},{4,3},{5,4},{6,5},{7,6},{8,15},{9,8},{10,9... | collective-permute-start | bytes 393224 | tf_op jit(solution)/shard_map/ppermute | solution.py:945

commit v5 on v4

--- a/solution.py
+++ b/solution.py
@@ -194,16 +194,18 @@
     result, through = [], []
     for t in range(2):
         v = [v_ref[t, c, here] for c in range(3)]
-        ahead = next_plane(v)
-        fx = [wx[t, c, here] * (v[c] - ahead[c]) for c in range(3)]
-        gx = last_plane(fx)
+        ahead, behind = next_plane(v), last_plane(v)
+        lower = last_plane([wx[t, c, here] for c in range(3)])
         total = []
         for c in range(3):
+            fx = wx[t, c, here] * (v[c] - ahead[c])
+            gx = lower[c] * (behind[c] - v[c])
             fy = wy[t, c, here] * (v[c] - v_ref[t, c, above])
             gy = wy[t, c, below] * (v_ref[t, c, below] - v[c])
             fz = wz[t, c, here] * (v[c] - pltpu.roll(v[c], 127, 1))
+            gz = pltpu.roll(wz[t, c, here], 1, 1) * (pltpu.roll(v[c], 1, 1) - v[c])
             through.append(fz)
-            total.append((fx[c] - gx[c]) + (fy - gy) + (fz - pltpu.roll(fz, 1, 1)))
+            total.append((fx - gx) + (fy - gy) + (fz - gz))
         result.append(total)
     for c in range(3):
         faces[c, here] = merge_faces(through[c], through[3 + c])
@@ -377,9 +379,9 @@
         out[p] = value
         low[p] = value[0:8]
         high[p] = value[8:16]
-        if 9 <= p < 33:
-            low[p + 33] = value[8:16]
-            high[p + 33] = value[0:8]
+        if 7 <= p < 35:
+            low[p + 35] = value[8:16]
+            high[p + 35] = value[0:8]
 
     for j in range(13):
         lo, hi = xlo[j], xhi[j]
@@ -397,7 +399,7 @@
     gy = pos[1]
     right = lanes_of(16) >= 64
     row = rows_of(16)
-    far = jnp.where((p >= 9) & (p < 33), p + 33, p)
+    far = jnp.where((p >= 7) & (p < 35), p + 35, p)
     lo = jnp.concatenate([ylo[far], ylo[p]], axis=0)
     hi = jnp.concatenate([yhi[p], yhi[far]], axis=0)
     lo = jnp.where(right & (row == 15) & (gy == 0), own[p, 0:1], lo)
@@ -924,7 +926,7 @@
     state2 = [eb, wx, wy, wz, wm, inv, xs, *rest]
     xlo, xhi = swap(low, high, "gx")
     own, low, high = call(
-        planes_kernel, (pos, bk3, xlo, xhi), [(N3, 16, 128)] + [(N3 + 24, 8, 128)] * 2
+        planes_kernel, (pos, bk3, xlo, xhi), [(N3, 16, 128)] + [(N3 + 28, 8, 128)] * 2
     )
     ylo, yhi = swap(low, high, "gy")
     low, high = call(slots_kernel, (pos, own, ylo, yhi), [(11, 48, 128)] * 2)

time: 96.4 us -> 96.8 us (level)
  no operation moved by 1% of the time
where the time goes in v5:
time: 96.8 us; the launch traced here: 96.6 us
  Pallas kernels  33.7 us (35%)
  starting transfers between devices  27.2 us (28%)
  waiting for transfers between devices  17.9 us (18%)
  blocking collectives  17.4 us (18%)
    pallas_call x11, Pallas kernels, call(): pl.pallas_call(kernel, out_shape=[out_type(shape, F32) for shape in outs]...  31.4 us
    all_to_all x1, blocking collectives, shards(): recv = lax.all_to_all(payload, AXES[:2], 0, 0, tiled=True).reshape(256, 128)  17.4 us
    ppermute x6, starting transfers between devices, swap(): after = lax.ppermute(low, axis, [(i, (i - 1) % count) for i in ring])  12.7 us
    ppermute x6, waiting for transfers between devices, swap(): before = lax.ppermute(high, axis, [(i, (i + 1) % count) for i in ring])  12.6 us
    ppermute x6, starting transfers between devices, swap(): before = lax.ppermute(high, axis, [(i, (i + 1) % count) for i in ring])  12.4 us
    ppermute x6, waiting for transfers between devices, swap(): after = lax.ppermute(low, axis, [(i, (i - 1) % count) for i in ring])  2.68 us
    ppermute x2, waiting for transfers between devices, shards(): lax.ppermute(recv, 'gz', [(i, (i - d) % DEV[2]) for i in ring])  2.64 us
    pallas_call x2, Pallas kernels, load(): pl.pallas_call(kernel, out_shape=[pltpu.VMEM(shape, F32)] * 2, in_specs=[...  2.31 us
  transfers between devices with their start and end apart: 14, of which 8 were waited for; matrix products, arithmetic and copies ran while one was open for 0% of the time, Pallas kernels for 5%

profile of v5, /device:TPU:1, one launch (start us, length us, event | category | flops | bytes accessed | tf_op | source)
XLA Modules:
  0.0 96.6 jit_solution(1458493608909845904)
XLA Ops:
  0.0 1.0 shard_map.29
  1.0 2.1 %collective-permute-start = (f32[7,32,128]{2,1,0:T(8,128)S(1)}, f32[7,32,128]{2,1,0:T(8,128)S(1)}, u32[]{:S(2)}, u32[]{:S(2)}) collective-permute-start(f32[7,32,128]{2,1,0:T(8,128)S(1)} %get-tuple-element.56), channel_id=1, source_target_pairs={{0,64},{64,128},{128,192},{192,0},{1,65},{65,129},{129,193},{193,1... | collective-permute-start | bytes 344072 | tf_op jit(solution)/shard_map/ppermute | solution.py:901
  3.1 1.4 %collective-permute-start.1 = (f32[7,32,128]{2,1,0:T(8,128)S(1)}, f32[7,32,128]{2,1,0:T(8,128)S(1)}, u32[]{:S(2)}, u32[]{:S(2)}) collective-permute-start(f32[7,32,128]{2,1,0:T(8,128)S(1)} %get-tuple-element.57), channel_id=1, source_target_pairs={{0,192},{64,0},{128,64},{192,128},{1,193},{65,1},{129,65},{193,129... | collective-permute-start | bytes 344072 | tf_op jit(solution)/shard_map/ppermute | solution.py:902
  4.4 1.3 %shard_map.28 = (f32[32,32,128]{2,1,0:T(8,128)S(1)}, f32[32,32,128]{2,1,0:T(8,128)S(1)}) custom-call(f32[32,32,128]{2,1,0:T(8,128)} %b.3, f32[32,32,128]{2,1,0:T(8,128)} %k.3), custom_call_target="tpu_custom_call" | custom-call | tf_op jit(solution)/shard_map/pallas_call | solution.py:889
  5.8 0.1 pad_add_fusion.pos
  5.9 0.7 collective-permute-done.xlo
  6.5 0.2 collective-permute-done.1.xhi
  6.7 0.6 shard_map.30
  7.4 2.1 %collective-permute-start.2 = (f32[40,8,128]{2,1,0:T(8,128)S(1)}, f32[40,8,128]{2,1,0:T(8,128)S(1)}, u32[]{:S(2)}, u32[]{:S(2)}) collective-permute-start(f32[40,8,128]{2,1,0:T(8,128)S(1)} %get-tuple-element.58), channel_id=1, source_target_pairs={{0,8},{8,16},{16,24},{24,32},{32,40},{40,48},{48,56},{56,0},{1,9},... | collective-permute-start | bytes 491528 | tf_op jit(solution)/shard_map/ppermute | solution.py:901
  9.5 4.0 %collective-permute-start.3 = (f32[40,8,128]{2,1,0:T(8,128)S(1)}, f32[40,8,128]{2,1,0:T(8,128)S(1)}, u32[]{:S(2)}, u32[]{:S(2)}) collective-permute-start(f32[40,8,128]{2,1,0:T(8,128)S(1)} %get-tuple-element.59), channel_id=1, source_target_pairs={{0,56},{8,0},{16,8},{24,16},{32,24},{40,32},{48,40},{56,48},{1,57}... | collective-permute-start | bytes 491528 | tf_op jit(solution)/shard_map/ppermute | solution.py:902
  13.5 2.6 %collective-permute-done.2.ylo = f32[40,8,128]{2,1,0:T(8,128)S(1)} collective-permute-done((f32[40,8,128]{2,1,0:T(8,128)S(1)}, f32[40,8,128]{2,1,0:T(8,128)S(1)}, u32[]{:S(2)}, u32[]{:S(2)}) %collective-permute-start.2) | collective-permute-done | bytes 163872 | tf_op jit(solution)/shard_map/ppermute | solution.py:901
  16.1 0.0 collective-permute-done.3.yhi
  16.1 1.8 %shard_map.31 = (f32[3,40,128]{2,1,0:T(8,128)S(1)}, f32[3,40,128]{2,1,0:T(8,128)S(1)}, f32[40,56,128]{2,1,0:T(8,128)S(1)}, f32[40,56,128]{2,1,0:T(8,128)S(1)}) custom-call(s32[3]{0:T(128)S(1)} %pad_add_fusion.pos, f32[32,32,128]{2,1,0:T(8,128)S(1)} %get-tuple-element.54.b, f32[32,32,128]{2,1,0:T(8,128)S(1)} %get-tuple-element.55.k, ...), custom_call_target="tpu_custom_call" | custom-call | tf_op jit(solution)/shard_map/pallas_call | solution.py:876
  17.9 2.6 %collective-permute-start.5 = (f32[3,40,128]{2,1,0:T(8,128)S(1)}, f32[3,40,128]{2,1,0:T(8,128)S(1)}, u32[]{:S(2)}, u32[]{:S(2)}) collective-permute-start(f32[3,40,128]{2,1,0:T(8,128)S(1)} %get-tuple-element.67.low), channel_id=1, source_target_pairs={{0,7},{1,0},{2,1},{3,2},{4,3},{5,4},{6,5},{7,6},{8,15},{9,8},{10,9... | collective-permute-start | bytes 184328 | tf_op jit(solution)/shard_map/ppermute | solution.py:902
  20.5 1.2 %collective-permute-start.4 = (f32[3,40,128]{2,1,0:T(8,128)S(1)}, f32[3,40,128]{2,1,0:T(8,128)S(1)}, u32[]{:S(2)}, u32[]{:S(2)}) collective-permute-start(f32[3,40,128]{2,1,0:T(8,128)S(1)} %get-tuple-element.68.high), channel_id=1, source_target_pairs={{0,1},{1,2},{2,3},{3,4},{4,5},{5,6},{6,7},{7,0},{8,9},{9,10},{10,1... | collective-permute-start | bytes 184328 | tf_op jit(solution)/shard_map/ppermute | solution.py:901
  21.7 2.0 %shard_map.32 = (f32[40,56,128]{2,1,0:T(8,128)S(1)}, f32[40,56,128]{2,1,0:T(8,128)S(1)}, f32[40,56,128]{2,1,0:T(8,128)S(1)}, f32[40,56,128]{2,1,0:T(8,128)S(1)}, f32[40,56,128]{2,1,0:T(8,128)S(1)}) custom-call(s32[3]{0:T(128)S(1)} %pad_add_fusion.pos, f32[40,56,128]{2,1,0:T(8,128)S(1)} %get-tuple-element.61.ek), custom_call_target="tpu_custom_call" | custom-call | tf_op jit(solution)/shard_map/pallas_call | solution.py:876
  23.7 0.0 collective-permute-done.5.zhi
  23.7 0.0 collective-permute-done.4.zlo
  23.7 4.3 %shard_map.33 = (f32[16,16,128]{2,1,0:T(8,128)S(1)}, f32[13,16,128]{2,1,0:T(8,128)S(1)}, f32[13,16,128]{2,1,0:T(8,128)S(1)}, f32[40,56,128]{2,1,0:T(8,128)S(1)},...) custom-call(s32[3]{0:T(128)S(1)} %pad_add_fusion.pos, ...), custom_call_target="tpu_custom_call" | custom-call | tf_op jit(solution)/shard_map/pallas_call | solution.py:876
  28.0 1.3 %collective-permute-start.6 = (f32[13,16,128]{2,1,0:T(8,128)S(1)}, f32[13,16,128]{2,1,0:T(8,128)S(1)}, u32[]{:S(2)}, u32[]{:S(2)}) collective-permute-start(f32[13,16,128]{2,1,0:T(8,128)S(1)} %get-tuple-element.70), channel_id=1, source_target_pairs={{0,64},{64,128},{128,192},{192,0},{1,65},{65,129},{129,193},{193,1... | collective-permute-start | bytes 319496 | tf_op jit(solution)/shard_map/ppermute | solution.py:901
  29.3 1.6 %collective-permute-start.7 = (f32[13,16,128]{2,1,0:T(8,128)S(1)}, f32[13,16,128]{2,1,0:T(8,128)S(1)}, u32[]{:S(2)}, u32[]{:S(2)}) collective-permute-start(f32[13,16,128]{2,1,0:T(8,128)S(1)} %get-tuple-element.71), channel_id=1, source_target_pairs={{0,192},{64,0},{128,64},{192,128},{1,193},{65,1},{129,65},{193,129... | collective-permute-start | bytes 319496 | tf_op jit(solution)/shard_map/ppermute | solution.py:902
  30.9 2.0 %collective-permute-done.6.xlo = f32[13,16,128]{2,1,0:T(8,128)S(1)} collective-permute-done((f32[13,16,128]{2,1,0:T(8,128)S(1)}, f32[13,16,128]{2,1,0:T(8,128)S(1)}, u32[]{:S(2)}, u32[]{:S(2)}) %collective-permute-start.6) | collective-permute-done | bytes 106528 | tf_op jit(solution)/shard_map/ppermute | solution.py:901
  32.9 0.0 collective-permute-done.7.xhi
  32.9 0.6 shard_map.34
  33.5 0.1 collective-permute-start.8
  33.6 3.1 %collective-permute-start.9 = (f32[70,8,128]{2,1,0:T(8,128)S(1)}, f32[70,8,128]{2,1,0:T(8,128)S(1)}, u32[]{:S(2)}, u32[]{:S(2)}) collective-permute-start(f32[70,8,128]{2,1,0:T(8,128)S(1)} %get-tuple-element.74), channel_id=1, source_target_pairs={{0,56},{8,0},{16,8},{24,16},{32,24},{40,32},{48,40},{56,48},{1,57}... | collective-permute-start | bytes 860168 | tf_op jit(solution)/shard_map/ppermute | solution.py:902
  36.7 3.9 %collective-permute-done.8.ylo = f32[70,8,128]{2,1,0:T(8,128)S(1)} collective-permute-done((f32[70,8,128]{2,1,0:T(8,128)S(1)}, f32[70,8,128]{2,1,0:T(8,128)S(1)}, u32[]{:S(2)}, u32[]{:S(2)}) %collective-permute-start.8) | collective-permute-done | bytes 286752 | tf_op jit(solution)/shard_map/ppermute | solution.py:901
  40.6 0.0 collective-permute-done.9.yhi
  40.6 1.2 %shard_map.35 = (f32[11,48,128]{2,1,0:T(8,128)S(1)}, f32[11,48,128]{2,1,0:T(8,128)S(1)}) custom-call(s32[3]{0:T(128)S(1)} %pad_add_fusion.pos, f32[42,16,128]{2,1,0:T(8,128)S(1)} %get-tuple-element.72.own, f32[70,8,128]{2,1,0:T(8,128)S(1)} %collective-permute-done.8.ylo, f32[70,8,128]{2,1,0:T(8,128)S(1)} %collective-permute-done.9.yhi), custom_call_target="tpu_custom_call" | custom-call | tf_op jit(solution)/shard_map/pallas_call | solution.py:876
  41.8 5.6 %collective-permute-start.10 = (f32[11,48,128]{2,1,0:T(8,128)S(1)}, f32[11,48,128]{2,1,0:T(8,128)S(1)}, u32[]{:S(2)}, u32[]{:S(2)}) collective-permute-start(f32[11,48,128]{2,1,0:T(8,128)S(1)} %get-tuple-element.75), channel_id=1, source_target_pairs={{0,1},{1,2},{2,3},{3,4},{4,5},{5,6},{6,7},{7,0},{8,9},{9,10},{10,1... | collective-permute-start | bytes 811016 | tf_op jit(solution)/shard_map/ppermute | solution.py:901
  47.4 0.0 collective-permute-start.11
  47.4 3.4 %collective-permute-done.10.zlo = f32[11,48,128]{2,1,0:T(8,128)S(1)} collective-permute-done((f32[11,48,128]{2,1,0:T(8,128)S(1)}, f32[11,48,128]{2,1,0:T(8,128)S(1)}, u32[]{:S(2)}, u32[]{:S(2)}) %collective-permute-start.10) | collective-permute-done | bytes 270368 | tf_op jit(solution)/shard_map/ppermute | solution.py:901
  50.8 2.5 %collective-permute-done.11.zhi = f32[11,48,128]{2,1,0:T(8,128)S(1)} collective-permute-done((f32[11,48,128]{2,1,0:T(8,128)S(1)}, f32[11,48,128]{2,1,0:T(8,128)S(1)}, u32[]{:S(2)}, u32[]{:S(2)}) %collective-permute-start.11) | collective-permute-done | bytes 270368 | tf_op jit(solution)/shard_map/ppermute | solution.py:902
  53.3 7.7 %shard_map.36 = (f32[32,8,128]{2,1,0:T(8,128)S(1)}, f32[42,64,128]{2,1,0:T(8,128)S(1)}, f32[42,64,128]{2,1,0:T(8,128)S(1)}, f32[42,64,128]{2,1,0:T(8,128)S(1)}, ...) custom-call(s32[3]{0:T(128)S(1)} %pad_add_fusion.pos, ...), custom_call_target="tpu_custom_call" | custom-call | tf_op jit(solution)/shard_map/pallas_call | solution.py:876
  61.1 17.4 %all_to_all.5 = f32[32,8,128]{2,1,0:T(8,128)S(1)} all-to-all(f32[32,8,128]{2,1,0:T(8,128)S(1)} %get-tuple-element.77), channel_id=1, replica_groups=mesh['gx'=4,'gy'=8,'gz'=8] {'gx','gy'}, dimensions={0} | all-to-all | bytes 262144 | tf_op jit(solution)/shard_map/all_to_all | solution.py:944
  78.5 2.0 %collective-permute-start.13 = (f32[256,128]{1,0:T(8,128)S(1)}, f32[256,128]{1,0:T(8,128)S(1)}, u32[]{:S(2)}, u32[]{:S(2)}) collective-permute-start(f32[256,128]{1,0:T(8,128)S(1)} %bitcast.4), channel_id=1, source_target_pairs={{0,1},{1,2},{2,3},{3,4},{4,5},{5,6},{6,7},{7,0},{8,9},{9,10},{10,1... | collective-permute-start | bytes 393224 | tf_op jit(solution)/shard_map/ppermute | solution.py:947
  80.4 0.1 collective-permute-start.12
  80.6 0.6 shard_map.39.xs
  81.2 0.6 shard_map.38.x4
  81.8 0.7 shard_map.37.x3
  82.5 0.0 collective-permute-done.13.down
  82.5 2.6 %collective-permute-done.12.up = f32[256,128]{1,0:T(8,128)S(1)} collective-permute-done((f32[256,128]{1,0:T(8,128)S(1)}, f32[256,128]{1,0:T(8,128)S(1)}, u32[]{:S(2)}, u32[]{:S(2)}) %collective-permute-start.12) | collective-permute-done | bytes 131104 | tf_op jit(solution)/shard_map/ppermute | solution.py:947
  85.1 11.3 %shard_map.40 = f32[32,32,128]{2,1,0:T(8,128)} custom-call(s32[3]{0:T(128)S(1)} %pad_add_fusion.pos, f32[256,128]{1,0:T(8,128)S(1)} %bitcast.6, f32[256,128]{1,0:T(8,128)S(1)} %collective-permute-done.12.up, f32[256,128]{1,0:T(8,128)S(1)} %collective-permute-done.13.down, f32[42,64,128]{2,1,0:T(8,128)S(1)} %get-tuple-element.78.b3, ...), custom_call_target="tpu_custom_call" | custom-call | tf_op jit(solution)/shard_map/pallas_call | solution.py:876
Async XLA Ops:
  1.0 5.6 %collective-permute-start = (f32[7,32,128]{2,1,0:T(8,128)S(1)}, f32[7,32,128]{2,1,0:T(8,128)S(1)}, u32[]{:S(2)}, u32[]{:S(2)}) collective-permute-start(f32[7,32,128]{2,1,0:T(8,128)S(1)} %get-tuple-element.56), channel_id=1, source_target_pairs={{0,64},{64,128},{128,192},{192,0},{1,65},{65,129},{129,193},{193,1... | collective-permute-start | bytes 344072 | tf_op jit(solution)/shard_map/ppermute | solution.py:901
  3.1 3.6 %collective-permute-start.1 = (f32[7,32,128]{2,1,0:T(8,128)S(1)}, f32[7,32,128]{2,1,0:T(8,128)S(1)}, u32[]{:S(2)}, u32[]{:S(2)}) collective-permute-start(f32[7,32,128]{2,1,0:T(8,128)S(1)} %get-tuple-element.57), channel_id=1, source_target_pairs={{0,192},{64,0},{128,64},{192,128},{1,193},{65,1},{129,65},{193,129... | collective-permute-start | bytes 344072 | tf_op jit(solution)/shard_map/ppermute | solution.py:902
  7.4 8.7 %collective-permute-start.2 = (f32[40,8,128]{2,1,0:T(8,128)S(1)}, f32[40,8,128]{2,1,0:T(8,128)S(1)}, u32[]{:S(2)}, u32[]{:S(2)}) collective-permute-start(f32[40,8,128]{2,1,0:T(8,128)S(1)} %get-tuple-element.58), channel_id=1, source_target_pairs={{0,8},{8,16},{16,24},{24,32},{32,40},{40,48},{48,56},{56,0},{1,9},... | collective-permute-start | bytes 491528 | tf_op jit(solution)/shard_map/ppermute | solution.py:901
  9.5 6.7 %collective-permute-start.3 = (f32[40,8,128]{2,1,0:T(8,128)S(1)}, f32[40,8,128]{2,1,0:T(8,128)S(1)}, u32[]{:S(2)}, u32[]{:S(2)}) collective-permute-start(f32[40,8,128]{2,1,0:T(8,128)S(1)} %get-tuple-element.59), channel_id=1, source_target_pairs={{0,56},{8,0},{16,8},{24,16},{32,24},{40,32},{48,40},{56,48},{1,57}... | collective-permute-start | bytes 491528 | tf_op jit(solution)/shard_map/ppermute | solution.py:902
  17.9 5.8 %collective-permute-start.5 = (f32[3,40,128]{2,1,0:T(8,128)S(1)}, f32[3,40,128]{2,1,0:T(8,128)S(1)}, u32[]{:S(2)}, u32[]{:S(2)}) collective-permute-start(f32[3,40,128]{2,1,0:T(8,128)S(1)} %get-tuple-element.67.low), channel_id=1, source_target_pairs={{0,7},{1,0},{2,1},{3,2},{4,3},{5,4},{6,5},{7,6},{8,15},{9,8},{10,9... | collective-permute-start | bytes 184328 | tf_op jit(solution)/shard_map/ppermute | solution.py:902
  20.5 3.2 %collective-permute-start.4 = (f32[3,40,128]{2,1,0:T(8,128)S(1)}, f32[3,40,128]{2,1,0:T(8,128)S(1)}, u32[]{:S(2)}, u32[]{:S(2)}) collective-permute-start(f32[3,40,128]{2,1,0:T(8,128)S(1)} %get-tuple-element.68.high), channel_id=1, source_target_pairs={{0,1},{1,2},{2,3},{3,4},{4,5},{5,6},{6,7},{7,0},{8,9},{9,10},{10,1... | collective-permute-start | bytes 184328 | tf_op jit(solution)/shard_map/ppermute | solution.py:901
  28.0 4.8 %collective-permute-start.6 = (f32[13,16,128]{2,1,0:T(8,128)S(1)}, f32[13,16,128]{2,1,0:T(8,128)S(1)}, u32[]{:S(2)}, u32[]{:S(2)}) collective-permute-start(f32[13,16,128]{2,1,0:T(8,128)S(1)} %get-tuple-element.70), channel_id=1, source_target_pairs={{0,64},{64,128},{128,192},{192,0},{1,65},{65,129},{129,193},{193,1... | collective-permute-start | bytes 319496 | tf_op jit(solution)/shard_map/ppermute | solution.py:901
  29.3 3.6 %collective-permute-start.7 = (f32[13,16,128]{2,1,0:T(8,128)S(1)}, f32[13,16,128]{2,1,0:T(8,128)S(1)}, u32[]{:S(2)}, u32[]{:S(2)}) collective-permute-start(f32[13,16,128]{2,1,0:T(8,128)S(1)} %get-tuple-element.71), channel_id=1, source_target_pairs={{0,192},{64,0},{128,64},{192,128},{1,193},{65,1},{129,65},{193,129... | collective-permute-start | bytes 319496 | tf_op jit(solution)/shard_map/ppermute | solution.py:902
  33.5 7.1 %collective-permute-start.8 = (f32[70,8,128]{2,1,0:T(8,128)S(1)}, f32[70,8,128]{2,1,0:T(8,128)S(1)}, u32[]{:S(2)}, u32[]{:S(2)}) collective-permute-start(f32[70,8,128]{2,1,0:T(8,128)S(1)} %get-tuple-element.73), channel_id=1, source_target_pairs={{0,8},{8,16},{16,24},{24,32},{32,40},{40,48},{48,56},{56,0},{1,9},... | collective-permute-start | bytes 860168 | tf_op jit(solution)/shard_map/ppermute | solution.py:901
  33.6 7.1 %collective-permute-start.9 = (f32[70,8,128]{2,1,0:T(8,128)S(1)}, f32[70,8,128]{2,1,0:T(8,128)S(1)}, u32[]{:S(2)}, u32[]{:S(2)}) collective-permute-start(f32[70,8,128]{2,1,0:T(8,128)S(1)} %get-tuple-element.74), channel_id=1, source_target_pairs={{0,56},{8,0},{16,8},{24,16},{32,24},{40,32},{48,40},{56,48},{1,57}... | collective-permute-start | bytes 860168 | tf_op jit(solution)/shard_map/ppermute | solution.py:902
  41.8 9.0 %collective-permute-start.10 = (f32[11,48,128]{2,1,0:T(8,128)S(1)}, f32[11,48,128]{2,1,0:T(8,128)S(1)}, u32[]{:S(2)}, u32[]{:S(2)}) collective-permute-start(f32[11,48,128]{2,1,0:T(8,128)S(1)} %get-tuple-element.75), channel_id=1, source_target_pairs={{0,1},{1,2},{2,3},{3,4},{4,5},{5,6},{6,7},{7,0},{8,9},{9,10},{10,1... | collective-permute-start | bytes 811016 | tf_op jit(solution)/shard_map/ppermute | solution.py:901
  47.4 5.9 %collective-permute-start.11 = (f32[11,48,128]{2,1,0:T(8,128)S(1)}, f32[11,48,128]{2,1,0:T(8,128)S(1)}, u32[]{:S(2)}, u32[]{:S(2)}) collective-permute-start(f32[11,48,128]{2,1,0:T(8,128)S(1)} %get-tuple-element.76), channel_id=1, source_target_pairs={{0,7},{1,0},{2,1},{3,2},{4,3},{5,4},{6,5},{7,6},{8,15},{9,8},{10,9... | collective-permute-start | bytes 811016 | tf_op jit(solution)/shard_map/ppermute | solution.py:902
  78.5 4.0 %collective-permute-start.13 = (f32[256,128]{1,0:T(8,128)S(1)}, f32[256,128]{1,0:T(8,128)S(1)}, u32[]{:S(2)}, u32[]{:S(2)}) collective-permute-start(f32[256,128]{1,0:T(8,128)S(1)} %bitcast.4), channel_id=1, source_target_pairs={{0,1},{1,2},{2,3},{3,4},{4,5},{5,6},{6,7},{7,0},{8,9},{9,10},{10,1... | collective-permute-start | bytes 393224 | tf_op jit(solution)/shard_map/ppermute | solution.py:947
  80.4 4.7 %collective-permute-start.12 = (f32[256,128]{1,0:T(8,128)S(1)}, f32[256,128]{1,0:T(8,128)S(1)}, u32[]{:S(2)}, u32[]{:S(2)}) collective-permute-start(f32[256,128]{1,0:T(8,128)S(1)} %bitcast.5), channel_id=1, source_target_pairs={{0,7},{1,0},{2,1},{3,2},{4,3},{5,4},{6,5},{7,6},{8,15},{9,8},{10,9... | collective-permute-start | bytes 393224 | tf_op jit(solution)/shard_map/ppermute | solution.py:947
